TPU v7x, 32 devices: a whole 2x2x4 slice. The times are simulated.
32 devices in a mesh: group: 4 (over z), width: 8 (over y, x, core).
Axes of the slice: x: 2, y: 2, z: 4, core: 2. Of those that a mesh axis runs over, the one named last changes fastest.
Arguments:
- momentum: bfloat16 [12, 1024, 7168], P('group', None, 'width'), may hold values from -0.049560547 to 0.049560547
- assignment: int32 [12], replicated, may hold values from -1 to 3, as said below
Outputs:
- update: bfloat16 [12, 1024, 7168], P('group', None, 'width')
- slot_update: bfloat16 [4, 2, 1024, 7168], P('group', None, None, 'width')
Inputs may be any that keep to these rules, and one draw needn't show every extreme that they name: `assignment`: owner o holds slots o * 3 to o * 3 + 2 and uses its first 1 to 3 of them (the others are -1), some owner all 3; 6 slots are used in all; no group is named by more than 2 slots, and some group by exactly 2.
All inputs are finite; a program needn't handle non-finite values.
Results may differ from a plain program's by a relative error of at most 0.0058.
Values may be sent and summed in bfloat16 or wider, within the bound.
No kernel may reach another device: no remote copies, remote signals or barrier semaphores. Data moves between devices by JAX's collectives and lax.ppermute only.
A program may use at most 128 MiB of HBM per device.

v0:
```python
import math

import jax
import jax.numpy as jnp
from jax import lax
from jax.sharding import PartitionSpec as P

D = 7168
CAP = 2


def slots_of(assignment):
    count = assignment.shape[0]
    order = jnp.arange(count, dtype=jnp.int32)
    earlier = order[:, None] > order[None, :]
    same = assignment[:, None] == assignment[None, :]
    return jnp.sum((earlier & same).astype(jnp.int32), axis=1)


def newton_blocks(blocks):
    partial_gram = jnp.einsum("krd,kcd->rkc", blocks, blocks, preferred_element_type=jnp.float32)
    gram_b = lax.psum(partial_gram, "width").astype(jnp.bfloat16)
    first = jnp.einsum("rkc,kcd->krd", gram_b, blocks, preferred_element_type=jnp.float32).astype(
        jnp.bfloat16
    )
    second = jnp.einsum("rkc,kcd->krd", gram_b, first, preferred_element_type=jnp.float32)
    mixed = (
        3.4445 * blocks.astype(jnp.float32) - 4.775 * first.astype(jnp.float32) + 2.0315 * second
    )
    return (math.sqrt(D) * mixed).astype(jnp.bfloat16)


def per_device(momentum, assignment):
    groups_total = lax.axis_size("group")
    own_index = lax.axis_index("group")
    holding = momentum.shape[0]
    slot = slots_of(assignment)
    mine_assign = lax.dynamic_slice_in_dim(assignment, own_index * holding, holding)
    mine_slot = lax.dynamic_slice_in_dim(slot, own_index * holding, holding)
    groups = jnp.arange(groups_total, dtype=jnp.int32)
    places = jnp.arange(CAP, dtype=jnp.int32)
    owner_sel = (mine_assign[:, None, None] == groups[None, :, None]) & (
        mine_slot[:, None, None] == places[None, None, :]
    )
    owner_sel = owner_sel.astype(jnp.bfloat16)
    sources = jnp.ones((groups_total,), jnp.bfloat16)
    live = (mine_assign >= 0).astype(jnp.float32)
    finished = newton_blocks(momentum)
    update = (finished.astype(jnp.float32) * live[:, None, None]).astype(jnp.bfloat16)
    outgoing = jnp.einsum(
        "jgs,jhd->gshd", owner_sel, update, preferred_element_type=jnp.float32
    ).astype(jnp.bfloat16)
    arrived = lax.all_to_all(outgoing, "group", split_axis=0, concat_axis=0, tiled=True)
    placed = jnp.einsum("g,gshd->shd", sources, arrived, preferred_element_type=jnp.float32)
    slot_update = placed.astype(jnp.bfloat16)[None]
    return (update, slot_update)


def solution(mesh):
    return jax.shard_map(
        per_device,
        mesh=mesh,
        in_specs=(P("group", None, "width"), P()),
        out_specs=(P("group", None, "width"), P("group", None, None, "width")),
        check_vma=False,
    )
```

profile of v0, /device:TPU:0, one launch (start us, length us, event | category | flops | bytes accessed | tf_op | source)
XLA Modules:
  0.0 650.7 jit_solution(11588036049022702570)
XLA Ops:
  0.6 0.9 convert_reduce_fusion
  1.5 0.7 compare_convert_fusion
  2.3 0.1 dynamic_slice.7
  2.4 0.1 iota_compare_fusion.1
  2.4 0.1 iota_compare_fusion.2
  2.5 0.1 and_bitcast_fusion
  2.6 0.1 copy.10
  2.7 13.0 %convolution_bitcast_fusion = f32[1024,3,1024]{0,2,1:T(8,128)} fusion(bf16[3,1024,896]{2,1,0:T(8,128)(2,1)} %param.2), kind=kOutput, calls=%fused_computation.8 | convolution fusion | flops 5637144576 | bytes 18087936 | tf_op jit(solution)/shard_map/krd,kcd->rkc/dot_general | solution.py:21
  15.7 250.5 %all-reduce.1 = bf16[1024,3,1024]{0,2,1:T(8,128)(2,1)} all-reduce(f32[1024,3,1024]{0,2,1:T(8,128)} %convolution_bitcast_fusion), channel_id=1, replica_groups=mesh['group'=4,'width'=8] {'width'}, use_global_device_ids=true, to_apply=%region_0.0 | all-reduce | flops 3145728 | bytes 18874368 | tf_op jit(solution)/shard_map/psum | solution.py:22
  266.1 10.4 %fusion.12 = bf16[3,1024,896]{2,1,0:T(8,128)(2,1)S(1)} fusion(bf16[1024,3,1024]{0,2,1:T(8,128)(2,1)} %all-reduce.1, bf16[3,1024,896]{2,1,0:T(8,128)(2,1)} %param.2), kind=kOutput, calls=%fused_computation.23 | convolution fusion | flops 5637144576 | bytes 17301504 | tf_op jit(solution)/shard_map/rkc,kcd->krd/dot_general | solution.py:23
  276.6 13.0 %multiply_convert_fusion = bf16[3,1024,896]{2,1,0:T(8,128)(2,1)S(1)} fusion(bf16[3,1024,896]{2,1,0:T(8,128)(2,1)} %param.2, f32[3]{0:T(128)S(1)} %get-tuple-element.2, bf16[3,1024,896]{2,1,0:T(8,128)(2,1)S(1)} %fusion.12, bf16[1024,3,1024]{0,2,1:T(8,128)(2,1)} %all-reduce.1), kind=kOutput, calls=%fused_computation.3 | convolution fusion | flops 5670174720 | bytes 22806540 | tf_op jit(solution)/shard_map/rkc,kcd->krd/dot_general | solution.py:26
  289.6 0.0 copy-start
  289.7 12.3 %fusion.2 = bf16[4,2,1024,896]{3,0,2,1:T(4,128)(2,1)S(1)} fusion(pred[3,4,2,1]{1,0,3,2:T(4,128)(4,1)S(1)} %copy.10, bf16[3,1024,896,1]{2,1,0,3:T(8,128)(2,1)S(1)} %bitcast.21), kind=kOutput, calls=%fused_computation.6 | convolution fusion | flops 44040192 | bytes 20185112 | tf_op jit(solution)/shard_map/jgs,jhd->gshd/dot_general | solution.py:50
  302.0 0.0 copy-done
  302.0 5.5 copy.24
  307.4 323.0 %all_to_all.5 = bf16[4,2,1024,896]{3,2,1,0:T(8,128)(2,1)} all-to-all(bf16[4,2,1024,896]{3,2,1,0:T(8,128)(2,1)S(1)} %copy.24), channel_id=1, replica_groups=mesh['group'=4,'width'=8] {'group'}, dimensions={0} | all-to-all | bytes 29360128 | tf_op jit(solution)/shard_map/all_to_all | solution.py:53
  630.5 17.8 %fusion = bf16[1,2,1024,896]{3,0,2,1:T(2,128)(2,1)S(1)} fusion(bf16[4,2,1024,896]{3,2,1,0:T(8,128)(2,1)} %all_to_all.5), kind=kOutput, calls=%fused_computation.1 | convolution fusion | flops 14680064 | bytes 18350080 | tf_op jit(solution)/shard_map/g,gshd->shd/dot_general | solution.py:54
  648.3 2.4 copy.25
Async XLA Ops:
  289.6 12.3 %copy-start = (bf16[3,1024,896]{2,1,0:T(8,128)(2,1)}, bf16[3,1024,896]{2,1,0:T(8,128)(2,1)S(1)}, u32[]{:S(2)}) copy-start(bf16[3,1024,896]{2,1,0:T(8,128)(2,1)S(1)} %multiply_convert_fusion) | copy-start | bytes 16515076
where the time goes:
time: 651 us
  blocking collectives  573 us (88%)
  matrix products  66.6 us (10%)
  local copies, waits for them, and re-layouts  8.09 us (1%)
    all_to_all x1, blocking collectives, per_device(): lax.all_to_all(outgoing, 'group', split_axis=0, concat_axis=0, tiled=True)  323 us
    psum x1, blocking collectives, newton_blocks(): gram_b = lax.psum(partial_gram, 'width').astype(jnp.bfloat16)  250 us
    dot_general x1, matrix products, per_device(): jnp.einsum('g,gshd->shd', sources, arrived, preferred_element_type=jnp.fl...  17.8 us
    dot_general x1, matrix products, newton_blocks(): jnp.einsum('rkc,kcd->krd', gram_b, first, preferred_element_type=jnp.floa...  13 us

commit v1 on v0

v1 whole, which is shorter than its diff:
```python
import functools
import math

import jax
import jax.numpy as jnp
from jax import lax
from jax.experimental import pallas as pl
from jax.experimental.pallas import tpu as pltpu
from jax.sharding import PartitionSpec as P

D = 7168
CAP = 2
CHUNKS = 2
DELAY = 2
STEPS = 4
EXTRA = (0, 2, 4, 6)
BLOCK = 256
SCALE = math.sqrt(D)
VMEM_BYTES = 56 * 1024 * 1024
NEVER = 1 << 20
FAR = 1 << 10
WORK = 5 * 10**9

SMEM = pl.BlockSpec(memory_space=pltpu.SMEM)
VMEM = pl.BlockSpec(memory_space=pltpu.VMEM)
ANY = pl.BlockSpec(memory_space=pl.ANY)


def compiler_params():
    return pltpu.CompilerParams(vmem_limit_bytes=VMEM_BYTES)


def most_steps(n, hold):
    end = 0
    for link in range(n - 1):
        load = min(hold * (link + 1), CAP * (n - 1 - link))
        end = max(CHUNKS, end - CHUNKS + DELAY) + CHUNKS * load
    return max(end, STEPS + max(EXTRA))


def plan_kernel(n, hold, assign, where, snd, meta, slot, key, ready, start, front):
    experts = n * hold
    me = where[0]
    names = [assign[e] for e in range(experts)]
    for e in range(experts):
        count = jnp.int32(0)
        for e2 in range(e):
            count += (names[e2] == names[e]).astype(jnp.int32)
        slot[e] = count
    for s in range(CAP):
        meta[2 + s] = -1
    for e in range(experts):

        @pl.when((names[e] == me) & (e // hold == me) & (slot[e] < CAP))
        def _():
            meta[2 + slot[e]] = e % hold

    for h in range(hold):
        meta[2 + CAP + h] = (assign[me * hold + h] >= 0).astype(jnp.int32)

    def crossing(e, side, link):
        owner = e // hold
        frm = owner if side == 0 else n - 1 - owner
        if frm > link:
            return None
        to = names[e] if side == 0 else n - 1 - names[e]
        return (names[e] >= 0) & (link < to)

    busy = []
    for side in range(2):
        most = jnp.int32(0)
        for link in range(n - 1):
            load = jnp.int32(0)
            for e in range(experts):
                here = crossing(e, side, link)
                if here is not None:
                    load += here.astype(jnp.int32)
            most = jnp.maximum(most, load)
        busy.append(most)

    for owner in range(n):
        best, chosen = jnp.int32(-2), jnp.int32(0)
        for h in range(hold):
            name = names[owner * hold + h]
            value = jnp.where(
                name > owner, busy[0] * 64 + name - owner, jnp.where(name < owner, busy[1] * 64 + owner - name, 0)
            )
            value = jnp.where(name < 0, -1, value)
            best, chosen = jnp.where(value > best, value, best), jnp.where(value > best, h, chosen)
        front[owner] = chosen
    chosen = front[me]
    meta[2 + CAP + hold] = chosen
    for place in range(1, hold):
        meta[2 + CAP + hold + place] = jnp.where(chosen >= place, place - 1, place)

    longest = jnp.int32(0)
    for side in range(2):
        mine = me if side == 0 else n - 1 - me

        def clear(t, _):
            snd[side, t] = 0
            return 0

        lax.fori_loop(0, snd.shape[1], clear, 0)
        for link in range(n - 1):
            for e in range(experts):
                here = crossing(e, side, link)
                if here is None:
                    key[e] = NEVER
                    continue
                owner = e // hold
                frm = owner if side == 0 else n - 1 - owner
                to = names[e] if side == 0 else n - 1 - names[e]
                if frm == link:
                    at = jnp.where(front[owner] == e % hold, 0, CHUNKS)
                else:
                    at = start[e] + DELAY
                ready[e] = at
                key[e] = jnp.where(here, at * 64 + (n - to), NEVER)

            def choose(_, cursor):
                low, e = key[0], jnp.int32(0)
                for e2 in range(1, experts):
                    better = key[e2] < low
                    low, e = jnp.where(better, key[e2], low), jnp.where(better, e2, e)
                begin = jnp.maximum(cursor, ready[e])

                @pl.when(low < NEVER)
                def _():
                    before = start[e]
                    key[e] = NEVER
                    start[e] = begin
                    local = e // hold == me
                    to = assign[e] if side == 0 else n - 1 - assign[e]

                    @pl.when(mine == link)
                    def _():
                        base = jnp.where(local, e % hold * CHUNKS, NEVER + before)
                        for j in range(CHUNKS):
                            snd[side, begin + j] = base + j

                    @pl.when((mine == link + 1) & (to == link + 1) & (slot[e] < CAP))
                    def _():
                        meta[2 + slot[e]] = hold + FAR * side + begin

                return jnp.where(low < NEVER, begin + CHUNKS, cursor)

            most = min(hold * (link + 1), CAP * (n - 1 - link))
            longest = jnp.maximum(longest, lax.fori_loop(0, most, choose, jnp.int32(0)))
    branch = jnp.int32(0)
    for extra in EXTRA:
        branch += (longest > STEPS + extra).astype(jnp.int32)
    meta[0] = branch
    meta[1] = where[1]
    meta[2 + CAP + 2 * hold] = longest


def make_plan(assignment, where, n, hold):
    i32 = jnp.int32
    return pl.pallas_call(
        functools.partial(plan_kernel, n, hold),
        out_shape=[
            jax.ShapeDtypeStruct((2, most_steps(n, hold)), i32),
            jax.ShapeDtypeStruct((3 + CAP + 2 * hold,), i32),
        ],
        in_specs=[SMEM, SMEM],
        out_specs=[SMEM] * 2,
        scratch_shapes=[pltpu.SMEM((n * hold,), i32) for _ in range(4)] + [pltpu.SMEM((n,), i32)],
        name="plan",
    )(assignment, where)


def pick_kernel(step, count, snd, own, *rest):
    came, (right, left, sems) = rest[: 2 * count], rest[-3:]
    for side, target in enumerate((right, left)):
        code = snd[side, step]

        @pl.when(code < NEVER)
        def _():
            pltpu.make_async_copy(own.at[code], target, sems.at[side]).start()

        for t in range(count):

            @pl.when(code == NEVER + t)
            def _():
                pltpu.make_async_copy(came[2 * t + side], target, sems.at[side]).start()

    for side, target in enumerate((right, left)):
        pltpu.make_async_copy(own.at[0], target, sems.at[side]).wait()


def pick(own, snd, came, step):
    count = max(step + 1 - DELAY, 0)
    earlier = [x for pair in came[:count] for x in pair]
    chunk = jax.ShapeDtypeStruct(own.shape[1:], own.dtype)
    return pl.pallas_call(
        functools.partial(pick_kernel, step, count),
        out_shape=[chunk, chunk],
        in_specs=[SMEM] + [ANY] * (1 + len(earlier)),
        out_specs=[VMEM, VMEM],
        scratch_shapes=[pltpu.SemaphoreType.DMA((2,))],
        cost_estimate=pl.CostEstimate(
            flops=0, bytes_accessed=1, transcendentals=0
        ),
        name="pick",
    )(snd, own, *earlier)


def hop(right, left, n):
    return (
        lax.ppermute(right, "group", [(i, i + 1) for i in range(n - 1)]),
        lax.ppermute(left, "group", [(i + 1, i) for i in range(n - 1)]),
    )


def place_kernel(hold, steps, meta, update_ref, *rest):
    came, (out_ref, sems) = rest[: 2 * steps], rest[2 * steps :]
    chunk = out_ref.shape[1] // CHUNKS

    def target(s, j):
        return out_ref.at[s, pl.ds(j * chunk, chunk)]

    for s in range(CAP):
        kind = meta[2 + s]

        @pl.when((kind >= 0) & (kind < hold))
        def _():
            for j in range(CHUNKS):
                pltpu.make_async_copy(
                    update_ref.at[kind, pl.ds(j * chunk, chunk)], target(s, j), sems.at[s, j]
                ).start()

        for side in range(2):
            for j in range(CHUNKS):
                for t in range(j, steps):

                    @pl.when(kind == hold + FAR * side + t - j)
                    def _():
                        pltpu.make_async_copy(came[2 * t + side], target(s, j), sems.at[s, j]).start()

        @pl.when(kind < 0)
        def _():
            out_ref[s] = jnp.zeros(out_ref.shape[1:], out_ref.dtype)

    for s in range(CAP):
        kind = meta[2 + s]
        at = kind - hold
        at = jnp.where(at >= FAR, at - FAR, at)
        for j in range(CHUNKS):

            @pl.when((kind >= 0) & (at + j < steps))
            def _():
                pltpu.make_async_copy(came[0], target(s, j), sems.at[s, j]).wait()


def last_kernel(hold, last, meta, _, *rest):
    came, (out_ref, sems) = rest[:2], rest[2:]
    chunk = came[0].shape[0]
    for wait in (False, True):
        for s in range(CAP):
            for side in range(2):
                for j in range(CHUNKS):

                    @pl.when((meta[2 + s] >= hold) & (meta[2 + s] == hold + FAR * side + last - j))
                    def _():
                        copy = pltpu.make_async_copy(
                            came[side], out_ref.at[s, pl.ds(j * chunk, chunk)], sems.at[s]
                        )
                        copy.wait() if wait else copy.start()


def place(meta, came, update):
    hold, rows, cols = update.shape
    arrived = [x for pair in came for x in pair]
    return pl.pallas_call(
        functools.partial(place_kernel, hold, len(came)),
        out_shape=jax.ShapeDtypeStruct((CAP, rows, cols), update.dtype),
        in_specs=[SMEM, ANY] + [ANY] * len(arrived),
        out_specs=VMEM,
        scratch_shapes=[pltpu.SemaphoreType.DMA((CAP, CHUNKS))],
        compiler_params=compiler_params(),
        cost_estimate=pl.CostEstimate(flops=WORK, bytes_accessed=1, transcendentals=0),
        name="place",
    )(meta, update, *arrived)


def place_last(meta, out, came, step, hold):
    return pl.pallas_call(
        functools.partial(last_kernel, hold, step),
        out_shape=jax.ShapeDtypeStruct(out.shape, out.dtype),
        in_specs=[SMEM, ANY, VMEM, VMEM],
        out_specs=ANY,
        scratch_shapes=[pltpu.SemaphoreType.DMA((CAP,))],
        input_output_aliases={1: 0},
        cost_estimate=pl.CostEstimate(flops=WORK, bytes_accessed=1, transcendentals=0),
        name="last",
    )(meta, out, *came)


def pieces_of(me, q, width):
    chips = width // 2
    core, chip = q // chips, q % chips
    return ((me & 1) ^ core) * chips + ((me >> 1) ^ chip)


def gram_kernel(blocks, width, meta, x_ref, *rest):
    outs, scratch = rest[:4], rest[4]
    high = BLOCK // width
    me = meta[1]
    for j in range(blocks):
        rows = (j + 1) * BLOCK
        scratch[j, pl.ds(0, rows), :] = lax.dot_general(
            x_ref[0, pl.ds(0, rows), :],
            x_ref[0, pl.ds(j * BLOCK, BLOCK), :],
            (((1,), (1,)), ((), ())),
            preferred_element_type=jnp.float32,
        ).astype(jnp.bfloat16)

    def sort(keep, send):
        for j in range(blocks):
            for q in range(width):
                piece = pieces_of(me, q, width)
                out = keep if q < width // 2 else send
                base = q % (width // 2) * (blocks * (blocks + 1) // 2)
                for i in range(j + 1):
                    at = base + j * (j + 1) // 2 + i
                    out[0, pl.ds(at * high, high), :] = scratch[
                        j, pl.ds(pl.multiple_of(i * BLOCK + piece * high, high), high), :
                    ]

    pl.when(pl.program_id(0) == 0)(lambda: sort(*outs[:2]))
    pl.when(pl.program_id(0) > 0)(lambda: sort(*outs[2:]))


def partial_gram(meta, momentum, width):
    hold, rows, cols = momentum.shape
    blocks = rows // BLOCK
    packed = blocks * (blocks + 1) // 2 * BLOCK
    shapes = [jax.ShapeDtypeStruct((count, packed // 2, BLOCK), jnp.bfloat16) for count in (1, 1, hold - 1, hold - 1)]
    one = pl.BlockSpec((1, packed // 2, BLOCK), lambda e, meta: (0, 0, 0))
    others = pl.BlockSpec((1, packed // 2, BLOCK), lambda e, meta: (jnp.maximum(e - 1, 0), 0, 0))
    return pl.pallas_call(
        functools.partial(gram_kernel, blocks, width),
        grid_spec=pltpu.PrefetchScalarGridSpec(
            num_scalar_prefetch=1,
            grid=(hold,),
            in_specs=[pl.BlockSpec((1, rows, cols), lambda e, meta: (meta[2 + CAP + hold + e], 0, 0))],
            out_specs=[one, one, others, others],
            scratch_shapes=[pltpu.VMEM((blocks, rows, BLOCK), jnp.bfloat16)],
        ),
        out_shape=shapes,
        compiler_params=compiler_params(),
        cost_estimate=pl.CostEstimate(
            flops=2 * hold * packed * BLOCK * cols,
            bytes_accessed=2 * hold * (rows * cols + packed * BLOCK),
            transcendentals=0,
        ),
        name="gram",
    )(meta, momentum)


def exchange(x, other, width):
    return lax.ppermute(x, "width", [(i, i ^ other) for i in range(width)])


def reduce_scatter(keep, send, width):
    chips = width // 2
    high = keep.shape[1] // chips
    total = keep.astype(jnp.float32) + exchange(send, 1, width).astype(jnp.float32)
    mine = total[:, :high]
    for r in range(1, chips):
        piece = total[:, r * high : (r + 1) * high].astype(jnp.bfloat16)
        mine = mine + exchange(piece, 2 * r, width).astype(jnp.float32)
    return mine.astype(jnp.bfloat16)


def all_gather(x, width):
    pieces = [x] + [exchange(x, 2 * r, width) for r in range(1, width // 2)]
    return pieces + [exchange(piece, 1, width) for piece in pieces]


def unpack(blocks, width, me, pieces, gram_ref):
    high = BLOCK // width
    for q in range(width):
        piece = pieces_of(me, q, width)
        for j in range(blocks):
            for i in range(j + 1):
                at = j * (j + 1) // 2 + i
                gram_ref[
                    pl.ds(pl.multiple_of(i * BLOCK + piece * high, high), high), pl.ds(j * BLOCK, BLOCK)
                ] = pieces[q][0, pl.ds(at * high, high), :]
    for j in range(blocks):
        for i in range(j):
            gram_ref[pl.ds(j * BLOCK, BLOCK), pl.ds(i * BLOCK, BLOCK)] = gram_ref[
                pl.ds(i * BLOCK, BLOCK), pl.ds(j * BLOCK, BLOCK)
            ].T


def update_kernel(blocks, width, hold, place, meta, x_ref, *rest):
    pieces, (gram_ref, first_ref, second_ref, sems) = rest[:width], rest[-4:]
    outs = rest[width + (place > 0) : -4]
    chosen = meta[2 + CAP + hold + place]
    live = meta[2 + CAP + chosen]
    rows = x_ref.shape[1]
    chunk = rows // CHUNKS

    def copies(j):
        span = pl.ds(j * chunk, chunk)
        targets = [outs[0].at[chosen, span]]
        if place == 0:
            targets.append(outs[1 + j])
        return [pltpu.make_async_copy(second_ref.at[span], to, sems.at[j, i]) for i, to in enumerate(targets)]

    @pl.when(live == 1)
    def _():
        unpack(blocks, width, meta[1], pieces, gram_ref)
        first_ref[...] = jnp.dot(gram_ref[...], x_ref[0], preferred_element_type=jnp.float32).astype(jnp.bfloat16)

    for j in range(CHUNKS):
        span = pl.ds(j * chunk, chunk)

        @pl.when(live == 1)
        def _():
            second = jnp.dot(gram_ref[span, :], first_ref[...], preferred_element_type=jnp.float32)
            x, first = x_ref[0, span, :].astype(jnp.float32), first_ref[span, :].astype(jnp.float32)
            mixed = 3.4445 * x - 4.775 * first + 2.0315 * second
            second_ref[span, :] = (SCALE * mixed).astype(jnp.bfloat16)

        @pl.when(live == 0)
        def _():
            second_ref[span, :] = jnp.zeros((chunk, second_ref.shape[1]), jnp.bfloat16)

        for copy in copies(j):
            copy.start()
    for j in range(CHUNKS):
        for copy in copies(j):
            copy.wait()


def one_update(meta, pieces, momentum, place, update=None):
    hold, rows, cols = momentum.shape
    index = max(place - 1, 0)
    width = len(pieces)
    out_shape = [jax.ShapeDtypeStruct(momentum.shape, momentum.dtype)]
    if place == 0:
        out_shape += [jax.ShapeDtypeStruct((rows // CHUNKS, cols), momentum.dtype)] * CHUNKS
    before = [] if update is None else [update]
    return pl.pallas_call(
        functools.partial(update_kernel, rows // BLOCK, width, hold, place),
        grid_spec=pltpu.PrefetchScalarGridSpec(
            num_scalar_prefetch=1,
            grid=(1,),
            in_specs=[pl.BlockSpec((1, rows, cols), lambda i, meta: (meta[2 + CAP + hold + place], 0, 0))]
            + [pl.BlockSpec((1,) + piece.shape[1:], lambda i, meta: (index, 0, 0)) for piece in pieces]
            + [ANY] * len(before),
            out_specs=[ANY] * len(out_shape),
            scratch_shapes=[
                pltpu.VMEM((rows, rows), jnp.bfloat16),
                pltpu.VMEM((rows, cols), jnp.bfloat16),
                pltpu.VMEM((rows, cols), jnp.bfloat16),
                pltpu.SemaphoreType.DMA((CHUNKS, 2)),
            ],
        ),
        out_shape=out_shape,
        input_output_aliases={2 + width: 0} if before else {},
        compiler_params=compiler_params(),
        cost_estimate=pl.CostEstimate(
            flops=4 * rows * rows * cols, bytes_accessed=6 * rows * cols, transcendentals=0
        ),
        name="update",
    )(meta, momentum, *pieces, *before)


def stream(meta, snd, update, came, out, extra, n):
    hold, rows, cols = update.shape
    chunks = update.reshape(-1, rows // CHUNKS, cols)
    came = list(came)
    for step in range(STEPS, STEPS + extra):
        came.append(hop(*pick(chunks, snd, came, step), n))
    for step in range(STEPS, STEPS + extra):
        out = place_last(meta, out, came[step], step, hold)
    return out[None]


def endless_pick_kernel(count, snd, step, own, came_in, *rest):
    came, (right, left, sems) = rest[:-3], rest[-3:]
    for side, target in enumerate((right, left)):
        code = snd[side, step[0]]

        @pl.when(code < NEVER)
        def _():
            pltpu.make_async_copy(own.at[code], target, sems.at[side]).start()

        @pl.when(code >= NEVER + count)
        def _():
            pltpu.make_async_copy(came_in.at[side, code - NEVER - count], target, sems.at[side]).start()

        for t in range(count):

            @pl.when(code == NEVER + t)
            def _():
                pltpu.make_async_copy(came[2 * t + side], target, sems.at[side]).start()

    for side, target in enumerate((right, left)):
        pltpu.make_async_copy(own.at[0], target, sems.at[side]).wait()


def endless_place_kernel(hold, count, meta, _, came_ref, out_ref, scratch, sem):
    chunk = scratch.shape[0]
    for s in range(CAP):
        for side in range(2):
            kind = meta[2 + s] - FAR * side
            for j in range(CHUNKS):
                t = kind - hold + j

                @pl.when((kind >= hold) & (kind < hold + FAR) & (t >= count))
                def _():
                    for copy in (
                        pltpu.make_async_copy(came_ref.at[side, t - count], scratch, sem),
                        pltpu.make_async_copy(scratch, out_ref.at[s, pl.ds(j * chunk, chunk)], sem),
                    ):
                        copy.start()
                        copy.wait()


def endless(meta, snd, update, came, out, n):
    hold, rows, cols = update.shape
    chunks = update.reshape(-1, rows // CHUNKS, cols)
    chunk = jax.ShapeDtypeStruct(chunks.shape[1:], update.dtype)
    arrived = [x for pair in came for x in pair]
    last = meta[2 + CAP + 2 * hold]

    def step(carry):
        t, kept = carry
        right, left = pl.pallas_call(
            functools.partial(endless_pick_kernel, len(came)),
            out_shape=[chunk, chunk],
            in_specs=[SMEM, SMEM] + [ANY] * (2 + len(arrived)),
            out_specs=[VMEM, VMEM],
            scratch_shapes=[pltpu.SemaphoreType.DMA((2,))],
            name="endless_pick",
        )(snd, t.reshape(1), chunks, kept, *arrived)
        both = jnp.stack(hop(right, left, n))[:, None]
        return t + 1, lax.dynamic_update_slice(kept, both, (0, t - STEPS, 0, 0))

    kept = jnp.zeros((2, snd.shape[1] - STEPS) + chunk.shape, update.dtype)
    _, kept = lax.while_loop(lambda carry: carry[0] < last, step, (jnp.int32(STEPS), kept))
    return pl.pallas_call(
        functools.partial(endless_place_kernel, hold, len(came)),
        out_shape=jax.ShapeDtypeStruct(out.shape, out.dtype),
        in_specs=[SMEM, ANY, ANY],
        out_specs=ANY,
        scratch_shapes=[pltpu.VMEM(chunk.shape, chunk.dtype), pltpu.SemaphoreType.DMA],
        input_output_aliases={1: 0},
        name="endless_place",
    )(meta, out, kept)[None]


def per_device(momentum, assignment):
    n = lax.axis_size("group")
    width = lax.axis_size("width")
    hold, rows, cols = momentum.shape
    where = jnp.stack([lax.axis_index("group"), lax.axis_index("width")]).astype(jnp.int32)
    snd, meta = make_plan(assignment, where, n, hold)
    keep, send, keeps, sends = partial_gram(meta, momentum, width)
    update, *done = one_update(meta, all_gather(reduce_scatter(keep, send, width), width), momentum, 0)
    pieces = all_gather(reduce_scatter(keeps, sends, width), width)
    for place_in_order in range(1, hold):
        (update,) = one_update(meta, pieces, momentum, place_in_order, update)
    chunks = update.reshape(-1, rows // CHUNKS, cols)
    came = []
    for step in range(STEPS):
        sent = (done[step], done[step]) if step < DELAY else pick(chunks, snd, came, step)
        came.append(hop(*sent, n))
    out = place(meta, came[:-1], update)
    out = place_last(meta, out, came[-1], STEPS - 1, hold)
    ways = [functools.partial(lambda extra, *args: stream(*args, extra, n), extra) for extra in EXTRA]
    ways.append(lambda *args: endless(*args, n))
    return update, lax.switch(meta[0], ways, meta, snd, update, came, out)


def solution(mesh):
    return jax.shard_map(
        per_device,
        mesh=mesh,
        in_specs=(P("group", None, "width"), P()),
        out_specs=(P("group", None, "width"), P("group", None, None, "width")),
        check_vma=False,
    )
```

time: 651 us -> 217 us (0.33)
  blocking collectives: 573 us -> 0 us
  waiting for transfers between devices: 0 us -> 102 us
  matrix products: 66.6 us -> 0 us
  starting transfers between devices: 0 us -> 55.8 us
  Pallas kernels: 0 us -> 52.3 us
    all_to_all x1 -> x0, blocking collectives: 323 us -> none  [per_device(): lax.all_to_all(outgoing, 'group', split_axis=0, concat_axis=0, tiled=True)]
    psum x1 -> x0, blocking collectives: 250 us -> none  [newton_blocks(): gram_b = lax.psum(partial_gram, 'width').astype(jnp.bfloat16)]
    ppermute x0 -> x34, waiting for transfers between devices: none -> 102 us  [the longest x6 47.5 us: hop(): lax.ppermute(right, 'group', [(i, i + 1) for i in range(n - 1)])]
    dot_general x5 -> x0, matrix products: 66.6 us -> none  [the longest x1 17.8 us: per_device(): jnp.einsum('g,gshd->shd', sources, arrived, preferred_element_type=jnp.fl...]
    ppermute x0 -> x34, starting transfers between devices: none -> 55.8 us  [the longest x6 27.9 us: hop(): lax.ppermute(right, 'group', [(i, i + 1) for i in range(n - 1)])]
    pallas_call x0 -> x13, Pallas kernels: none -> 52.3 us  [the longest x3 16.4 us: one_update(): pl.pallas_call(functools.partial(update_kernel, rows // BLOCK, width, hol...]
    dot_general x2 -> x0, local copies, waits for them, and re-layouts: 7.88 us -> none  [the longest x1 5.45 us: per_device(): jnp.einsum('jgs,jhd->gshd', owner_sel, update, preferred_element_type=jnp...]
  transfers between devices with their start and end apart: 0 -> 34, of which waited for: 0 -> 21; matrix products, arithmetic and copies ran while one was open for 0% -> 1% of each run, Pallas kernels for 0% -> 15%
where the time goes in v1:
time: 217 us; the launch traced here: 216 us
  waiting for transfers between devices  102 us (47%)
  starting transfers between devices  55.8 us (26%)
  Pallas kernels  52.3 us (24%)
  other arithmetic  2.54 us (1%)
  local copies, waits for them, and re-layouts  2.49 us (1%)
    ppermute x6, waiting for transfers between devices, hop(): lax.ppermute(right, 'group', [(i, i + 1) for i in range(n - 1)])  47.5 us
    ppermute x22, waiting for transfers between devices, exchange(): return lax.ppermute(x, 'width', [(i, i ^ other) for i in range(width)])  30.7 us
    ppermute x6, starting transfers between devices, hop(): lax.ppermute(right, 'group', [(i, i + 1) for i in range(n - 1)])  27.9 us
    ppermute x6, waiting for transfers between devices, hop(): lax.ppermute(left, 'group', [(i + 1, i) for i in range(n - 1)])  23.4 us
    ppermute x22, starting transfers between devices, exchange(): return lax.ppermute(x, 'width', [(i, i ^ other) for i in range(width)])  20.2 us
    pallas_call x3, Pallas kernels, one_update(): pl.pallas_call(functools.partial(update_kernel, rows // BLOCK, width, hol...  16.4 us
    pallas_call x4, Pallas kernels, pick(): pl.pallas_call(functools.partial(pick_kernel, step, count), out_shape=[ch...  13.7 us
    pallas_call x1, Pallas kernels, partial_gram(): pl.pallas_call(functools.partial(gram_kernel, blocks, width), grid_spec=p...  8.61 us
  transfers between devices with their start and end apart: 34, of which 21 were waited for; matrix products, arithmetic and copies ran while one was open for 1% of the time, Pallas kernels for 15%

profile of v1, /device:TPU:0, one launch (start us, length us, event | category | flops | bytes accessed | tf_op | source)
XLA Modules:
  0.0 216.1 jit_solution(11123709533120761558)
XLA Ops:
  0.6 0.7 pad_add_fusion.where
  1.3 2.7 %plan.1 = (s32[2,20]{1,0:T(2,128)S(1)}, s32[11]{0:T(128)S(1)}) custom-call(s32[12]{0:T(128)} %assign.1, s32[2]{0:T(128)} %pad_add_fusion.where), custom_call_target="tpu_custom_call" | custom-call | tf_op jit(solution)/shard_map/plan/pallas_call | solution.py:160
  4.0 8.6 %gram.1 = (bf16[1,1280,256]{2,1,0:T(8,128)(2,1)}, bf16[1,1280,256]{2,1,0:T(8,128)(2,1)}, bf16[2,1280,256]{2,1,0:T(8,128)(2,1)}, bf16[2,1280,256]{2,1,0:T(8,128)(2,1)}) custom-call(s32[11]{0:T(128)S(1)} %get-tuple-element.642.meta, bf16[3,1024,896]{2,1,0:T(8,128)(2,1)} %x_ref.7), custom_call_target="tpu_custom_call" | custom-call | flops 3523215360 | bytes 9437184 | tf_op jit(solution)/shard_map/gram/pallas_call | solution.py:342
  12.6 0.5 collective-permute-start.37
  13.1 1.9 collective-permute-done.37
  15.0 1.3 fusion.7
  16.3 2.9 %collective-permute-start.38 = (bf16[1,320,256]{2,1,0:T(8,128)(2,1)S(1)}, bf16[1,320,256]{2,1,0:T(8,128)(2,1)S(1)}, u32[]{:S(2)}, u32[]{:S(2)}) collective-permute-start(bf16[1,320,256]{2,1,0:T(8,128)(2,1)S(1)} %get-tuple-element.492), channel_id=1, source_target_pairs={{0,2},{1,3},{2,0},{3,1},{4,6},{5,7},{6,4},{7,5},{8,10},{9,11},{10,... | collective-permute-start | bytes 491528 | tf_op jit(solution)/shard_map/ppermute | solution.py:363
  19.3 1.5 collective-permute-start.40
  21.2 2.0 collective-permute-start.27
  23.2 1.5 collective-permute-start.29
  24.7 1.6 collective-permute-start.28
  26.3 3.0 %collective-permute-done.40 = bf16[1,320,256]{2,1,0:T(8,128)(2,1)S(1)} collective-permute-done((bf16[1,320,256]{2,1,0:T(8,128)(2,1)S(1)}, bf16[1,320,256]{2,1,0:T(8,128)(2,1)S(1)}, u32[]{:S(2)}, u32[]{:S(2)}) %collective-permute-start.40) | collective-permute-done | bytes 163872 | tf_op jit(solution)/shard_map/ppermute | solution.py:363
  29.3 1.9 collective-permute-done.39
  31.4 1.5 collective-permute-start.43
  32.9 1.9 collective-permute-done.27
  34.8 2.1 collective-permute-start.42
  36.9 6.6 %collective-permute-done.29 = bf16[2,320,256]{2,1,0:T(8,128)(2,1)S(1)} collective-permute-done((bf16[2,320,256]{2,1,0:T(8,128)(2,1)S(1)}, bf16[2,320,256]{2,1,0:T(8,128)(2,1)S(1)}, u32[]{:S(2)}, u32[]{:S(2)}) %collective-permute-start.29) | collective-permute-done | bytes 327712 | tf_op jit(solution)/shard_map/ppermute | solution.py:363
  43.5 1.5 collective-permute-start.41
  45.0 3.8 %collective-permute-done.28 = bf16[2,320,256]{2,1,0:T(8,128)(2,1)S(1)} collective-permute-done((bf16[2,320,256]{2,1,0:T(8,128)(2,1)S(1)}, bf16[2,320,256]{2,1,0:T(8,128)(2,1)S(1)}, u32[]{:S(2)}, u32[]{:S(2)}) %collective-permute-start.28) | collective-permute-done | bytes 327712 | tf_op jit(solution)/shard_map/ppermute | solution.py:363
  49.0 1.5 collective-permute-start.32
  50.5 1.5 collective-permute-start.31
  52.0 0.5 collective-permute-start.30
  52.6 5.5 %collective-permute-done.42.rest_2_ = bf16[1,320,256]{2,1,0:T(8,128)(2,1)S(1)} collective-permute-done((bf16[1,320,256]{2,1,0:T(8,128)(2,1)S(1)}, bf16[1,320,256]{2,1,0:T(8,128)(2,1)S(1)}, u32[]{:S(2)}, u32[]{:S(2)}) %collective-permute-start.42) | collective-permute-done | bytes 163872 | tf_op jit(solution)/shard_map/ppermute | solution.py:363
  58.1 0.5 collective-permute-start.46
  58.6 0.9 collective-permute-done.47.rest_7_
  60.3 4.8 %collective-permute-done.31.rest_2_ = bf16[2,320,256]{2,1,0:T(8,128)(2,1)S(1)} collective-permute-done((bf16[2,320,256]{2,1,0:T(8,128)(2,1)S(1)}, bf16[2,320,256]{2,1,0:T(8,128)(2,1)S(1)}, u32[]{:S(2)}, u32[]{:S(2)}) %collective-permute-start.31) | collective-permute-done | bytes 327712 | tf_op jit(solution)/shard_map/ppermute | solution.py:363
  65.1 0.5 collective-permute-start.34
  65.6 0.7 copy-done.22
  66.3 8.6 %update.3 = (bf16[3,1024,896]{2,1,0:T(8,128)(2,1)}, bf16[512,896]{1,0:T(8,128)(2,1)}, bf16[512,896]{1,0:T(8,128)(2,1)}) custom-call(s32[11]{0:T(128)S(1)} %get-tuple-element.642.meta, bf16[3,1024,896]{2,1,0:T(8,128)(2,1)} %x_ref.7, bf16[1,320,256]{2,1,0:T(8,128)(2,1)} %copy-done.9, bf16[1,320,256]{2,1,0:T(8,128)(2,1)} %copy-done.19, ...), custom_call_target="tpu_custom_call" | custom-call | flops 3758096384 | bytes 5505024 | tf_op jit(solution)/shard_map/update/pallas_call | solution.py:448
  75.0 1.3 collective-permute-start.49
  76.3 4.6 %collective-permute-start.48 = (bf16[512,896]{1,0:T(8,128)(2,1)}, bf16[512,896]{1,0:T(8,128)(2,1)S(1)}, u32[]{:S(2)}, u32[]{:S(2)}) collective-permute-start(bf16[512,896]{1,0:T(8,128)(2,1)} %get-tuple-element.452), channel_id=1, source_target_pairs={{0,8},{8,16},{16,24},{1,9},{9,17},{17,25},{2,10},{10,18},{18,26},{... | collective-permute-start | bytes 2752520 | tf_op jit(solution)/shard_map/ppermute | solution.py:211
  81.0 1.3 collective-permute-start.51
  82.3 5.5 %collective-permute-start.50 = (bf16[512,896]{1,0:T(8,128)(2,1)}, bf16[512,896]{1,0:T(8,128)(2,1)}, u32[]{:S(2)}, u32[]{:S(2)}) collective-permute-start(bf16[512,896]{1,0:T(8,128)(2,1)} %get-tuple-element.453), channel_id=1, source_target_pairs={{0,8},{8,16},{16,24},{1,9},{9,17},{17,25},{2,10},{10,18},{18,26},{... | collective-permute-start | bytes 2752520 | tf_op jit(solution)/shard_map/ppermute | solution.py:211
  87.8 0.7 copy-done.8
  88.5 4.0 %update.4.rest_8_ = bf16[3,1024,896]{2,1,0:T(8,128)(2,1)} custom-call(s32[11]{0:T(128)S(1)} %get-tuple-element.642.meta, bf16[3,1024,896]{2,1,0:T(8,128)(2,1)} %x_ref.7, bf16[2,320,256]{2,1,0:T(8,128)(2,1)} %copy-done, bf16[2,320,256]{2,1,0:T(8,128)(2,1)} %copy-done.4, bf16[2,320,256]{2,1,0:T(8,128)(2,1)} %copy-done.3, ...), custom_call_target="tpu_custom_call", output_to_operand_aliasing={{}: (10, {})} | custom-call | flops 3758096384 | bytes 5505024 | tf_op jit(solution)/shard_map/update/pallas_call | solution.py:448
  92.5 3.8 %update.5.update_ref = bf16[3,1024,896]{2,1,0:T(8,128)(2,1)} custom-call(s32[11]{0:T(128)S(1)} %get-tuple-element.642.meta, bf16[3,1024,896]{2,1,0:T(8,128)(2,1)} %x_ref.7, bf16[2,320,256]{2,1,0:T(8,128)(2,1)} %copy-done, bf16[2,320,256]{2,1,0:T(8,128)(2,1)} %copy-done.4, bf16[2,320,256]{2,1,0:T(8,128)(2,1)} %copy-done.3, ...), custom_call_target="tpu_custom_call", output_to_operand_aliasing={{}: (10, {})} | custom-call | flops 3758096384 | bytes 5505024 | tf_op jit(solution)/shard_map/update/pallas_call | solution.py:448
  96.3 4.0 %collective-permute-done.49.rest_1_ = bf16[512,896]{1,0:T(8,128)(2,1)S(1)} collective-permute-done((bf16[512,896]{1,0:T(8,128)(2,1)}, bf16[512,896]{1,0:T(8,128)(2,1)S(1)}, u32[]{:S(2)}, u32[]{:S(2)}) %collective-permute-start.49) | collective-permute-done | bytes 917536 | tf_op jit(solution)/shard_map/ppermute | solution.py:212
  100.3 1.6 collective-permute-done.48.rest_0_
  102.0 3.4 %pick.26 = (bf16[512,896]{1,0:T(8,128)(2,1)}, bf16[512,896]{1,0:T(8,128)(2,1)}) custom-call(s32[2,20]{1,0:T(2,128)S(1)} %get-tuple-element.644.snd, bf16[6,512,896]{2,1,0:T(8,128)(2,1)} %bitcast.19.own, bf16[512,896]{1,0:T(8,128)(2,1)S(1)} %collective-permute-done.48.rest_0_, bf16[512,896]{1,0:T(8,128)(2,1)S(1)} %collective-permute-done.49.rest_1_), custom_call_target="tpu_custom_call" | custom-call | bytes 1 | tf_op jit(solution)/shard_map/pick/pallas_call | solution.py:196
  105.4 4.1 %collective-permute-start.52 = (bf16[512,896]{1,0:T(8,128)(2,1)}, bf16[512,896]{1,0:T(8,128)(2,1)}, u32[]{:S(2)}, u32[]{:S(2)}) collective-permute-start(bf16[512,896]{1,0:T(8,128)(2,1)} %get-tuple-element.455), channel_id=1, source_target_pairs={{0,8},{8,16},{16,24},{1,9},{9,17},{17,25},{2,10},{10,18},{18,26},{... | collective-permute-start | bytes 2752520 | tf_op jit(solution)/shard_map/ppermute | solution.py:211
  109.5 1.3 collective-permute-start.53
  110.8 9.2 %collective-permute-done.51.rest_3_ = bf16[512,896]{1,0:T(8,128)(2,1)S(1)} collective-permute-done((bf16[512,896]{1,0:T(8,128)(2,1)}, bf16[512,896]{1,0:T(8,128)(2,1)S(1)}, u32[]{:S(2)}, u32[]{:S(2)}) %collective-permute-start.51) | collective-permute-done | bytes 917536 | tf_op jit(solution)/shard_map/ppermute | solution.py:212
  120.0 1.6 collective-permute-done.50.rest_2_
  121.6 3.5 %pick.27 = (bf16[512,896]{1,0:T(8,128)(2,1)}, bf16[512,896]{1,0:T(8,128)(2,1)}) custom-call(s32[2,20]{1,0:T(2,128)S(1)} %get-tuple-element.644.snd, bf16[6,512,896]{2,1,0:T(8,128)(2,1)} %bitcast.19.own, bf16[512,896]{1,0:T(8,128)(2,1)S(1)} %collective-permute-done.48.rest_0_, bf16[512,896]{1,0:T(8,128)(2,1)S(1)} %collective-permute-done.49.rest_1_, ...), custom_call_target="tpu_custom_call" | custom-call | bytes 1 | tf_op jit(solution)/shard_map/pick/pallas_call | solution.py:196
  125.1 4.9 %collective-permute-start.54 = (bf16[512,896]{1,0:T(8,128)(2,1)}, bf16[512,896]{1,0:T(8,128)(2,1)}, u32[]{:S(2)}, u32[]{:S(2)}) collective-permute-start(bf16[512,896]{1,0:T(8,128)(2,1)} %get-tuple-element.457), channel_id=1, source_target_pairs={{0,8},{8,16},{16,24},{1,9},{9,17},{17,25},{2,10},{10,18},{18,26},{... | collective-permute-start | bytes 2752520 | tf_op jit(solution)/shard_map/ppermute | solution.py:211
  130.0 1.3 collective-permute-start.55
  131.3 9.9 %collective-permute-done.52.rest_4_ = bf16[512,896]{1,0:T(8,128)(2,1)} collective-permute-done((bf16[512,896]{1,0:T(8,128)(2,1)}, bf16[512,896]{1,0:T(8,128)(2,1)}, u32[]{:S(2)}, u32[]{:S(2)}) %collective-permute-start.52) | collective-permute-done | bytes 917536 | tf_op jit(solution)/shard_map/ppermute | solution.py:211
  141.3 3.6 %place.1._ = bf16[2,1024,896]{2,1,0:T(8,128)(2,1)} custom-call(s32[11]{0:T(128)S(1)} %get-tuple-element.642.meta, bf16[3,1024,896]{2,1,0:T(8,128)(2,1)} %update.5.update_ref, bf16[512,896]{1,0:T(8,128)(2,1)S(1)} %collective-permute-done.48.rest_0_, bf16[512,896]{1,0:T(8,128)(2,1)S(1)} %collective-permute-done.49.rest_1_, ...), custom_call_target="tpu_custom_call" | custom-call | flops 5000000000 | bytes 1 | tf_op jit(solution)/shard_map/place/pallas_call | solution.py:275
  144.9 14.8 %collective-permute-done.54.rest_0_ = bf16[512,896]{1,0:T(8,128)(2,1)} collective-permute-done((bf16[512,896]{1,0:T(8,128)(2,1)}, bf16[512,896]{1,0:T(8,128)(2,1)}, u32[]{:S(2)}, u32[]{:S(2)}) %collective-permute-start.54) | collective-permute-done | bytes 917536 | tf_op jit(solution)/shard_map/ppermute | solution.py:211
  159.7 2.4 %last.25 = bf16[2,1024,896]{2,1,0:T(8,128)(2,1)} custom-call(s32[11]{0:T(128)S(1)} %get-tuple-element.642.meta, bf16[2,1024,896]{2,1,0:T(8,128)(2,1)} %place.1._, bf16[512,896]{1,0:T(8,128)(2,1)} %collective-permute-done.54.rest_0_, bf16[512,896]{1,0:T(8,128)(2,1)} %collective-permute-done.55.rest_1_), custom_call_target="tpu_custom_call", output_to_operand_aliasing={{}: (1, {})} | custom-call | flops 5000000000 | bytes 1 | tf_op jit(solution)/shard_map/last/pallas_call | solution.py:288
  162.2 53.8 %conditional.1 = (bf16[1,2,1024,896]{3,2,1,0:T(8,128)(2,1)}) conditional(s32[]{:T(128)} %bitcast.18, bf16[2,1024,896]{2,1,0:T(8,128)(2,1)} %last.25, (bf16[3,1024,896]{2,1,0:T(8,128)(2,1)}, s32[2,20]{1,0:T(2,128)S(1)}, bf16[512,896]{1,0:T(8,128)(2,1)S(1)}, bf16[512,896]{1,0:T(8,128)(2,1)S(1)}, ...), branch_computations={%region_0.0_spmd, %region_1.0_spmd, %region_2.0_spmd, %region_3.0_... | conditional | flops 29999998976 | bytes 51380772 | solution.py:579
  162.2 3.4 %pick.14 = (bf16[512,896]{1,0:T(8,128)(2,1)}, bf16[512,896]{1,0:T(8,128)(2,1)}) custom-call(s32[2,20]{1,0:T(2,128)S(1)} %get-tuple-element.343.snd, bf16[6,512,896]{2,1,0:T(8,128)(2,1)} %bitcast.1.own, bf16[512,896]{1,0:T(8,128)(2,1)S(1)} %get-tuple-element.345.rest_0_, bf16[512,896]{1,0:T(8,128)(2,1)S(1)} %get-tuple-element.346.rest_1_, ...), custom_call_target="tpu_custom_call" | custom-call | bytes 1 | tf_op jit(solution)/shard_map/cond/branch_1_fun/pick/pallas_call | solution.py:196
  165.6 4.3 %collective-permute-start = (bf16[512,896]{1,0:T(8,128)(2,1)}, bf16[512,896]{1,0:T(8,128)(2,1)}, u32[]{:S(2)}, u32[]{:S(2)}) collective-permute-start(bf16[512,896]{1,0:T(8,128)(2,1)} %get-tuple-element.351), channel_id=1, source_target_pairs={{0,8},{8,16},{16,24},{1,9},{9,17},{17,25},{2,10},{10,18},{18,26},{... | collective-permute-start | bytes 2752520 | tf_op jit(solution)/shard_map/cond/branch_1_fun/ppermute | solution.py:211
  169.9 1.3 collective-permute-start.1
  171.2 3.4 %pick.15 = (bf16[512,896]{1,0:T(8,128)(2,1)}, bf16[512,896]{1,0:T(8,128)(2,1)}) custom-call(s32[2,20]{1,0:T(2,128)S(1)} %get-tuple-element.343.snd, bf16[6,512,896]{2,1,0:T(8,128)(2,1)} %bitcast.1.own, bf16[512,896]{1,0:T(8,128)(2,1)S(1)} %get-tuple-element.345.rest_0_, bf16[512,896]{1,0:T(8,128)(2,1)S(1)} %get-tuple-element.346.rest_1_, ...), custom_call_target="tpu_custom_call" | custom-call | bytes 1 | tf_op jit(solution)/shard_map/cond/branch_1_fun/pick/pallas_call | solution.py:196
  174.6 4.5 %collective-permute-start.2 = (bf16[512,896]{1,0:T(8,128)(2,1)}, bf16[512,896]{1,0:T(8,128)(2,1)S(1)}, u32[]{:S(2)}, u32[]{:S(2)}) collective-permute-start(bf16[512,896]{1,0:T(8,128)(2,1)} %get-tuple-element.355), channel_id=1, source_target_pairs={{0,8},{8,16},{16,24},{1,9},{9,17},{17,25},{2,10},{10,18},{18,26},{... | collective-permute-start | bytes 2752520 | tf_op jit(solution)/shard_map/cond/branch_1_fun/ppermute | solution.py:211
  179.1 1.3 collective-permute-start.3
  180.4 9.7 %collective-permute-done.rest_0_ = bf16[512,896]{1,0:T(8,128)(2,1)} collective-permute-done((bf16[512,896]{1,0:T(8,128)(2,1)}, bf16[512,896]{1,0:T(8,128)(2,1)}, u32[]{:S(2)}, u32[]{:S(2)}) %collective-permute-start) | collective-permute-done | bytes 917536 | tf_op jit(solution)/shard_map/cond/branch_1_fun/ppermute | solution.py:211
  190.1 5.3 %collective-permute-done.1.rest_1_ = bf16[512,896]{1,0:T(8,128)(2,1)} collective-permute-done((bf16[512,896]{1,0:T(8,128)(2,1)}, bf16[512,896]{1,0:T(8,128)(2,1)}, u32[]{:S(2)}, u32[]{:S(2)}) %collective-permute-start.1) | collective-permute-done | bytes 917536 | tf_op jit(solution)/shard_map/cond/branch_1_fun/ppermute | solution.py:212
  195.4 2.4 %last.13._ = bf16[2,1024,896]{2,1,0:T(8,128)(2,1)} custom-call(s32[11]{0:T(128)S(1)} %get-tuple-element.341.meta, bf16[2,1024,896]{2,1,0:T(8,128)(2,1)} %get-tuple-element.342._, bf16[512,896]{1,0:T(8,128)(2,1)} %collective-permute-done.rest_0_, bf16[512,896]{1,0:T(8,128)(2,1)} %collective-permute-done.1.rest_1_), custom_call_target="tpu_custom_call", output_to_operand_aliasing={{}: (1, {})} | custom-call | flops 5000000000 | bytes 1 | tf_op jit(solution)/shard_map/cond/branch_1_fun/last/pallas_call | solution.py:288
  197.8 9.8 %collective-permute-done.2.rest_0_ = bf16[512,896]{1,0:T(8,128)(2,1)S(1)} collective-permute-done((bf16[512,896]{1,0:T(8,128)(2,1)}, bf16[512,896]{1,0:T(8,128)(2,1)S(1)}, u32[]{:S(2)}, u32[]{:S(2)}) %collective-permute-start.2) | collective-permute-done | bytes 917536 | tf_op jit(solution)/shard_map/cond/branch_1_fun/ppermute | solution.py:211
  207.6 4.9 %collective-permute-done.3.rest_1_ = bf16[512,896]{1,0:T(8,128)(2,1)S(1)} collective-permute-done((bf16[512,896]{1,0:T(8,128)(2,1)}, bf16[512,896]{1,0:T(8,128)(2,1)S(1)}, u32[]{:S(2)}, u32[]{:S(2)}) %collective-permute-start.3) | collective-permute-done | bytes 917536 | tf_op jit(solution)/shard_map/cond/branch_1_fun/ppermute | solution.py:212
  212.6 0.9 copy-done.11
  213.5 2.4 %last.14 = bf16[2,1024,896]{2,1,0:T(8,128)(2,1)} custom-call(s32[11]{0:T(128)S(1)} %get-tuple-element.341.meta, bf16[2,1024,896]{2,1,0:T(8,128)(2,1)} %last.13._, bf16[512,896]{1,0:T(8,128)(2,1)} %copy-done.10, bf16[512,896]{1,0:T(8,128)(2,1)} %copy-done.11), custom_call_target="tpu_custom_call", output_to_operand_aliasing={{}: (1, {})} | custom-call | flops 5000000000 | bytes 1 | tf_op jit(solution)/shard_map/cond/branch_1_fun/last/pallas_call | solution.py:288
  (63 shorter events, 1.8 us)
Async XLA Ops:
  12.6 8.2 %copy-start.1 = (bf16[2,1280,256]{2,1,0:T(8,128)(2,1)S(1)}, bf16[2,1280,256]{2,1,0:T(8,128)(2,1)}, u32[]{:S(2)}) copy-start(bf16[2,1280,256]{2,1,0:T(8,128)(2,1)} %get-tuple-element.447) | copy-start | bytes 3932164
  12.6 2.4 %collective-permute-start.37 = (bf16[1,1280,256]{2,1,0:T(8,128)(2,1)}, bf16[1,1280,256]{2,1,0:T(8,128)(2,1)S(1)}, u32[]{:S(2)}, u32[]{:S(2)}) collective-permute-start(bf16[1,1280,256]{2,1,0:T(8,128)(2,1)} %get-tuple-element.450), channel_id=1, source_target_pairs={{0,1},{1,0},{2,3},{3,2},{4,5},{5,4},{6,7},{7,6},{8,9},{9,8},{10,11... | collective-permute-start | bytes 1966088 | tf_op jit(solution)/shard_map/ppermute | solution.py:363
  13.0 7.8 %collective-permute-start.26 = (bf16[2,1280,256]{2,1,0:T(8,128)(2,1)}, bf16[2,1280,256]{2,1,0:T(8,128)(2,1)S(1)}, u32[]{:S(2)}, u32[]{:S(2)}) collective-permute-start(bf16[2,1280,256]{2,1,0:T(8,128)(2,1)} %get-tuple-element.448), channel_id=1, source_target_pairs={{0,1},{1,0},{2,3},{3,2},{4,5},{5,4},{6,7},{7,6},{8,9},{9,8},{10,11... | collective-permute-start | bytes 3932168 | tf_op jit(solution)/shard_map/ppermute | solution.py:363
  16.3 8.4 %collective-permute-start.38 = (bf16[1,320,256]{2,1,0:T(8,128)(2,1)S(1)}, bf16[1,320,256]{2,1,0:T(8,128)(2,1)S(1)}, u32[]{:S(2)}, u32[]{:S(2)}) collective-permute-start(bf16[1,320,256]{2,1,0:T(8,128)(2,1)S(1)} %get-tuple-element.492), channel_id=1, source_target_pairs={{0,2},{1,3},{2,0},{3,1},{4,6},{5,7},{6,4},{7,5},{8,10},{9,11},{10,... | collective-permute-start | bytes 491528 | tf_op jit(solution)/shard_map/ppermute | solution.py:363
  19.3 10.1 %collective-permute-start.40 = (bf16[1,320,256]{2,1,0:T(8,128)(2,1)S(1)}, bf16[1,320,256]{2,1,0:T(8,128)(2,1)S(1)}, u32[]{:S(2)}, u32[]{:S(2)}) collective-permute-start(bf16[1,320,256]{2,1,0:T(8,128)(2,1)S(1)} %get-tuple-element.493), channel_id=1, source_target_pairs={{0,6},{1,7},{2,4},{3,5},{4,2},{5,3},{6,0},{7,1},{8,14},{9,15},{10,... | collective-permute-start | bytes 491528 | tf_op jit(solution)/shard_map/ppermute | solution.py:363
  20.8 10.5 %collective-permute-start.39 = (bf16[1,320,256]{2,1,0:T(8,128)(2,1)S(1)}, bf16[1,320,256]{2,1,0:T(8,128)(2,1)S(1)}, u32[]{:S(2)}, u32[]{:S(2)}) collective-permute-start(bf16[1,320,256]{2,1,0:T(8,128)(2,1)S(1)} %get-tuple-element.494), channel_id=1, source_target_pairs={{0,4},{1,5},{2,6},{3,7},{4,0},{5,1},{6,2},{7,3},{8,12},{9,13},{10,... | collective-permute-start | bytes 491528 | tf_op jit(solution)/shard_map/ppermute | solution.py:363
  21.2 13.6 %collective-permute-start.27 = (bf16[2,320,256]{2,1,0:T(8,128)(2,1)S(1)}, bf16[2,320,256]{2,1,0:T(8,128)(2,1)S(1)}, u32[]{:S(2)}, u32[]{:S(2)}) collective-permute-start(bf16[2,320,256]{2,1,0:T(8,128)(2,1)S(1)} %get-tuple-element.489), channel_id=1, source_target_pairs={{0,2},{1,3},{2,0},{3,1},{4,6},{5,7},{6,4},{7,5},{8,10},{9,11},{10,... | collective-permute-start | bytes 983048 | tf_op jit(solution)/shard_map/ppermute | solution.py:363
  23.2 20.2 %collective-permute-start.29 = (bf16[2,320,256]{2,1,0:T(8,128)(2,1)S(1)}, bf16[2,320,256]{2,1,0:T(8,128)(2,1)S(1)}, u32[]{:S(2)}, u32[]{:S(2)}) collective-permute-start(bf16[2,320,256]{2,1,0:T(8,128)(2,1)S(1)} %get-tuple-element.490), channel_id=1, source_target_pairs={{0,6},{1,7},{2,4},{3,5},{4,2},{5,3},{6,0},{7,1},{8,14},{9,15},{10,... | collective-permute-start | bytes 983048 | tf_op jit(solution)/shard_map/ppermute | solution.py:363
  24.7 24.1 %collective-permute-start.28 = (bf16[2,320,256]{2,1,0:T(8,128)(2,1)S(1)}, bf16[2,320,256]{2,1,0:T(8,128)(2,1)S(1)}, u32[]{:S(2)}, u32[]{:S(2)}) collective-permute-start(bf16[2,320,256]{2,1,0:T(8,128)(2,1)S(1)} %get-tuple-element.491), channel_id=1, source_target_pairs={{0,4},{1,5},{2,6},{3,7},{4,0},{5,1},{6,2},{7,3},{8,12},{9,13},{10,... | collective-permute-start | bytes 983048 | tf_op jit(solution)/shard_map/ppermute | solution.py:363
  31.3 34.3 %copy-start.9 = (bf16[1,320,256]{2,1,0:T(8,128)(2,1)}, bf16[1,320,256]{2,1,0:T(8,128)(2,1)S(1)}, u32[]{:S(2)}) copy-start(bf16[1,320,256]{2,1,0:T(8,128)(2,1)S(1)} %fusion.6.rest_0_) | copy-start | bytes 491524
  31.3 19.2 %collective-permute-start.44 = (bf16[1,320,256]{2,1,0:T(8,128)(2,1)S(1)}, bf16[1,320,256]{2,1,0:T(8,128)(2,1)S(1)}, u32[]{:S(2)}, u32[]{:S(2)}) collective-permute-start(bf16[1,320,256]{2,1,0:T(8,128)(2,1)S(1)} %fusion.6.rest_0_), channel_id=1, source_target_pairs={{0,1},{1,0},{2,3},{3,2},{4,5},{5,4},{6,7},{7,6},{8,9},{9,8},{10,11... | collective-permute-start | bytes 491528 | tf_op jit(solution)/shard_map/ppermute | solution.py:363
  31.4 20.6 %collective-permute-start.43 = (bf16[1,320,256]{2,1,0:T(8,128)(2,1)S(1)}, bf16[1,320,256]{2,1,0:T(8,128)(2,1)S(1)}, u32[]{:S(2)}, u32[]{:S(2)}) collective-permute-start(bf16[1,320,256]{2,1,0:T(8,128)(2,1)S(1)} %fusion.6.rest_0_), channel_id=1, source_target_pairs={{0,6},{1,7},{2,4},{3,5},{4,2},{5,3},{6,0},{7,1},{8,14},{9,15},{10,... | collective-permute-start | bytes 491528 | tf_op jit(solution)/shard_map/ppermute | solution.py:363
  34.8 23.2 %collective-permute-start.42 = (bf16[1,320,256]{2,1,0:T(8,128)(2,1)S(1)}, bf16[1,320,256]{2,1,0:T(8,128)(2,1)S(1)}, u32[]{:S(2)}, u32[]{:S(2)}) collective-permute-start(bf16[1,320,256]{2,1,0:T(8,128)(2,1)S(1)} %fusion.6.rest_0_), channel_id=1, source_target_pairs={{0,4},{1,5},{2,6},{3,7},{4,0},{5,1},{6,2},{7,3},{8,12},{9,13},{10,... | collective-permute-start | bytes 491528 | tf_op jit(solution)/shard_map/ppermute | solution.py:363
  43.5 14.6 %collective-permute-start.41 = (bf16[1,320,256]{2,1,0:T(8,128)(2,1)S(1)}, bf16[1,320,256]{2,1,0:T(8,128)(2,1)S(1)}, u32[]{:S(2)}, u32[]{:S(2)}) collective-permute-start(bf16[1,320,256]{2,1,0:T(8,128)(2,1)S(1)} %fusion.6.rest_0_), channel_id=1, source_target_pairs={{0,2},{1,3},{2,0},{3,1},{4,6},{5,7},{6,4},{7,5},{8,10},{9,11},{10,... | collective-permute-start | bytes 491528 | tf_op jit(solution)/shard_map/ppermute | solution.py:363
  49.0 26.0 %copy-start = (bf16[2,320,256]{2,1,0:T(8,128)(2,1)}, bf16[2,320,256]{2,1,0:T(8,128)(2,1)S(1)}, u32[]{:S(2)}) copy-start(bf16[2,320,256]{2,1,0:T(8,128)(2,1)S(1)} %fusion.3.rest_0_) | copy-start | bytes 983044
  49.0 11.3 %collective-permute-start.32 = (bf16[2,320,256]{2,1,0:T(8,128)(2,1)S(1)}, bf16[2,320,256]{2,1,0:T(8,128)(2,1)S(1)}, u32[]{:S(2)}, u32[]{:S(2)}) collective-permute-start(bf16[2,320,256]{2,1,0:T(8,128)(2,1)S(1)} %fusion.3.rest_0_), channel_id=1, source_target_pairs={{0,6},{1,7},{2,4},{3,5},{4,2},{5,3},{6,0},{7,1},{8,14},{9,15},{10,... | collective-permute-start | bytes 983048 | tf_op jit(solution)/shard_map/ppermute | solution.py:363
  50.5 15.1 %copy-start.16 = (bf16[1,320,256]{2,1,0:T(8,128)(2,1)}, bf16[1,320,256]{2,1,0:T(8,128)(2,1)S(1)}, u32[]{:S(2)}) copy-start(bf16[1,320,256]{2,1,0:T(8,128)(2,1)S(1)} %collective-permute-done.44.rest_4_) | copy-start | bytes 491524
  50.5 14.6 %collective-permute-start.31 = (bf16[2,320,256]{2,1,0:T(8,128)(2,1)S(1)}, bf16[2,320,256]{2,1,0:T(8,128)(2,1)S(1)}, u32[]{:S(2)}, u32[]{:S(2)}) collective-permute-start(bf16[2,320,256]{2,1,0:T(8,128)(2,1)S(1)} %fusion.3.rest_0_), channel_id=1, source_target_pairs={{0,4},{1,5},{2,6},{3,7},{4,0},{5,1},{6,2},{7,3},{8,12},{9,13},{10,... | collective-permute-start | bytes 983048 | tf_op jit(solution)/shard_map/ppermute | solution.py:363
  52.0 13.6 %copy-start.17 = (bf16[1,320,256]{2,1,0:T(8,128)(2,1)}, bf16[1,320,256]{2,1,0:T(8,128)(2,1)S(1)}, u32[]{:S(2)}) copy-start(bf16[1,320,256]{2,1,0:T(8,128)(2,1)S(1)} %collective-permute-done.43.rest_3_) | copy-start | bytes 491524
  52.0 13.0 %collective-permute-start.30 = (bf16[2,320,256]{2,1,0:T(8,128)(2,1)S(1)}, bf16[2,320,256]{2,1,0:T(8,128)(2,1)S(1)}, u32[]{:S(2)}, u32[]{:S(2)}) collective-permute-start(bf16[2,320,256]{2,1,0:T(8,128)(2,1)S(1)} %fusion.3.rest_0_), channel_id=1, source_target_pairs={{0,2},{1,3},{2,0},{3,1},{4,6},{5,7},{6,4},{7,5},{8,10},{9,11},{10,... | collective-permute-start | bytes 983048 | tf_op jit(solution)/shard_map/ppermute | solution.py:363
  58.1 7.5 %copy-start.18 = (bf16[1,320,256]{2,1,0:T(8,128)(2,1)}, bf16[1,320,256]{2,1,0:T(8,128)(2,1)S(1)}, u32[]{:S(2)}) copy-start(bf16[1,320,256]{2,1,0:T(8,128)(2,1)S(1)} %collective-permute-done.42.rest_2_) | copy-start | bytes 491524
  58.1 1.4 collective-permute-start.47
  58.1 7.5 %copy-start.19 = (bf16[1,320,256]{2,1,0:T(8,128)(2,1)}, bf16[1,320,256]{2,1,0:T(8,128)(2,1)S(1)}, u32[]{:S(2)}) copy-start(bf16[1,320,256]{2,1,0:T(8,128)(2,1)S(1)} %collective-permute-done.41.rest_1_) | copy-start | bytes 491524
  58.1 1.6 collective-permute-start.46
  59.5 6.2 %copy-start.20 = (bf16[1,320,256]{2,1,0:T(8,128)(2,1)}, bf16[1,320,256]{2,1,0:T(8,128)(2,1)S(1)}, u32[]{:S(2)}) copy-start(bf16[1,320,256]{2,1,0:T(8,128)(2,1)S(1)} %collective-permute-done.47.rest_7_) | copy-start | bytes 491524
  59.5 6.1 %collective-permute-start.45 = (bf16[1,320,256]{2,1,0:T(8,128)(2,1)S(1)}, bf16[1,320,256]{2,1,0:T(8,128)(2,1)S(1)}, u32[]{:S(2)}, u32[]{:S(2)}) collective-permute-start(bf16[1,320,256]{2,1,0:T(8,128)(2,1)S(1)} %collective-permute-done.41.rest_1_), channel_id=1, source_target_pairs={{0,1},{1,0},{2,3},{3,2},{4,5},{5,4},{6,7},{7,6},{8,9},{9,8},{10,11... | collective-permute-start | bytes 491528 | tf_op jit(solution)/shard_map/ppermute | solution.py:363
  59.7 5.9 %copy-start.21 = (bf16[1,320,256]{2,1,0:T(8,128)(2,1)}, bf16[1,320,256]{2,1,0:T(8,128)(2,1)S(1)}, u32[]{:S(2)}) copy-start(bf16[1,320,256]{2,1,0:T(8,128)(2,1)S(1)} %collective-permute-done.46.rest_6_) | copy-start | bytes 491524
  59.7 16.6 %collective-permute-start.33 = (bf16[2,320,256]{2,1,0:T(8,128)(2,1)S(1)}, bf16[2,320,256]{2,1,0:T(8,128)(2,1)S(1)}, u32[]{:S(2)}, u32[]{:S(2)}) collective-permute-start(bf16[2,320,256]{2,1,0:T(8,128)(2,1)S(1)} %fusion.3.rest_0_), channel_id=1, source_target_pairs={{0,1},{1,0},{2,3},{3,2},{4,5},{5,4},{6,7},{7,6},{8,9},{9,8},{10,11... | collective-permute-start | bytes 983048 | tf_op jit(solution)/shard_map/ppermute | solution.py:363
  60.3 14.7 %copy-start.2 = (bf16[2,320,256]{2,1,0:T(8,128)(2,1)}, bf16[2,320,256]{2,1,0:T(8,128)(2,1)S(1)}, u32[]{:S(2)}) copy-start(bf16[2,320,256]{2,1,0:T(8,128)(2,1)S(1)} %collective-permute-done.32.rest_3_) | copy-start | bytes 983044
  60.3 20.7 %collective-permute-start.36 = (bf16[2,320,256]{2,1,0:T(8,128)(2,1)S(1)}, bf16[2,320,256]{2,1,0:T(8,128)(2,1)S(1)}, u32[]{:S(2)}, u32[]{:S(2)}) collective-permute-start(bf16[2,320,256]{2,1,0:T(8,128)(2,1)S(1)} %collective-permute-done.32.rest_3_), channel_id=1, source_target_pairs={{0,1},{1,0},{2,3},{3,2},{4,5},{5,4},{6,7},{7,6},{8,9},{9,8},{10,11... | collective-permute-start | bytes 983048 | tf_op jit(solution)/shard_map/ppermute | solution.py:363
  65.1 9.9 %copy-start.3 = (bf16[2,320,256]{2,1,0:T(8,128)(2,1)}, bf16[2,320,256]{2,1,0:T(8,128)(2,1)S(1)}, u32[]{:S(2)}) copy-start(bf16[2,320,256]{2,1,0:T(8,128)(2,1)S(1)} %collective-permute-done.31.rest_2_) | copy-start | bytes 983044
  65.1 17.2 %collective-permute-start.35 = (bf16[2,320,256]{2,1,0:T(8,128)(2,1)S(1)}, bf16[2,320,256]{2,1,0:T(8,128)(2,1)S(1)}, u32[]{:S(2)}, u32[]{:S(2)}) collective-permute-start(bf16[2,320,256]{2,1,0:T(8,128)(2,1)S(1)} %collective-permute-done.31.rest_2_), channel_id=1, source_target_pairs={{0,1},{1,0},{2,3},{3,2},{4,5},{5,4},{6,7},{7,6},{8,9},{9,8},{10,11... | collective-permute-start | bytes 983048 | tf_op jit(solution)/shard_map/ppermute | solution.py:363
  65.1 9.9 %copy-start.4 = (bf16[2,320,256]{2,1,0:T(8,128)(2,1)}, bf16[2,320,256]{2,1,0:T(8,128)(2,1)S(1)}, u32[]{:S(2)}) copy-start(bf16[2,320,256]{2,1,0:T(8,128)(2,1)S(1)} %collective-permute-done.30.rest_1_) | copy-start | bytes 983044
  65.1 22.7 %collective-permute-start.34 = (bf16[2,320,256]{2,1,0:T(8,128)(2,1)S(1)}, bf16[2,320,256]{2,1,0:T(8,128)(2,1)S(1)}, u32[]{:S(2)}, u32[]{:S(2)}) collective-permute-start(bf16[2,320,256]{2,1,0:T(8,128)(2,1)S(1)} %collective-permute-done.30.rest_1_), channel_id=1, source_target_pairs={{0,1},{1,0},{2,3},{3,2},{4,5},{5,4},{6,7},{7,6},{8,9},{9,8},{10,11... | collective-permute-start | bytes 983048 | tf_op jit(solution)/shard_map/ppermute | solution.py:363
  65.6 0.7 copy-start.22
  75.0 25.3 %collective-permute-start.49 = (bf16[512,896]{1,0:T(8,128)(2,1)}, bf16[512,896]{1,0:T(8,128)(2,1)S(1)}, u32[]{:S(2)}, u32[]{:S(2)}) collective-permute-start(bf16[512,896]{1,0:T(8,128)(2,1)} %get-tuple-element.452), channel_id=1, source_target_pairs={{8,0},{16,8},{24,16},{9,1},{17,9},{25,17},{10,2},{18,10},{26,18},{... | collective-permute-start | bytes 2752520 | tf_op jit(solution)/shard_map/ppermute | solution.py:212
  76.3 11.5 %copy-start.5 = (bf16[2,320,256]{2,1,0:T(8,128)(2,1)}, bf16[2,320,256]{2,1,0:T(8,128)(2,1)S(1)}, u32[]{:S(2)}) copy-start(bf16[2,320,256]{2,1,0:T(8,128)(2,1)S(1)} %collective-permute-done.33.rest_4_) | copy-start | bytes 983044
  76.3 25.6 %collective-permute-start.48 = (bf16[512,896]{1,0:T(8,128)(2,1)}, bf16[512,896]{1,0:T(8,128)(2,1)S(1)}, u32[]{:S(2)}, u32[]{:S(2)}) collective-permute-start(bf16[512,896]{1,0:T(8,128)(2,1)} %get-tuple-element.452), channel_id=1, source_target_pairs={{0,8},{8,16},{16,24},{1,9},{9,17},{17,25},{2,10},{10,18},{18,26},{... | collective-permute-start | bytes 2752520 | tf_op jit(solution)/shard_map/ppermute | solution.py:211
  81.0 6.8 %copy-start.6 = (bf16[2,320,256]{2,1,0:T(8,128)(2,1)}, bf16[2,320,256]{2,1,0:T(8,128)(2,1)S(1)}, u32[]{:S(2)}) copy-start(bf16[2,320,256]{2,1,0:T(8,128)(2,1)S(1)} %collective-permute-done.36.rest_7_) | copy-start | bytes 983044
  81.0 39.0 %collective-permute-start.51 = (bf16[512,896]{1,0:T(8,128)(2,1)}, bf16[512,896]{1,0:T(8,128)(2,1)S(1)}, u32[]{:S(2)}, u32[]{:S(2)}) collective-permute-start(bf16[512,896]{1,0:T(8,128)(2,1)} %get-tuple-element.453), channel_id=1, source_target_pairs={{8,0},{16,8},{24,16},{9,1},{17,9},{25,17},{10,2},{18,10},{26,18},{... | collective-permute-start | bytes 2752520 | tf_op jit(solution)/shard_map/ppermute | solution.py:212
  82.3 5.5 %copy-start.7 = (bf16[2,320,256]{2,1,0:T(8,128)(2,1)}, bf16[2,320,256]{2,1,0:T(8,128)(2,1)S(1)}, u32[]{:S(2)}) copy-start(bf16[2,320,256]{2,1,0:T(8,128)(2,1)S(1)} %collective-permute-done.35.rest_6_) | copy-start | bytes 983044
  82.3 39.3 %collective-permute-start.50 = (bf16[512,896]{1,0:T(8,128)(2,1)}, bf16[512,896]{1,0:T(8,128)(2,1)}, u32[]{:S(2)}, u32[]{:S(2)}) collective-permute-start(bf16[512,896]{1,0:T(8,128)(2,1)} %get-tuple-element.453), channel_id=1, source_target_pairs={{0,8},{8,16},{16,24},{1,9},{9,17},{17,25},{2,10},{10,18},{18,26},{... | collective-permute-start | bytes 2752520 | tf_op jit(solution)/shard_map/ppermute | solution.py:211
  87.8 0.7 copy-start.8
  105.4 35.9 %collective-permute-start.52 = (bf16[512,896]{1,0:T(8,128)(2,1)}, bf16[512,896]{1,0:T(8,128)(2,1)}, u32[]{:S(2)}, u32[]{:S(2)}) collective-permute-start(bf16[512,896]{1,0:T(8,128)(2,1)} %get-tuple-element.455), channel_id=1, source_target_pairs={{0,8},{8,16},{16,24},{1,9},{9,17},{17,25},{2,10},{10,18},{18,26},{... | collective-permute-start | bytes 2752520 | tf_op jit(solution)/shard_map/ppermute | solution.py:211
  109.5 31.8 %collective-permute-start.53 = (bf16[512,896]{1,0:T(8,128)(2,1)}, bf16[512,896]{1,0:T(8,128)(2,1)}, u32[]{:S(2)}, u32[]{:S(2)}) collective-permute-start(bf16[512,896]{1,0:T(8,128)(2,1)} %get-tuple-element.456), channel_id=1, source_target_pairs={{8,0},{16,8},{24,16},{9,1},{17,9},{25,17},{10,2},{18,10},{26,18},{... | collective-permute-start | bytes 2752520 | tf_op jit(solution)/shard_map/ppermute | solution.py:212
  125.1 34.6 %collective-permute-start.54 = (bf16[512,896]{1,0:T(8,128)(2,1)}, bf16[512,896]{1,0:T(8,128)(2,1)}, u32[]{:S(2)}, u32[]{:S(2)}) collective-permute-start(bf16[512,896]{1,0:T(8,128)(2,1)} %get-tuple-element.457), channel_id=1, source_target_pairs={{0,8},{8,16},{16,24},{1,9},{9,17},{17,25},{2,10},{10,18},{18,26},{... | collective-permute-start | bytes 2752520 | tf_op jit(solution)/shard_map/ppermute | solution.py:211
  130.0 29.7 %collective-permute-start.55 = (bf16[512,896]{1,0:T(8,128)(2,1)}, bf16[512,896]{1,0:T(8,128)(2,1)}, u32[]{:S(2)}, u32[]{:S(2)}) collective-permute-start(bf16[512,896]{1,0:T(8,128)(2,1)} %get-tuple-element.458), channel_id=1, source_target_pairs={{8,0},{16,8},{24,16},{9,1},{17,9},{25,17},{10,2},{18,10},{26,18},{... | collective-permute-start | bytes 2752520 | tf_op jit(solution)/shard_map/ppermute | solution.py:212
  165.6 24.5 %collective-permute-start = (bf16[512,896]{1,0:T(8,128)(2,1)}, bf16[512,896]{1,0:T(8,128)(2,1)}, u32[]{:S(2)}, u32[]{:S(2)}) collective-permute-start(bf16[512,896]{1,0:T(8,128)(2,1)} %get-tuple-element.351), channel_id=1, source_target_pairs={{0,8},{8,16},{16,24},{1,9},{9,17},{17,25},{2,10},{10,18},{18,26},{... | collective-permute-start | bytes 2752520 | tf_op jit(solution)/shard_map/cond/branch_1_fun/ppermute | solution.py:211
  169.9 25.5 %collective-permute-start.1 = (bf16[512,896]{1,0:T(8,128)(2,1)}, bf16[512,896]{1,0:T(8,128)(2,1)}, u32[]{:S(2)}, u32[]{:S(2)}) collective-permute-start(bf16[512,896]{1,0:T(8,128)(2,1)} %get-tuple-element.352), channel_id=1, source_target_pairs={{8,0},{16,8},{24,16},{9,1},{17,9},{25,17},{10,2},{18,10},{26,18},{... | collective-permute-start | bytes 2752520 | tf_op jit(solution)/shard_map/cond/branch_1_fun/ppermute | solution.py:212
  174.6 33.0 %collective-permute-start.2 = (bf16[512,896]{1,0:T(8,128)(2,1)}, bf16[512,896]{1,0:T(8,128)(2,1)S(1)}, u32[]{:S(2)}, u32[]{:S(2)}) collective-permute-start(bf16[512,896]{1,0:T(8,128)(2,1)} %get-tuple-element.355), channel_id=1, source_target_pairs={{0,8},{8,16},{16,24},{1,9},{9,17},{17,25},{2,10},{10,18},{18,26},{... | collective-permute-start | bytes 2752520 | tf_op jit(solution)/shard_map/cond/branch_1_fun/ppermute | solution.py:211
  179.1 33.5 %collective-permute-start.3 = (bf16[512,896]{1,0:T(8,128)(2,1)}, bf16[512,896]{1,0:T(8,128)(2,1)S(1)}, u32[]{:S(2)}, u32[]{:S(2)}) collective-permute-start(bf16[512,896]{1,0:T(8,128)(2,1)} %get-tuple-element.356), channel_id=1, source_target_pairs={{8,0},{16,8},{24,16},{9,1},{17,9},{25,17},{10,2},{18,10},{26,18},{... | collective-permute-start | bytes 2752520 | tf_op jit(solution)/shard_map/cond/branch_1_fun/ppermute | solution.py:212
  207.6 4.9 %copy-start.10 = (bf16[512,896]{1,0:T(8,128)(2,1)}, bf16[512,896]{1,0:T(8,128)(2,1)S(1)}, u32[]{:S(2)}) copy-start(bf16[512,896]{1,0:T(8,128)(2,1)S(1)} %collective-permute-done.2.rest_0_) | copy-start | bytes 2752516 | tf_op jit(solution)/shard_map/cond
  212.6 0.9 copy-start.11

commit v2 on v1

--- a/solution.py
+++ b/solution.py
@@ -214,7 +214,7 @@
 
 
 def place_kernel(hold, steps, meta, update_ref, *rest):
-    came, (out_ref, sems) = rest[: 2 * steps], rest[2 * steps :]
+    came, (out_ref, sems) = rest[: 2 * steps], rest[-2:]
     chunk = out_ref.shape[1] // CHUNKS
 
     def target(s, j):
@@ -269,19 +269,19 @@
                         copy.wait() if wait else copy.start()
 
 
-def place(meta, came, update):
+def place(meta, came, update, after):
     hold, rows, cols = update.shape
     arrived = [x for pair in came for x in pair]
     return pl.pallas_call(
         functools.partial(place_kernel, hold, len(came)),
         out_shape=jax.ShapeDtypeStruct((CAP, rows, cols), update.dtype),
-        in_specs=[SMEM, ANY] + [ANY] * len(arrived),
+        in_specs=[SMEM, ANY] + [ANY] * (1 + len(arrived)),
         out_specs=VMEM,
         scratch_shapes=[pltpu.SemaphoreType.DMA((CAP, CHUNKS))],
         compiler_params=compiler_params(),
         cost_estimate=pl.CostEstimate(flops=WORK, bytes_accessed=1, transcendentals=0),
         name="place",
-    )(meta, update, *arrived)
+    )(meta, update, *arrived, after)
 
 
 def place_last(meta, out, came, step, hold):
@@ -307,25 +307,25 @@
     outs, scratch = rest[:4], rest[4]
     high = BLOCK // width
     me = meta[1]
-    for j in range(blocks):
-        rows = (j + 1) * BLOCK
-        scratch[j, pl.ds(0, rows), :] = lax.dot_general(
-            x_ref[0, pl.ds(0, rows), :],
-            x_ref[0, pl.ds(j * BLOCK, BLOCK), :],
+    rows = blocks * BLOCK
+    for i in range(blocks):
+        scratch[i, :, pl.ds(i * BLOCK, rows - i * BLOCK)] = lax.dot_general(
+            x_ref[0, pl.ds(i * BLOCK, BLOCK), :],
+            x_ref[0, pl.ds(i * BLOCK, rows - i * BLOCK), :],
             (((1,), (1,)), ((), ())),
             preferred_element_type=jnp.float32,
         ).astype(jnp.bfloat16)
 
     def sort(keep, send):
-        for j in range(blocks):
-            for q in range(width):
-                piece = pieces_of(me, q, width)
-                out = keep if q < width // 2 else send
-                base = q % (width // 2) * (blocks * (blocks + 1) // 2)
+        for q in range(width):
+            piece = pieces_of(me, q, width)
+            out = keep if q < width // 2 else send
+            base = q % (width // 2) * (blocks * (blocks + 1) // 2)
+            for j in range(blocks):
                 for i in range(j + 1):
                     at = base + j * (j + 1) // 2 + i
                     out[0, pl.ds(at * high, high), :] = scratch[
-                        j, pl.ds(pl.multiple_of(i * BLOCK + piece * high, high), high), :
+                        i, pl.ds(pl.multiple_of(piece * high, high), high), pl.ds(j * BLOCK, BLOCK)
                     ]
 
     pl.when(pl.program_id(0) == 0)(lambda: sort(*outs[:2]))
@@ -346,7 +346,7 @@
             grid=(hold,),
             in_specs=[pl.BlockSpec((1, rows, cols), lambda e, meta: (meta[2 + CAP + hold + e], 0, 0))],
             out_specs=[one, one, others, others],
-            scratch_shapes=[pltpu.VMEM((blocks, rows, BLOCK), jnp.bfloat16)],
+            scratch_shapes=[pltpu.VMEM((blocks, BLOCK, rows), jnp.bfloat16)],
         ),
         out_shape=shapes,
         compiler_params=compiler_params(),
@@ -372,6 +372,49 @@
         piece = total[:, r * high : (r + 1) * high].astype(jnp.bfloat16)
         mine = mine + exchange(piece, 2 * r, width).astype(jnp.float32)
     return mine.astype(jnp.bfloat16)
+
+
+def share_kernel(chips, keep, other, _, mine, *pieces):
+    high = mine.shape[1]
+    for r in range(chips):
+        rows = pl.ds(r * high, high)
+        total = keep[:, rows, :].astype(jnp.float32) + other[:, rows, :].astype(jnp.float32)
+        if r == 0:
+            mine[...] = total
+        else:
+            pieces[r - 1][...] = total.astype(jnp.bfloat16)
+
+
+def total_kernel(mine, *rest):
+    came, out = rest[:-2], rest[-1]
+    total = mine[...]
+    for other in came:
+        total = total + other[...].astype(jnp.float32)
+    out[...] = total.astype(jnp.bfloat16)
+
+
+def reduce_scatter_late(keep, send, width, after_share, after_total):
+    chips = width // 2
+    shape = (keep.shape[0], keep.shape[1] // chips, keep.shape[2])
+    half = jax.ShapeDtypeStruct(shape, jnp.bfloat16)
+    mine, *pieces = pl.pallas_call(
+        functools.partial(share_kernel, chips),
+        out_shape=[jax.ShapeDtypeStruct(shape, jnp.float32)] + [half] * (chips - 1),
+        in_specs=[VMEM, VMEM, ANY],
+        out_specs=[VMEM] * chips,
+        compiler_params=compiler_params(),
+        name="share",
+    )(keep, exchange(send, 1, width), after_share)
+    came = [exchange(piece, 2 * r, width) for r, piece in enumerate(pieces, 1)]
+    return pl.pallas_call(
+        total_kernel,
+        out_shape=half,
+        in_specs=[VMEM] * chips + [ANY],
+        out_specs=VMEM,
+        compiler_params=compiler_params(),
+        cost_estimate=pl.CostEstimate(flops=0, bytes_accessed=1, transcendentals=0),
+        name="total",
+    )(mine, *came, after_total)
 
 
 def all_gather(x, width):
@@ -414,24 +457,28 @@
     @pl.when(live == 1)
     def _():
         unpack(blocks, width, meta[1], pieces, gram_ref)
-        first_ref[...] = jnp.dot(gram_ref[...], x_ref[0], preferred_element_type=jnp.float32).astype(jnp.bfloat16)
-
-    for j in range(CHUNKS):
-        span = pl.ds(j * chunk, chunk)
-
-        @pl.when(live == 1)
-        def _():
-            second = jnp.dot(gram_ref[span, :], first_ref[...], preferred_element_type=jnp.float32)
-            x, first = x_ref[0, span, :].astype(jnp.float32), first_ref[span, :].astype(jnp.float32)
-            mixed = 3.4445 * x - 4.775 * first + 2.0315 * second
-            second_ref[span, :] = (SCALE * mixed).astype(jnp.bfloat16)
-
-        @pl.when(live == 0)
-        def _():
-            second_ref[span, :] = jnp.zeros((chunk, second_ref.shape[1]), jnp.bfloat16)
-
-        for copy in copies(j):
-            copy.start()
+        for at in range(0, rows, BLOCK):
+            span = pl.ds(at, BLOCK)
+            first_ref[span, :] = jnp.dot(
+                gram_ref[span, :], x_ref[0], preferred_element_type=jnp.float32
+            ).astype(jnp.bfloat16)
+        for j in range(CHUNKS):
+            for at in range(j * chunk, (j + 1) * chunk, BLOCK):
+                span = pl.ds(at, BLOCK)
+                second = jnp.dot(gram_ref[span, :], first_ref[...], preferred_element_type=jnp.float32)
+                x, first = x_ref[0, span, :].astype(jnp.float32), first_ref[span, :].astype(jnp.float32)
+                mixed = 3.4445 * x - 4.775 * first + 2.0315 * second
+                second_ref[span, :] = (SCALE * mixed).astype(jnp.bfloat16)
+            for copy in copies(j):
+                copy.start()
+
+    @pl.when(live == 0)
+    def _():
+        second_ref[...] = jnp.zeros_like(second_ref)
+        for j in range(CHUNKS):
+            for copy in copies(j):
+                copy.start()
+
     for j in range(CHUNKS):
         for copy in copies(j):
             copy.wait()
@@ -465,18 +512,18 @@
         input_output_aliases={2 + width: 0} if before else {},
         compiler_params=compiler_params(),
         cost_estimate=pl.CostEstimate(
-            flops=4 * rows * rows * cols, bytes_accessed=6 * rows * cols, transcendentals=0
+            flops=0 if before else 4 * rows * rows * cols, bytes_accessed=1, transcendentals=0
         ),
         name="update",
     )(meta, momentum, *pieces, *before)
 
 
-def stream(meta, snd, update, came, out, extra, n):
+def stream(meta, snd, update, came, out, sent, extra, n):
     hold, rows, cols = update.shape
     chunks = update.reshape(-1, rows // CHUNKS, cols)
     came = list(came)
     for step in range(STEPS, STEPS + extra):
-        came.append(hop(*pick(chunks, snd, came, step), n))
+        came.append(hop(*(sent if step == STEPS else pick(chunks, snd, came, step)), n))
     for step in range(STEPS, STEPS + extra):
         out = place_last(meta, out, came[step], step, hold)
     return out[None]
@@ -523,7 +570,7 @@
                         copy.wait()
 
 
-def endless(meta, snd, update, came, out, n):
+def endless(meta, snd, update, came, out, _, n):
     hold, rows, cols = update.shape
     chunks = update.reshape(-1, rows // CHUNKS, cols)
     chunk = jax.ShapeDtypeStruct(chunks.shape[1:], update.dtype)
@@ -563,8 +610,9 @@
     where = jnp.stack([lax.axis_index("group"), lax.axis_index("width")]).astype(jnp.int32)
     snd, meta = make_plan(assignment, where, n, hold)
     keep, send, keeps, sends = partial_gram(meta, momentum, width)
-    update, *done = one_update(meta, all_gather(reduce_scatter(keep, send, width), width), momentum, 0)
-    pieces = all_gather(reduce_scatter(keeps, sends, width), width)
+    pieces = all_gather(reduce_scatter(keep, send, width), width)
+    update, *done = one_update(meta, pieces, momentum, 0)
+    pieces = all_gather(reduce_scatter_late(keeps, sends, width, pieces[1], done[0]), width)
     for place_in_order in range(1, hold):
         (update,) = one_update(meta, pieces, momentum, place_in_order, update)
     chunks = update.reshape(-1, rows // CHUNKS, cols)
@@ -572,11 +620,12 @@
     for step in range(STEPS):
         sent = (done[step], done[step]) if step < DELAY else pick(chunks, snd, came, step)
         came.append(hop(*sent, n))
-    out = place(meta, came[:-1], update)
+    sent = pick(chunks, snd, came, STEPS)
+    out = place(meta, came[:-1], update, sent[0])
     out = place_last(meta, out, came[-1], STEPS - 1, hold)
     ways = [functools.partial(lambda extra, *args: stream(*args, extra, n), extra) for extra in EXTRA]
     ways.append(lambda *args: endless(*args, n))
-    return update, lax.switch(meta[0], ways, meta, snd, update, came, out)
+    return update, lax.switch(meta[0], ways, meta, snd, update, came, out, sent)
 
 
 def solution(mesh):

time: 217 us -> 209 us (0.963)
  waiting for transfers between devices: 102 us -> 89.2 us
  Pallas kernels: 52.3 us -> 56.7 us
  local copies, waits for them, and re-layouts: 2.49 us -> 4.83 us
    ppermute x6, waiting for transfers between devices: 23.4 us -> 14.4 us  [hop(): lax.ppermute(left, 'group', [(i + 1, i) for i in range(n - 1)])]
    pallas_call x0 -> x2, Pallas kernels: none -> 5.22 us  [the longest x1 2.98 us: reduce_scatter_late(): pl.pallas_call(functools.partial(share_kernel, chips), out_shape=[jax.Sha...]
    ppermute x22, starting transfers between devices: 20.2 us -> 16.1 us  [exchange(): return lax.ppermute(x, 'width', [(i, i ^ other) for i in range(width)])]
    ppermute x6, waiting for transfers between devices: 47.5 us -> 43.7 us  [hop(): lax.ppermute(right, 'group', [(i, i + 1) for i in range(n - 1)])]
    unnamed x34 -> x38, local copies, waits for them, and re-layouts: 1.46 us -> 3.87 us
  transfers between devices with their start and end apart: 34 -> 34, of which waited for: 21 -> 18; matrix products, arithmetic and copies ran while one was open for 1% -> 1% of each run, Pallas kernels for 15% -> 18%
where the time goes in v2:
time: 209 us; the launch traced here: 208 us
  waiting for transfers between devices  89.2 us (43%)
  Pallas kernels  56.7 us (27%)
  starting transfers between devices  53.8 us (26%)
  local copies, waits for them, and re-layouts  4.83 us (2%)
    ppermute x6, waiting for transfers between devices, hop(): lax.ppermute(right, 'group', [(i, i + 1) for i in range(n - 1)])  43.7 us
    ppermute x22, waiting for transfers between devices, exchange(): return lax.ppermute(x, 'width', [(i, i ^ other) for i in range(width)])  31.1 us
    ppermute x6, starting transfers between devices, hop(): lax.ppermute(right, 'group', [(i, i + 1) for i in range(n - 1)])  30 us
    pallas_call x3, Pallas kernels, one_update(): pl.pallas_call(functools.partial(update_kernel, rows // BLOCK, width, hol...  16.3 us
    ppermute x22, starting transfers between devices, exchange(): return lax.ppermute(x, 'width', [(i, i ^ other) for i in range(width)])  16.1 us
    ppermute x6, waiting for transfers between devices, hop(): lax.ppermute(left, 'group', [(i + 1, i) for i in range(n - 1)])  14.4 us
    pallas_call x4, Pallas kernels, pick(): pl.pallas_call(functools.partial(pick_kernel, step, count), out_shape=[ch...  13.1 us
    pallas_call x1, Pallas kernels, partial_gram(): pl.pallas_call(functools.partial(gram_kernel, blocks, width), grid_spec=p...  8.55 us
  transfers between devices with their start and end apart: 34, of which 18 were waited for; matrix products, arithmetic and copies ran while one was open for 1% of the time, Pallas kernels for 18%

profile of v2, /device:TPU:0, one launch (start us, length us, event | category | flops | bytes accessed | tf_op | source)
XLA Modules:
  0.0 207.8 jit_solution(18216932367829447362)
XLA Ops:
  0.6 0.6 pad_add_fusion.where
  1.2 2.7 %plan.1 = (s32[2,20]{1,0:T(2,128)S(1)}, s32[11]{0:T(128)S(1)}) custom-call(s32[12]{0:T(128)} %assign.1, s32[2]{0:T(128)} %pad_add_fusion.where), custom_call_target="tpu_custom_call" | custom-call | tf_op jit(solution)/shard_map/plan/pallas_call | solution.py:160
  3.9 8.5 %gram.1 = (bf16[1,1280,256]{2,1,0:T(8,128)(2,1)}, bf16[1,1280,256]{2,1,0:T(8,128)(2,1)}, bf16[2,1280,256]{2,1,0:T(8,128)(2,1)}, bf16[2,1280,256]{2,1,0:T(8,128)(2,1)}) custom-call(s32[11]{0:T(128)S(1)} %get-tuple-element.663.meta, bf16[3,1024,896]{2,1,0:T(8,128)(2,1)} %x_ref.7), custom_call_target="tpu_custom_call" | custom-call | flops 3523215360 | bytes 9437184 | tf_op jit(solution)/shard_map/gram/pallas_call | solution.py:342
  13.0 1.9 collective-permute-done.27
  14.9 1.3 fusion.4
  16.2 2.9 %collective-permute-start.28 = (bf16[1,320,256]{2,1,0:T(8,128)(2,1)S(1)}, bf16[1,320,256]{2,1,0:T(8,128)(2,1)S(1)}, u32[]{:S(2)}, u32[]{:S(2)}) collective-permute-start(bf16[1,320,256]{2,1,0:T(8,128)(2,1)S(1)} %get-tuple-element.511), channel_id=1, source_target_pairs={{0,2},{1,3},{2,0},{3,1},{4,6},{5,7},{6,4},{7,5},{8,10},{9,11},{10,... | collective-permute-start | bytes 491528 | tf_op jit(solution)/shard_map/ppermute | solution.py:363
  19.1 1.5 collective-permute-start.30
  20.7 3.4 %collective-permute-done.28 = bf16[1,320,256]{2,1,0:T(8,128)(2,1)S(1)} collective-permute-done((bf16[1,320,256]{2,1,0:T(8,128)(2,1)S(1)}, bf16[1,320,256]{2,1,0:T(8,128)(2,1)S(1)}, u32[]{:S(2)}, u32[]{:S(2)}) %collective-permute-start.28) | collective-permute-done | bytes 163872 | tf_op jit(solution)/shard_map/ppermute | solution.py:363
  24.1 4.3 %collective-permute-done.30 = bf16[1,320,256]{2,1,0:T(8,128)(2,1)S(1)} collective-permute-done((bf16[1,320,256]{2,1,0:T(8,128)(2,1)S(1)}, bf16[1,320,256]{2,1,0:T(8,128)(2,1)S(1)}, u32[]{:S(2)}, u32[]{:S(2)}) %collective-permute-start.30) | collective-permute-done | bytes 163872 | tf_op jit(solution)/shard_map/ppermute | solution.py:363
  28.5 1.4 collective-permute-done.29
  29.9 1.5 collective-permute-start.36
  31.4 1.5 collective-permute-start.35
  33.0 0.5 collective-permute-start.31
  33.5 3.3 %collective-permute-done.36.rest_3_ = bf16[1,320,256]{2,1,0:T(8,128)(2,1)S(1)} collective-permute-done((bf16[1,320,256]{2,1,0:T(8,128)(2,1)S(1)}, bf16[1,320,256]{2,1,0:T(8,128)(2,1)S(1)}, u32[]{:S(2)}, u32[]{:S(2)}) %collective-permute-start.36) | collective-permute-done | bytes 163872 | tf_op jit(solution)/shard_map/ppermute | solution.py:363
  36.8 1.6 collective-permute-done.35.rest_2_
  39.1 0.9 copy-done
  40.0 3.0 %share.1 = (f32[2,320,256]{2,1,0:T(8,128)}, bf16[2,320,256]{2,1,0:T(8,128)(2,1)}, bf16[2,320,256]{2,1,0:T(8,128)(2,1)}, bf16[2,320,256]{2,1,0:T(8,128)(2,1)}) custom-call(bf16[2,1280,256]{2,1,0:T(8,128)(2,1)} %get-tuple-element.465.keep, bf16[2,1280,256]{2,1,0:T(8,128)(2,1)} %copy-done, bf16[1,320,256]{2,1,0:T(8,128)(2,1)} %copy-done.12), custom_call_target="tpu_custom_call" | custom-call | tf_op jit(solution)/shard_map/share/pallas_call | solution.py:400
  43.0 1.5 collective-permute-start.32
  45.0 1.5 collective-permute-start.34
  46.5 0.6 copy-done.23
  47.1 0.7 copy-done.24
  47.8 8.6 %update.3 = (bf16[3,1024,896]{2,1,0:T(8,128)(2,1)}, bf16[512,896]{1,0:T(8,128)(2,1)}, bf16[512,896]{1,0:T(8,128)(2,1)}) custom-call(s32[11]{0:T(128)S(1)} %get-tuple-element.663.meta, bf16[3,1024,896]{2,1,0:T(8,128)(2,1)} %x_ref.7, bf16[1,320,256]{2,1,0:T(8,128)(2,1)} %copy-done.11, bf16[1,320,256]{2,1,0:T(8,128)(2,1)} %copy-done.12, ...), custom_call_target="tpu_custom_call" | custom-call | flops 3758096384 | bytes 1 | tf_op jit(solution)/shard_map/update/pallas_call | solution.py:495
  56.4 4.7 %collective-permute-done.33.rest_1_ = bf16[2,320,256]{2,1,0:T(8,128)(2,1)S(1)} collective-permute-done((bf16[2,320,256]{2,1,0:T(8,128)(2,1)}, bf16[2,320,256]{2,1,0:T(8,128)(2,1)S(1)}, u32[]{:S(2)}, u32[]{:S(2)}) %collective-permute-start.33) | collective-permute-done | bytes 327712 | tf_op jit(solution)/shard_map/ppermute | solution.py:363
  61.1 0.7 copy-done.9
  61.9 2.2 %total.1.rest_0_ = bf16[2,320,256]{2,1,0:T(8,128)(2,1)} custom-call(f32[2,320,256]{2,1,0:T(8,128)} %get-tuple-element.469.mine, bf16[2,320,256]{2,1,0:T(8,128)(2,1)} %copy-done.8, bf16[2,320,256]{2,1,0:T(8,128)(2,1)} %copy-done.9, bf16[2,320,256]{2,1,0:T(8,128)(2,1)} %copy-done.10, bf16[512,896]{1,0:T(8,128)(2,1)} %get-tuple-element.473.rest_3_), custom_call_target="tpu_custom_call" | custom-call | bytes 1 | tf_op jit(solution)/shard_map/total/pallas_call | solution.py:409
  64.2 1.4 collective-permute-start.43
  65.6 0.6 collective-permute-start.42
  66.2 1.3 collective-permute-start.49
  67.5 4.6 %collective-permute-start.48 = (bf16[512,896]{1,0:T(8,128)(2,1)}, bf16[512,896]{1,0:T(8,128)(2,1)S(1)}, u32[]{:S(2)}, u32[]{:S(2)}) collective-permute-start(bf16[512,896]{1,0:T(8,128)(2,1)} %get-tuple-element.473.rest_3_), channel_id=1, source_target_pairs={{0,8},{8,16},{16,24},{1,9},{9,17},{17,25},{2,10},{10,18},{18,26},{... | collective-permute-start | bytes 2752520 | tf_op jit(solution)/shard_map/ppermute | solution.py:211
  72.1 1.6 collective-permute-start.41
  73.6 2.0 collective-permute-done.43.rest_3_
  75.6 6.8 %collective-permute-done.42.rest_2_ = bf16[2,320,256]{2,1,0:T(8,128)(2,1)S(1)} collective-permute-done((bf16[2,320,256]{2,1,0:T(8,128)(2,1)}, bf16[2,320,256]{2,1,0:T(8,128)(2,1)S(1)}, u32[]{:S(2)}, u32[]{:S(2)}) %collective-permute-start.42) | collective-permute-done | bytes 327712 | tf_op jit(solution)/shard_map/ppermute | solution.py:363
  82.5 1.3 collective-permute-start.51
  83.8 5.5 %collective-permute-start.50 = (bf16[512,896]{1,0:T(8,128)(2,1)}, bf16[512,896]{1,0:T(8,128)(2,1)}, u32[]{:S(2)}, u32[]{:S(2)}) collective-permute-start(bf16[512,896]{1,0:T(8,128)(2,1)} %get-tuple-element.475), channel_id=1, source_target_pairs={{0,8},{8,16},{16,24},{1,9},{9,17},{17,25},{2,10},{10,18},{18,26},{... | collective-permute-start | bytes 2752520 | tf_op jit(solution)/shard_map/ppermute | solution.py:211
  89.3 1.6 collective-permute-done.45.rest_5_
  91.0 0.7 copy-done.7
  91.6 3.9 %update.4.rest_8_ = bf16[3,1024,896]{2,1,0:T(8,128)(2,1)} custom-call(s32[11]{0:T(128)S(1)} %get-tuple-element.663.meta, bf16[3,1024,896]{2,1,0:T(8,128)(2,1)} %x_ref.7, bf16[2,320,256]{2,1,0:T(8,128)(2,1)} %total.1.rest_0_, bf16[2,320,256]{2,1,0:T(8,128)(2,1)} %copy-done.4, bf16[2,320,256]{2,1,0:T(8,128)(2,1)} %copy-done.3, ...), custom_call_target="tpu_custom_call", output_to_operand_aliasing={{}: (10, {})} | custom-call | bytes 1 | tf_op jit(solution)/shard_map/update/pallas_call | solution.py:495
  95.5 3.9 %update.5.update_ref = bf16[3,1024,896]{2,1,0:T(8,128)(2,1)} custom-call(s32[11]{0:T(128)S(1)} %get-tuple-element.663.meta, bf16[3,1024,896]{2,1,0:T(8,128)(2,1)} %x_ref.7, bf16[2,320,256]{2,1,0:T(8,128)(2,1)} %total.1.rest_0_, bf16[2,320,256]{2,1,0:T(8,128)(2,1)} %copy-done.4, bf16[2,320,256]{2,1,0:T(8,128)(2,1)} %copy-done.3, ...), custom_call_target="tpu_custom_call", output_to_operand_aliasing={{}: (10, {})} | custom-call | bytes 1 | tf_op jit(solution)/shard_map/update/pallas_call | solution.py:495
  99.4 3.3 %pick.21 = (bf16[512,896]{1,0:T(8,128)(2,1)}, bf16[512,896]{1,0:T(8,128)(2,1)}) custom-call(s32[2,20]{1,0:T(2,128)S(1)} %get-tuple-element.665.snd, bf16[6,512,896]{2,1,0:T(8,128)(2,1)} %bitcast.19.own, bf16[512,896]{1,0:T(8,128)(2,1)S(1)} %collective-permute-done.48.rest_0_, bf16[512,896]{1,0:T(8,128)(2,1)S(1)} %collective-permute-done.49.rest_1_), custom_call_target="tpu_custom_call" | custom-call | bytes 1 | tf_op jit(solution)/shard_map/pick/pallas_call | solution.py:196
  102.7 2.3 %collective-permute-start.52 = (bf16[512,896]{1,0:T(8,128)(2,1)}, bf16[512,896]{1,0:T(8,128)(2,1)}, u32[]{:S(2)}, u32[]{:S(2)}) collective-permute-start(bf16[512,896]{1,0:T(8,128)(2,1)} %get-tuple-element.477), channel_id=1, source_target_pairs={{0,8},{8,16},{16,24},{1,9},{9,17},{17,25},{2,10},{10,18},{18,26},{... | collective-permute-start | bytes 2752520 | tf_op jit(solution)/shard_map/ppermute | solution.py:211
  105.0 1.3 collective-permute-start.53
  106.3 4.1 %collective-permute-done.51.rest_3_ = bf16[512,896]{1,0:T(8,128)(2,1)S(1)} collective-permute-done((bf16[512,896]{1,0:T(8,128)(2,1)}, bf16[512,896]{1,0:T(8,128)(2,1)S(1)}, u32[]{:S(2)}, u32[]{:S(2)}) %collective-permute-start.51) | collective-permute-done | bytes 917536 | tf_op jit(solution)/shard_map/ppermute | solution.py:212
  110.4 2.4 %collective-permute-done.50.rest_2_ = bf16[512,896]{1,0:T(8,128)(2,1)} collective-permute-done((bf16[512,896]{1,0:T(8,128)(2,1)}, bf16[512,896]{1,0:T(8,128)(2,1)}, u32[]{:S(2)}, u32[]{:S(2)}) %collective-permute-start.50) | collective-permute-done | bytes 917536 | tf_op jit(solution)/shard_map/ppermute | solution.py:211
  112.7 3.3 %pick.23 = (bf16[512,896]{1,0:T(8,128)(2,1)}, bf16[512,896]{1,0:T(8,128)(2,1)}) custom-call(s32[2,20]{1,0:T(2,128)S(1)} %get-tuple-element.665.snd, bf16[6,512,896]{2,1,0:T(8,128)(2,1)} %bitcast.19.own, bf16[512,896]{1,0:T(8,128)(2,1)S(1)} %collective-permute-done.48.rest_0_, bf16[512,896]{1,0:T(8,128)(2,1)S(1)} %collective-permute-done.49.rest_1_, ...), custom_call_target="tpu_custom_call" | custom-call | bytes 1 | tf_op jit(solution)/shard_map/pick/pallas_call | solution.py:196
  116.0 5.1 %collective-permute-start.54 = (bf16[512,896]{1,0:T(8,128)(2,1)}, bf16[512,896]{1,0:T(8,128)(2,1)}, u32[]{:S(2)}, u32[]{:S(2)}) collective-permute-start(bf16[512,896]{1,0:T(8,128)(2,1)} %get-tuple-element.480), channel_id=1, source_target_pairs={{0,8},{8,16},{16,24},{1,9},{9,17},{17,25},{2,10},{10,18},{18,26},{... | collective-permute-start | bytes 2752520 | tf_op jit(solution)/shard_map/ppermute | solution.py:211
  121.1 1.3 collective-permute-start.55
  122.4 10.0 %collective-permute-done.52.rest_4_ = bf16[512,896]{1,0:T(8,128)(2,1)} collective-permute-done((bf16[512,896]{1,0:T(8,128)(2,1)}, bf16[512,896]{1,0:T(8,128)(2,1)}, u32[]{:S(2)}, u32[]{:S(2)}) %collective-permute-start.52) | collective-permute-done | bytes 917536 | tf_op jit(solution)/shard_map/ppermute | solution.py:211
  132.4 3.3 %pick.22 = (bf16[512,896]{1,0:T(8,128)(2,1)}, bf16[512,896]{1,0:T(8,128)(2,1)}) custom-call(s32[2,20]{1,0:T(2,128)S(1)} %get-tuple-element.665.snd, bf16[6,512,896]{2,1,0:T(8,128)(2,1)} %bitcast.19.own, bf16[512,896]{1,0:T(8,128)(2,1)S(1)} %collective-permute-done.48.rest_0_, bf16[512,896]{1,0:T(8,128)(2,1)S(1)} %collective-permute-done.49.rest_1_, ...), custom_call_target="tpu_custom_call" | custom-call | bytes 1 | tf_op jit(solution)/shard_map/pick/pallas_call | solution.py:196
  135.7 3.6 %place.1._ = bf16[2,1024,896]{2,1,0:T(8,128)(2,1)} custom-call(s32[11]{0:T(128)S(1)} %get-tuple-element.663.meta, bf16[3,1024,896]{2,1,0:T(8,128)(2,1)} %update.5.update_ref, bf16[512,896]{1,0:T(8,128)(2,1)S(1)} %collective-permute-done.48.rest_0_, bf16[512,896]{1,0:T(8,128)(2,1)S(1)} %collective-permute-done.49.rest_1_, ...), custom_call_target="tpu_custom_call" | custom-call | flops 5000000000 | bytes 1 | tf_op jit(solution)/shard_map/place/pallas_call | solution.py:275
  139.3 11.4 %collective-permute-done.54.rest_0_ = bf16[512,896]{1,0:T(8,128)(2,1)} collective-permute-done((bf16[512,896]{1,0:T(8,128)(2,1)}, bf16[512,896]{1,0:T(8,128)(2,1)}, u32[]{:S(2)}, u32[]{:S(2)}) %collective-permute-start.54) | collective-permute-done | bytes 917536 | tf_op jit(solution)/shard_map/ppermute | solution.py:211
  150.7 2.4 %last.25 = bf16[2,1024,896]{2,1,0:T(8,128)(2,1)} custom-call(s32[11]{0:T(128)S(1)} %get-tuple-element.663.meta, bf16[2,1024,896]{2,1,0:T(8,128)(2,1)} %place.1._, bf16[512,896]{1,0:T(8,128)(2,1)} %collective-permute-done.54.rest_0_, bf16[512,896]{1,0:T(8,128)(2,1)} %collective-permute-done.55.rest_1_), custom_call_target="tpu_custom_call", output_to_operand_aliasing={{}: (1, {})} | custom-call | flops 5000000000 | bytes 1 | tf_op jit(solution)/shard_map/last/pallas_call | solution.py:288
  153.2 54.5 %conditional.1 = (bf16[1,2,1024,896]{3,2,1,0:T(8,128)(2,1)}) conditional(s32[]{:T(128)} %bitcast.18, bf16[2,1024,896]{2,1,0:T(8,128)(2,1)} %last.25, (bf16[512,896]{1,0:T(8,128)(2,1)}, bf16[512,896]{1,0:T(8,128)(2,1)}, s32[11]{0:T(128)S(1)}, bf16[2,1024,896]{2,1,0:T(8,128)(2,1)}, bf16[3,1024,896]{2,1,0:T(8,128)(2,1)}, ...), branch_computations={%region_0.0_spmd, %region_1.0_spmd, %region_2.0_spmd, %region_3.0_... | conditional | flops 29999998976 | bytes 51380772 | solution.py:628
  153.2 8.0 %collective-permute-start = (bf16[512,896]{1,0:T(8,128)(2,1)}, bf16[512,896]{1,0:T(8,128)(2,1)}, u32[]{:S(2)}, u32[]{:S(2)}) collective-permute-start(bf16[512,896]{1,0:T(8,128)(2,1)} %get-tuple-element.355), channel_id=1, source_target_pairs={{0,8},{8,16},{16,24},{1,9},{9,17},{17,25},{2,10},{10,18},{18,26},{... | collective-permute-start | bytes 2752520 | tf_op jit(solution)/shard_map/cond/branch_1_fun/ppermute | solution.py:211
  161.2 1.3 collective-permute-start.1
  162.5 3.3 %pick.12 = (bf16[512,896]{1,0:T(8,128)(2,1)}, bf16[512,896]{1,0:T(8,128)(2,1)}) custom-call(s32[2,20]{1,0:T(2,128)S(1)} %get-tuple-element.357.snd, bf16[6,512,896]{2,1,0:T(8,128)(2,1)} %bitcast.1.own, bf16[512,896]{1,0:T(8,128)(2,1)S(1)} %get-tuple-element.359.rest_0_, bf16[512,896]{1,0:T(8,128)(2,1)S(1)} %get-tuple-element.360.rest_1_, ...), custom_call_target="tpu_custom_call" | custom-call | bytes 1 | tf_op jit(solution)/shard_map/cond/branch_1_fun/pick/pallas_call | solution.py:196
  165.8 4.6 %collective-permute-start.2 = (bf16[512,896]{1,0:T(8,128)(2,1)}, bf16[512,896]{1,0:T(8,128)(2,1)S(1)}, u32[]{:S(2)}, u32[]{:S(2)}) collective-permute-start(bf16[512,896]{1,0:T(8,128)(2,1)} %get-tuple-element.367), channel_id=1, source_target_pairs={{0,8},{8,16},{16,24},{1,9},{9,17},{17,25},{2,10},{10,18},{18,26},{... | collective-permute-start | bytes 2752520 | tf_op jit(solution)/shard_map/cond/branch_1_fun/ppermute | solution.py:211
  170.4 1.3 collective-permute-start.3
  171.7 9.7 %collective-permute-done.rest_0_ = bf16[512,896]{1,0:T(8,128)(2,1)} collective-permute-done((bf16[512,896]{1,0:T(8,128)(2,1)}, bf16[512,896]{1,0:T(8,128)(2,1)}, u32[]{:S(2)}, u32[]{:S(2)}) %collective-permute-start) | collective-permute-done | bytes 917536 | tf_op jit(solution)/shard_map/cond/branch_1_fun/ppermute | solution.py:211
  181.4 5.3 %collective-permute-done.1.rest_1_ = bf16[512,896]{1,0:T(8,128)(2,1)} collective-permute-done((bf16[512,896]{1,0:T(8,128)(2,1)}, bf16[512,896]{1,0:T(8,128)(2,1)}, u32[]{:S(2)}, u32[]{:S(2)}) %collective-permute-start.1) | collective-permute-done | bytes 917536 | tf_op jit(solution)/shard_map/cond/branch_1_fun/ppermute | solution.py:212
  186.7 2.4 %last.13._ = bf16[2,1024,896]{2,1,0:T(8,128)(2,1)} custom-call(s32[11]{0:T(128)S(1)} %get-tuple-element.353.meta, bf16[2,1024,896]{2,1,0:T(8,128)(2,1)} %get-tuple-element.354._, bf16[512,896]{1,0:T(8,128)(2,1)} %collective-permute-done.rest_0_, bf16[512,896]{1,0:T(8,128)(2,1)} %collective-permute-done.1.rest_1_), custom_call_target="tpu_custom_call", output_to_operand_aliasing={{}: (1, {})} | custom-call | flops 5000000000 | bytes 1 | tf_op jit(solution)/shard_map/cond/branch_1_fun/last/pallas_call | solution.py:288
  189.1 10.2 %collective-permute-done.2.rest_0_ = bf16[512,896]{1,0:T(8,128)(2,1)S(1)} collective-permute-done((bf16[512,896]{1,0:T(8,128)(2,1)}, bf16[512,896]{1,0:T(8,128)(2,1)S(1)}, u32[]{:S(2)}, u32[]{:S(2)}) %collective-permute-start.2) | collective-permute-done | bytes 917536 | tf_op jit(solution)/shard_map/cond/branch_1_fun/ppermute | solution.py:211
  199.4 4.9 %collective-permute-done.3.rest_1_ = bf16[512,896]{1,0:T(8,128)(2,1)S(1)} collective-permute-done((bf16[512,896]{1,0:T(8,128)(2,1)}, bf16[512,896]{1,0:T(8,128)(2,1)S(1)}, u32[]{:S(2)}, u32[]{:S(2)}) %collective-permute-start.3) | collective-permute-done | bytes 917536 | tf_op jit(solution)/shard_map/cond/branch_1_fun/ppermute | solution.py:212
  204.3 0.9 copy-done.18
  205.2 2.4 %last.14 = bf16[2,1024,896]{2,1,0:T(8,128)(2,1)} custom-call(s32[11]{0:T(128)S(1)} %get-tuple-element.353.meta, bf16[2,1024,896]{2,1,0:T(8,128)(2,1)} %last.13._, bf16[512,896]{1,0:T(8,128)(2,1)} %copy-done.17, bf16[512,896]{1,0:T(8,128)(2,1)} %copy-done.18), custom_call_target="tpu_custom_call", output_to_operand_aliasing={{}: (1, {})} | custom-call | flops 5000000000 | bytes 1 | tf_op jit(solution)/shard_map/cond/branch_1_fun/last/pallas_call | solution.py:288
  (66 shorter events, 2.1 us)
Async XLA Ops:
  12.5 2.4 %collective-permute-start.27 = (bf16[1,1280,256]{2,1,0:T(8,128)(2,1)}, bf16[1,1280,256]{2,1,0:T(8,128)(2,1)S(1)}, u32[]{:S(2)}, u32[]{:S(2)}) collective-permute-start(bf16[1,1280,256]{2,1,0:T(8,128)(2,1)} %get-tuple-element.468), channel_id=1, source_target_pairs={{0,1},{1,0},{2,3},{3,2},{4,5},{5,4},{6,7},{7,6},{8,9},{9,8},{10,11... | collective-permute-start | bytes 1966088 | tf_op jit(solution)/shard_map/ppermute | solution.py:363
  13.0 26.0 %collective-permute-start.26 = (bf16[2,1280,256]{2,1,0:T(8,128)(2,1)}, bf16[2,1280,256]{2,1,0:T(8,128)(2,1)S(1)}, u32[]{:S(2)}, u32[]{:S(2)}) collective-permute-start(bf16[2,1280,256]{2,1,0:T(8,128)(2,1)} %get-tuple-element.466), channel_id=1, source_target_pairs={{0,1},{1,0},{2,3},{3,2},{4,5},{5,4},{6,7},{7,6},{8,9},{9,8},{10,11... | collective-permute-start | bytes 3932168 | tf_op jit(solution)/shard_map/ppermute | solution.py:363
  16.2 7.9 %collective-permute-start.28 = (bf16[1,320,256]{2,1,0:T(8,128)(2,1)S(1)}, bf16[1,320,256]{2,1,0:T(8,128)(2,1)S(1)}, u32[]{:S(2)}, u32[]{:S(2)}) collective-permute-start(bf16[1,320,256]{2,1,0:T(8,128)(2,1)S(1)} %get-tuple-element.511), channel_id=1, source_target_pairs={{0,2},{1,3},{2,0},{3,1},{4,6},{5,7},{6,4},{7,5},{8,10},{9,11},{10,... | collective-permute-start | bytes 491528 | tf_op jit(solution)/shard_map/ppermute | solution.py:363
  19.1 9.3 %collective-permute-start.30 = (bf16[1,320,256]{2,1,0:T(8,128)(2,1)S(1)}, bf16[1,320,256]{2,1,0:T(8,128)(2,1)S(1)}, u32[]{:S(2)}, u32[]{:S(2)}) collective-permute-start(bf16[1,320,256]{2,1,0:T(8,128)(2,1)S(1)} %get-tuple-element.512), channel_id=1, source_target_pairs={{0,6},{1,7},{2,4},{3,5},{4,2},{5,3},{6,0},{7,1},{8,14},{9,15},{10,... | collective-permute-start | bytes 491528 | tf_op jit(solution)/shard_map/ppermute | solution.py:363
  20.6 9.2 %collective-permute-start.29 = (bf16[1,320,256]{2,1,0:T(8,128)(2,1)S(1)}, bf16[1,320,256]{2,1,0:T(8,128)(2,1)S(1)}, u32[]{:S(2)}, u32[]{:S(2)}) collective-permute-start(bf16[1,320,256]{2,1,0:T(8,128)(2,1)S(1)} %get-tuple-element.513), channel_id=1, source_target_pairs={{0,4},{1,5},{2,6},{3,7},{4,0},{5,1},{6,2},{7,3},{8,12},{9,13},{10,... | collective-permute-start | bytes 491528 | tf_op jit(solution)/shard_map/ppermute | solution.py:363
  29.9 16.6 %copy-start.11 = (bf16[1,320,256]{2,1,0:T(8,128)(2,1)}, bf16[1,320,256]{2,1,0:T(8,128)(2,1)S(1)}, u32[]{:S(2)}) copy-start(bf16[1,320,256]{2,1,0:T(8,128)(2,1)S(1)} %fusion.3.rest_0_) | copy-start | bytes 491524
  29.9 6.8 %collective-permute-start.36 = (bf16[1,320,256]{2,1,0:T(8,128)(2,1)S(1)}, bf16[1,320,256]{2,1,0:T(8,128)(2,1)S(1)}, u32[]{:S(2)}, u32[]{:S(2)}) collective-permute-start(bf16[1,320,256]{2,1,0:T(8,128)(2,1)S(1)} %fusion.3.rest_0_), channel_id=1, source_target_pairs={{0,6},{1,7},{2,4},{3,5},{4,2},{5,3},{6,0},{7,1},{8,14},{9,15},{10,... | collective-permute-start | bytes 491528 | tf_op jit(solution)/shard_map/ppermute | solution.py:363
  31.4 7.0 %collective-permute-start.35 = (bf16[1,320,256]{2,1,0:T(8,128)(2,1)S(1)}, bf16[1,320,256]{2,1,0:T(8,128)(2,1)S(1)}, u32[]{:S(2)}, u32[]{:S(2)}) collective-permute-start(bf16[1,320,256]{2,1,0:T(8,128)(2,1)S(1)} %fusion.3.rest_0_), channel_id=1, source_target_pairs={{0,4},{1,5},{2,6},{3,7},{4,0},{5,1},{6,2},{7,3},{8,12},{9,13},{10,... | collective-permute-start | bytes 491528 | tf_op jit(solution)/shard_map/ppermute | solution.py:363
  33.0 5.5 %collective-permute-start.31 = (bf16[1,320,256]{2,1,0:T(8,128)(2,1)S(1)}, bf16[1,320,256]{2,1,0:T(8,128)(2,1)S(1)}, u32[]{:S(2)}, u32[]{:S(2)}) collective-permute-start(bf16[1,320,256]{2,1,0:T(8,128)(2,1)S(1)} %fusion.3.rest_0_), channel_id=1, source_target_pairs={{0,2},{1,3},{2,0},{3,1},{4,6},{5,7},{6,4},{7,5},{8,10},{9,11},{10,... | collective-permute-start | bytes 491528 | tf_op jit(solution)/shard_map/ppermute | solution.py:363
  33.5 11.0 %collective-permute-start.37 = (bf16[1,320,256]{2,1,0:T(8,128)(2,1)S(1)}, bf16[1,320,256]{2,1,0:T(8,128)(2,1)S(1)}, u32[]{:S(2)}, u32[]{:S(2)}) collective-permute-start(bf16[1,320,256]{2,1,0:T(8,128)(2,1)S(1)} %fusion.3.rest_0_), channel_id=1, source_target_pairs={{0,1},{1,0},{2,3},{3,2},{4,5},{5,4},{6,7},{7,6},{8,9},{9,8},{10,11... | collective-permute-start | bytes 491528 | tf_op jit(solution)/shard_map/ppermute | solution.py:363
  36.8 9.7 %copy-start.19 = (bf16[1,320,256]{2,1,0:T(8,128)(2,1)}, bf16[1,320,256]{2,1,0:T(8,128)(2,1)S(1)}, u32[]{:S(2)}) copy-start(bf16[1,320,256]{2,1,0:T(8,128)(2,1)S(1)} %collective-permute-done.36.rest_3_) | copy-start | bytes 491524
  36.8 8.2 %collective-permute-start.40 = (bf16[1,320,256]{2,1,0:T(8,128)(2,1)S(1)}, bf16[1,320,256]{2,1,0:T(8,128)(2,1)S(1)}, u32[]{:S(2)}, u32[]{:S(2)}) collective-permute-start(bf16[1,320,256]{2,1,0:T(8,128)(2,1)S(1)} %collective-permute-done.36.rest_3_), channel_id=1, source_target_pairs={{0,1},{1,0},{2,3},{3,2},{4,5},{5,4},{6,7},{7,6},{8,9},{9,8},{10,11... | collective-permute-start | bytes 491528 | tf_op jit(solution)/shard_map/ppermute | solution.py:363
  38.4 8.1 %copy-start.20 = (bf16[1,320,256]{2,1,0:T(8,128)(2,1)}, bf16[1,320,256]{2,1,0:T(8,128)(2,1)S(1)}, u32[]{:S(2)}) copy-start(bf16[1,320,256]{2,1,0:T(8,128)(2,1)S(1)} %collective-permute-done.35.rest_2_) | copy-start | bytes 491524
  38.4 8.1 %collective-permute-start.39 = (bf16[1,320,256]{2,1,0:T(8,128)(2,1)S(1)}, bf16[1,320,256]{2,1,0:T(8,128)(2,1)S(1)}, u32[]{:S(2)}, u32[]{:S(2)}) collective-permute-start(bf16[1,320,256]{2,1,0:T(8,128)(2,1)S(1)} %collective-permute-done.35.rest_2_), channel_id=1, source_target_pairs={{0,1},{1,0},{2,3},{3,2},{4,5},{5,4},{6,7},{7,6},{8,9},{9,8},{10,11... | collective-permute-start | bytes 491528 | tf_op jit(solution)/shard_map/ppermute | solution.py:363
  38.4 0.7 copy-start.12
  38.4 8.0 %collective-permute-start.38 = (bf16[1,320,256]{2,1,0:T(8,128)(2,1)S(1)}, bf16[1,320,256]{2,1,0:T(8,128)(2,1)S(1)}, u32[]{:S(2)}, u32[]{:S(2)}) collective-permute-start(bf16[1,320,256]{2,1,0:T(8,128)(2,1)S(1)} %collective-permute-done.31._.rest_1_), channel_id=1, source_target_pairs={{0,1},{1,0},{2,3},{3,2},{4,5},{5,4},{6,7},{7,6},{8,9},{9,8},{10,11... | collective-permute-start | bytes 491528 | tf_op jit(solution)/shard_map/ppermute | solution.py:363
  38.9 1.1 copy-start
  43.0 13.4 %collective-permute-start.32 = (bf16[2,320,256]{2,1,0:T(8,128)(2,1)}, bf16[2,320,256]{2,1,0:T(8,128)(2,1)S(1)}, u32[]{:S(2)}, u32[]{:S(2)}) collective-permute-start(bf16[2,320,256]{2,1,0:T(8,128)(2,1)} %get-tuple-element.470), channel_id=1, source_target_pairs={{0,2},{1,3},{2,0},{3,1},{4,6},{5,7},{6,4},{7,5},{8,10},{9,11},{10,... | collective-permute-start | bytes 983048 | tf_op jit(solution)/shard_map/ppermute | solution.py:363
  44.5 2.0 copy-start.21
  44.5 16.6 %collective-permute-start.33 = (bf16[2,320,256]{2,1,0:T(8,128)(2,1)}, bf16[2,320,256]{2,1,0:T(8,128)(2,1)S(1)}, u32[]{:S(2)}, u32[]{:S(2)}) collective-permute-start(bf16[2,320,256]{2,1,0:T(8,128)(2,1)} %get-tuple-element.471), channel_id=1, source_target_pairs={{0,4},{1,5},{2,6},{3,7},{4,0},{5,1},{6,2},{7,3},{8,12},{9,13},{10,... | collective-permute-start | bytes 983048 | tf_op jit(solution)/shard_map/ppermute | solution.py:363
  45.0 1.5 copy-start.22
  45.0 16.1 %collective-permute-start.34 = (bf16[2,320,256]{2,1,0:T(8,128)(2,1)}, bf16[2,320,256]{2,1,0:T(8,128)(2,1)S(1)}, u32[]{:S(2)}, u32[]{:S(2)}) collective-permute-start(bf16[2,320,256]{2,1,0:T(8,128)(2,1)} %get-tuple-element.472), channel_id=1, source_target_pairs={{0,6},{1,7},{2,4},{3,5},{4,2},{5,3},{6,0},{7,1},{8,14},{9,15},{10,... | collective-permute-start | bytes 983048 | tf_op jit(solution)/shard_map/ppermute | solution.py:363
  46.5 0.7 copy-start.23
  47.1 0.7 copy-start.24
  56.4 4.7 %copy-start.8 = (bf16[2,320,256]{2,1,0:T(8,128)(2,1)}, bf16[2,320,256]{2,1,0:T(8,128)(2,1)S(1)}, u32[]{:S(2)}) copy-start(bf16[2,320,256]{2,1,0:T(8,128)(2,1)S(1)} %collective-permute-done.32.rest_0_) | copy-start | bytes 983044
  61.1 0.7 copy-start.9
  61.1 0.8 copy-start.10
  64.2 7.9 %collective-permute-start.44 = (bf16[2,320,256]{2,1,0:T(8,128)(2,1)}, bf16[2,320,256]{2,1,0:T(8,128)(2,1)S(1)}, u32[]{:S(2)}, u32[]{:S(2)}) collective-permute-start(bf16[2,320,256]{2,1,0:T(8,128)(2,1)} %total.1.rest_0_), channel_id=1, source_target_pairs={{0,1},{1,0},{2,3},{3,2},{4,5},{5,4},{6,7},{7,6},{8,9},{9,8},{10,11... | collective-permute-start | bytes 983048 | tf_op jit(solution)/shard_map/ppermute | solution.py:363
  64.2 11.5 %collective-permute-start.43 = (bf16[2,320,256]{2,1,0:T(8,128)(2,1)}, bf16[2,320,256]{2,1,0:T(8,128)(2,1)S(1)}, u32[]{:S(2)}, u32[]{:S(2)}) collective-permute-start(bf16[2,320,256]{2,1,0:T(8,128)(2,1)} %total.1.rest_0_), channel_id=1, source_target_pairs={{0,6},{1,7},{2,4},{3,5},{4,2},{5,3},{6,0},{7,1},{8,14},{9,15},{10,... | collective-permute-start | bytes 983048 | tf_op jit(solution)/shard_map/ppermute | solution.py:363
  65.6 16.9 %collective-permute-start.42 = (bf16[2,320,256]{2,1,0:T(8,128)(2,1)}, bf16[2,320,256]{2,1,0:T(8,128)(2,1)S(1)}, u32[]{:S(2)}, u32[]{:S(2)}) collective-permute-start(bf16[2,320,256]{2,1,0:T(8,128)(2,1)} %total.1.rest_0_), channel_id=1, source_target_pairs={{0,4},{1,5},{2,6},{3,7},{4,0},{5,1},{6,2},{7,3},{8,12},{9,13},{10,... | collective-permute-start | bytes 983048 | tf_op jit(solution)/shard_map/ppermute | solution.py:363
  66.2 33.2 %collective-permute-start.49 = (bf16[512,896]{1,0:T(8,128)(2,1)}, bf16[512,896]{1,0:T(8,128)(2,1)S(1)}, u32[]{:S(2)}, u32[]{:S(2)}) collective-permute-start(bf16[512,896]{1,0:T(8,128)(2,1)} %get-tuple-element.473.rest_3_), channel_id=1, source_target_pairs={{8,0},{16,8},{24,16},{9,1},{17,9},{25,17},{10,2},{18,10},{26,18},{... | collective-permute-start | bytes 2752520 | tf_op jit(solution)/shard_map/ppermute | solution.py:212
  67.5 32.0 %collective-permute-start.48 = (bf16[512,896]{1,0:T(8,128)(2,1)}, bf16[512,896]{1,0:T(8,128)(2,1)S(1)}, u32[]{:S(2)}, u32[]{:S(2)}) collective-permute-start(bf16[512,896]{1,0:T(8,128)(2,1)} %get-tuple-element.473.rest_3_), channel_id=1, source_target_pairs={{0,8},{8,16},{16,24},{1,9},{9,17},{17,25},{2,10},{10,18},{18,26},{... | collective-permute-start | bytes 2752520 | tf_op jit(solution)/shard_map/ppermute | solution.py:211
  72.1 18.8 %copy-start.1 = (bf16[2,320,256]{2,1,0:T(8,128)(2,1)}, bf16[2,320,256]{2,1,0:T(8,128)(2,1)S(1)}, u32[]{:S(2)}) copy-start(bf16[2,320,256]{2,1,0:T(8,128)(2,1)S(1)} %collective-permute-done.44.rest_4_) | copy-start | bytes 983044
  72.1 10.4 %collective-permute-start.41 = (bf16[2,320,256]{2,1,0:T(8,128)(2,1)}, bf16[2,320,256]{2,1,0:T(8,128)(2,1)S(1)}, u32[]{:S(2)}, u32[]{:S(2)}) collective-permute-start(bf16[2,320,256]{2,1,0:T(8,128)(2,1)} %total.1.rest_0_), channel_id=1, source_target_pairs={{0,2},{1,3},{2,0},{3,1},{4,6},{5,7},{6,4},{7,5},{8,10},{9,11},{10,... | collective-permute-start | bytes 983048 | tf_op jit(solution)/shard_map/ppermute | solution.py:363
  75.6 15.3 %copy-start.2 = (bf16[2,320,256]{2,1,0:T(8,128)(2,1)}, bf16[2,320,256]{2,1,0:T(8,128)(2,1)S(1)}, u32[]{:S(2)}) copy-start(bf16[2,320,256]{2,1,0:T(8,128)(2,1)S(1)} %collective-permute-done.43.rest_3_) | copy-start | bytes 983044
  75.6 8.1 %collective-permute-start.47 = (bf16[2,320,256]{2,1,0:T(8,128)(2,1)S(1)}, bf16[2,320,256]{2,1,0:T(8,128)(2,1)S(1)}, u32[]{:S(2)}, u32[]{:S(2)}) collective-permute-start(bf16[2,320,256]{2,1,0:T(8,128)(2,1)S(1)} %collective-permute-done.43.rest_3_), channel_id=1, source_target_pairs={{0,1},{1,0},{2,3},{3,2},{4,5},{5,4},{6,7},{7,6},{8,9},{9,8},{10,11... | collective-permute-start | bytes 983048 | tf_op jit(solution)/shard_map/ppermute | solution.py:363
  82.4 8.5 %copy-start.3 = (bf16[2,320,256]{2,1,0:T(8,128)(2,1)}, bf16[2,320,256]{2,1,0:T(8,128)(2,1)S(1)}, u32[]{:S(2)}) copy-start(bf16[2,320,256]{2,1,0:T(8,128)(2,1)S(1)} %collective-permute-done.42.rest_2_) | copy-start | bytes 983044
  82.4 6.9 %collective-permute-start.46 = (bf16[2,320,256]{2,1,0:T(8,128)(2,1)S(1)}, bf16[2,320,256]{2,1,0:T(8,128)(2,1)S(1)}, u32[]{:S(2)}, u32[]{:S(2)}) collective-permute-start(bf16[2,320,256]{2,1,0:T(8,128)(2,1)S(1)} %collective-permute-done.42.rest_2_), channel_id=1, source_target_pairs={{0,1},{1,0},{2,3},{3,2},{4,5},{5,4},{6,7},{7,6},{8,9},{9,8},{10,11... | collective-permute-start | bytes 983048 | tf_op jit(solution)/shard_map/ppermute | solution.py:363
  82.5 8.5 %copy-start.4 = (bf16[2,320,256]{2,1,0:T(8,128)(2,1)}, bf16[2,320,256]{2,1,0:T(8,128)(2,1)S(1)}, u32[]{:S(2)}) copy-start(bf16[2,320,256]{2,1,0:T(8,128)(2,1)S(1)} %collective-permute-done.41.rest_1_) | copy-start | bytes 983044
  82.5 27.9 %collective-permute-start.51 = (bf16[512,896]{1,0:T(8,128)(2,1)}, bf16[512,896]{1,0:T(8,128)(2,1)S(1)}, u32[]{:S(2)}, u32[]{:S(2)}) collective-permute-start(bf16[512,896]{1,0:T(8,128)(2,1)} %get-tuple-element.475), channel_id=1, source_target_pairs={{8,0},{16,8},{24,16},{9,1},{17,9},{25,17},{10,2},{18,10},{26,18},{... | collective-permute-start | bytes 2752520 | tf_op jit(solution)/shard_map/ppermute | solution.py:212
  83.8 7.2 %copy-start.5 = (bf16[2,320,256]{2,1,0:T(8,128)(2,1)}, bf16[2,320,256]{2,1,0:T(8,128)(2,1)S(1)}, u32[]{:S(2)}) copy-start(bf16[2,320,256]{2,1,0:T(8,128)(2,1)S(1)} %collective-permute-done.47.rest_7_) | copy-start | bytes 983044
  83.8 29.0 %collective-permute-start.50 = (bf16[512,896]{1,0:T(8,128)(2,1)}, bf16[512,896]{1,0:T(8,128)(2,1)}, u32[]{:S(2)}, u32[]{:S(2)}) collective-permute-start(bf16[512,896]{1,0:T(8,128)(2,1)} %get-tuple-element.475), channel_id=1, source_target_pairs={{0,8},{8,16},{16,24},{1,9},{9,17},{17,25},{2,10},{10,18},{18,26},{... | collective-permute-start | bytes 2752520 | tf_op jit(solution)/shard_map/ppermute | solution.py:211
  89.3 1.7 copy-start.6
  89.3 1.6 collective-permute-start.45
  90.9 0.7 copy-start.7
  102.7 29.7 %collective-permute-start.52 = (bf16[512,896]{1,0:T(8,128)(2,1)}, bf16[512,896]{1,0:T(8,128)(2,1)}, u32[]{:S(2)}, u32[]{:S(2)}) collective-permute-start(bf16[512,896]{1,0:T(8,128)(2,1)} %get-tuple-element.477), channel_id=1, source_target_pairs={{0,8},{8,16},{16,24},{1,9},{9,17},{17,25},{2,10},{10,18},{18,26},{... | collective-permute-start | bytes 2752520 | tf_op jit(solution)/shard_map/ppermute | solution.py:211
  105.0 27.4 %collective-permute-start.53 = (bf16[512,896]{1,0:T(8,128)(2,1)}, bf16[512,896]{1,0:T(8,128)(2,1)}, u32[]{:S(2)}, u32[]{:S(2)}) collective-permute-start(bf16[512,896]{1,0:T(8,128)(2,1)} %get-tuple-element.478), channel_id=1, source_target_pairs={{8,0},{16,8},{24,16},{9,1},{17,9},{25,17},{10,2},{18,10},{26,18},{... | collective-permute-start | bytes 2752520 | tf_op jit(solution)/shard_map/ppermute | solution.py:212
  116.0 34.7 %collective-permute-start.54 = (bf16[512,896]{1,0:T(8,128)(2,1)}, bf16[512,896]{1,0:T(8,128)(2,1)}, u32[]{:S(2)}, u32[]{:S(2)}) collective-permute-start(bf16[512,896]{1,0:T(8,128)(2,1)} %get-tuple-element.480), channel_id=1, source_target_pairs={{0,8},{8,16},{16,24},{1,9},{9,17},{17,25},{2,10},{10,18},{18,26},{... | collective-permute-start | bytes 2752520 | tf_op jit(solution)/shard_map/ppermute | solution.py:211
  121.1 29.6 %collective-permute-start.55 = (bf16[512,896]{1,0:T(8,128)(2,1)}, bf16[512,896]{1,0:T(8,128)(2,1)}, u32[]{:S(2)}, u32[]{:S(2)}) collective-permute-start(bf16[512,896]{1,0:T(8,128)(2,1)} %get-tuple-element.481), channel_id=1, source_target_pairs={{8,0},{16,8},{24,16},{9,1},{17,9},{25,17},{10,2},{18,10},{26,18},{... | collective-permute-start | bytes 2752520 | tf_op jit(solution)/shard_map/ppermute | solution.py:212
  153.2 28.2 %collective-permute-start = (bf16[512,896]{1,0:T(8,128)(2,1)}, bf16[512,896]{1,0:T(8,128)(2,1)}, u32[]{:S(2)}, u32[]{:S(2)}) collective-permute-start(bf16[512,896]{1,0:T(8,128)(2,1)} %get-tuple-element.355), channel_id=1, source_target_pairs={{0,8},{8,16},{16,24},{1,9},{9,17},{17,25},{2,10},{10,18},{18,26},{... | collective-permute-start | bytes 2752520 | tf_op jit(solution)/shard_map/cond/branch_1_fun/ppermute | solution.py:211
  161.2 25.5 %collective-permute-start.1 = (bf16[512,896]{1,0:T(8,128)(2,1)}, bf16[512,896]{1,0:T(8,128)(2,1)}, u32[]{:S(2)}, u32[]{:S(2)}) collective-permute-start(bf16[512,896]{1,0:T(8,128)(2,1)} %get-tuple-element.356), channel_id=1, source_target_pairs={{8,0},{16,8},{24,16},{9,1},{17,9},{25,17},{10,2},{18,10},{26,18},{... | collective-permute-start | bytes 2752520 | tf_op jit(solution)/shard_map/cond/branch_1_fun/ppermute | solution.py:212
  165.8 33.6 %collective-permute-start.2 = (bf16[512,896]{1,0:T(8,128)(2,1)}, bf16[512,896]{1,0:T(8,128)(2,1)S(1)}, u32[]{:S(2)}, u32[]{:S(2)}) collective-permute-start(bf16[512,896]{1,0:T(8,128)(2,1)} %get-tuple-element.367), channel_id=1, source_target_pairs={{0,8},{8,16},{16,24},{1,9},{9,17},{17,25},{2,10},{10,18},{18,26},{... | collective-permute-start | bytes 2752520 | tf_op jit(solution)/shard_map/cond/branch_1_fun/ppermute | solution.py:211
  170.4 33.9 %collective-permute-start.3 = (bf16[512,896]{1,0:T(8,128)(2,1)}, bf16[512,896]{1,0:T(8,128)(2,1)S(1)}, u32[]{:S(2)}, u32[]{:S(2)}) collective-permute-start(bf16[512,896]{1,0:T(8,128)(2,1)} %get-tuple-element.368), channel_id=1, source_target_pairs={{8,0},{16,8},{24,16},{9,1},{17,9},{25,17},{10,2},{18,10},{26,18},{... | collective-permute-start | bytes 2752520 | tf_op jit(solution)/shard_map/cond/branch_1_fun/ppermute | solution.py:212
  199.4 4.9 %copy-start.17 = (bf16[512,896]{1,0:T(8,128)(2,1)}, bf16[512,896]{1,0:T(8,128)(2,1)S(1)}, u32[]{:S(2)}) copy-start(bf16[512,896]{1,0:T(8,128)(2,1)S(1)} %collective-permute-done.2.rest_0_) | copy-start | bytes 2752516 | tf_op jit(solution)/shard_map/cond
  204.3 0.9 copy-start.18

commit v3 on v2

--- a/solution.py
+++ b/solution.py
@@ -397,20 +397,26 @@
     chips = width // 2
     shape = (keep.shape[0], keep.shape[1] // chips, keep.shape[2])
     half = jax.ShapeDtypeStruct(shape, jnp.bfloat16)
+
+    def block(shape):
+        return pl.BlockSpec((1,) + shape[1:], lambda e: (e, 0, 0))
+
     mine, *pieces = pl.pallas_call(
         functools.partial(share_kernel, chips),
+        grid=(shape[0],),
         out_shape=[jax.ShapeDtypeStruct(shape, jnp.float32)] + [half] * (chips - 1),
-        in_specs=[VMEM, VMEM, ANY],
-        out_specs=[VMEM] * chips,
+        in_specs=[block(keep.shape), block(keep.shape), ANY],
+        out_specs=[block(shape)] * chips,
         compiler_params=compiler_params(),
         name="share",
     )(keep, exchange(send, 1, width), after_share)
     came = [exchange(piece, 2 * r, width) for r, piece in enumerate(pieces, 1)]
     return pl.pallas_call(
         total_kernel,
+        grid=(shape[0],),
         out_shape=half,
-        in_specs=[VMEM] * chips + [ANY],
-        out_specs=VMEM,
+        in_specs=[block(shape)] * chips + [ANY],
+        out_specs=block(shape),
         compiler_params=compiler_params(),
         cost_estimate=pl.CostEstimate(flops=0, bytes_accessed=1, transcendentals=0),
         name="total",
@@ -518,6 +524,53 @@
     )(meta, momentum, *pieces, *before)
 
 
+def rest_kernel(blocks, width, hold, meta, x_ref, *rest):
+    pieces, (out_ref, gram_ref, first_ref) = rest[:width], rest[-3:]
+    live = meta[2 + CAP + meta[2 + CAP + hold + 1 + pl.program_id(0)]]
+
+    @pl.when(live == 1)
+    def _():
+        unpack(blocks, width, meta[1], pieces, gram_ref)
+        for i in range(blocks):
+            span = pl.ds(i * BLOCK, BLOCK)
+            first_ref[span, :] = jnp.dot(
+                gram_ref[span, :], x_ref[0], preferred_element_type=jnp.float32
+            ).astype(jnp.bfloat16)
+        for i in range(blocks):
+            span = pl.ds(i * BLOCK, BLOCK)
+            second = jnp.dot(gram_ref[span, :], first_ref[...], preferred_element_type=jnp.float32)
+            x, first = x_ref[0, span, :].astype(jnp.float32), first_ref[span, :].astype(jnp.float32)
+            mixed = 3.4445 * x - 4.775 * first + 2.0315 * second
+            out_ref[0, span, :] = (SCALE * mixed).astype(jnp.bfloat16)
+
+    @pl.when(live == 0)
+    def _():
+        out_ref[...] = jnp.zeros_like(out_ref)
+
+
+def other_updates(meta, pieces, momentum, update):
+    hold, rows, cols = momentum.shape
+    width = len(pieces)
+    block = pl.BlockSpec((1, rows, cols), lambda e, meta: (meta[2 + CAP + hold + 1 + e], 0, 0))
+    return pl.pallas_call(
+        functools.partial(rest_kernel, rows // BLOCK, width, hold),
+        grid_spec=pltpu.PrefetchScalarGridSpec(
+            num_scalar_prefetch=1,
+            grid=(hold - 1,),
+            in_specs=[block]
+            + [pl.BlockSpec((1,) + piece.shape[1:], lambda e, meta: (e, 0, 0)) for piece in pieces]
+            + [ANY],
+            out_specs=block,
+            scratch_shapes=[pltpu.VMEM((rows, rows), jnp.bfloat16), pltpu.VMEM((rows, cols), jnp.bfloat16)],
+        ),
+        out_shape=jax.ShapeDtypeStruct(update.shape, update.dtype),
+        input_output_aliases={2 + width: 0},
+        compiler_params=compiler_params(),
+        cost_estimate=pl.CostEstimate(flops=0, bytes_accessed=1, transcendentals=0),
+        name="others",
+    )(meta, momentum, *pieces, update)
+
+
 def stream(meta, snd, update, came, out, sent, extra, n):
     hold, rows, cols = update.shape
     chunks = update.reshape(-1, rows // CHUNKS, cols)
@@ -612,9 +665,8 @@
     keep, send, keeps, sends = partial_gram(meta, momentum, width)
     pieces = all_gather(reduce_scatter(keep, send, width), width)
     update, *done = one_update(meta, pieces, momentum, 0)
-    pieces = all_gather(reduce_scatter_late(keeps, sends, width, pieces[1], done[0]), width)
-    for place_in_order in range(1, hold):
-        (update,) = one_update(meta, pieces, momentum, place_in_order, update)
+    pieces = all_gather(reduce_scatter_late(keeps, sends, width, pieces[width // 2 - 1], done[0]), width)
+    update = other_updates(meta, pieces, momentum, update)
     chunks = update.reshape(-1, rows // CHUNKS, cols)
     came = []
     for step in range(STEPS):

time: 209 us -> 206 us (0.986)
  Pallas kernels: 56.7 us -> 50.3 us
  waiting for transfers between devices: 89.2 us -> 92.1 us
    pallas_call x3 -> x1, Pallas kernels: 16.3 us -> 8.59 us  [one_update(): pl.pallas_call(functools.partial(update_kernel, rows // BLOCK, width, hol...]
    pallas_call x2 -> x3, Pallas kernels: 5.22 us -> 9.72 us  [the longest x1 4.83 us: other_updates(): pl.pallas_call(functools.partial(rest_kernel, rows // BLOCK, width, hold)...]
    pallas_call x3, Pallas kernels: 7.24 us -> 4.59 us  [place_last(): pl.pallas_call(functools.partial(last_kernel, hold, step), out_shape=jax....]
    ppermute x6, waiting for transfers between devices: 14.4 us -> 16.8 us  [hop(): lax.ppermute(left, 'group', [(i + 1, i) for i in range(n - 1)])]
  transfers between devices with their start and end apart: 34 -> 34, of which waited for: 18 -> 18; matrix products, arithmetic and copies ran while one was open for 1% -> 1% of each run, Pallas kernels for 18% -> 16%
where the time goes in v3:
time: 206 us; the launch traced here: 205 us
  waiting for transfers between devices  92.1 us (45%)
  starting transfers between devices  54.9 us (27%)
  Pallas kernels  50.3 us (24%)
  local copies, waits for them, and re-layouts  4.87 us (2%)
    ppermute x6, waiting for transfers between devices, hop(): lax.ppermute(right, 'group', [(i, i + 1) for i in range(n - 1)])  44.1 us
    ppermute x22, waiting for transfers between devices, exchange(): return lax.ppermute(x, 'width', [(i, i ^ other) for i in range(width)])  31.2 us
    ppermute x6, starting transfers between devices, hop(): lax.ppermute(right, 'group', [(i, i + 1) for i in range(n - 1)])  31.1 us
    ppermute x6, waiting for transfers between devices, hop(): lax.ppermute(left, 'group', [(i + 1, i) for i in range(n - 1)])  16.8 us
    ppermute x22, starting transfers between devices, exchange(): return lax.ppermute(x, 'width', [(i, i ^ other) for i in range(width)])  16.1 us
    pallas_call x4, Pallas kernels, pick(): pl.pallas_call(functools.partial(pick_kernel, step, count), out_shape=[ch...  13.1 us
    pallas_call x1, Pallas kernels, one_update(): pl.pallas_call(functools.partial(update_kernel, rows // BLOCK, width, hol...  8.59 us
    pallas_call x1, Pallas kernels, partial_gram(): pl.pallas_call(functools.partial(gram_kernel, blocks, width), grid_spec=p...  8.55 us
  transfers between devices with their start and end apart: 34, of which 18 were waited for; matrix products, arithmetic and copies ran while one was open for 1% of the time, Pallas kernels for 16%

profile of v3, /device:TPU:0, one launch (start us, length us, event | category | flops | bytes accessed | tf_op | source)
XLA Modules:
  0.0 205.4 jit_solution(4499976828645535593)
XLA Ops:
  0.6 0.6 pad_add_fusion.where
  1.2 2.7 %plan.1 = (s32[2,20]{1,0:T(2,128)S(1)}, s32[11]{0:T(128)S(1)}) custom-call(s32[12]{0:T(128)} %assign.1, s32[2]{0:T(128)} %pad_add_fusion.where), custom_call_target="tpu_custom_call" | custom-call | tf_op jit(solution)/shard_map/plan/pallas_call | solution.py:160
  3.9 8.5 %gram.1 = (bf16[1,1280,256]{2,1,0:T(8,128)(2,1)}, bf16[1,1280,256]{2,1,0:T(8,128)(2,1)}, bf16[2,1280,256]{2,1,0:T(8,128)(2,1)}, bf16[2,1280,256]{2,1,0:T(8,128)(2,1)}) custom-call(s32[11]{0:T(128)S(1)} %get-tuple-element.663.meta, bf16[3,1024,896]{2,1,0:T(8,128)(2,1)} %x_ref.5), custom_call_target="tpu_custom_call" | custom-call | flops 3523215360 | bytes 9437184 | tf_op jit(solution)/shard_map/gram/pallas_call | solution.py:342
  13.0 1.9 collective-permute-done.27
  14.9 1.3 fusion.4
  16.2 2.9 %collective-permute-start.28 = (bf16[1,320,256]{2,1,0:T(8,128)(2,1)S(1)}, bf16[1,320,256]{2,1,0:T(8,128)(2,1)S(1)}, u32[]{:S(2)}, u32[]{:S(2)}) collective-permute-start(bf16[1,320,256]{2,1,0:T(8,128)(2,1)S(1)} %get-tuple-element.511), channel_id=1, source_target_pairs={{0,2},{1,3},{2,0},{3,1},{4,6},{5,7},{6,4},{7,5},{8,10},{9,11},{10,... | collective-permute-start | bytes 491528 | tf_op jit(solution)/shard_map/ppermute | solution.py:363
  19.1 1.5 collective-permute-start.30
  20.7 3.4 %collective-permute-done.28 = bf16[1,320,256]{2,1,0:T(8,128)(2,1)S(1)} collective-permute-done((bf16[1,320,256]{2,1,0:T(8,128)(2,1)S(1)}, bf16[1,320,256]{2,1,0:T(8,128)(2,1)S(1)}, u32[]{:S(2)}, u32[]{:S(2)}) %collective-permute-start.28) | collective-permute-done | bytes 163872 | tf_op jit(solution)/shard_map/ppermute | solution.py:363
  24.1 4.3 %collective-permute-done.30 = bf16[1,320,256]{2,1,0:T(8,128)(2,1)S(1)} collective-permute-done((bf16[1,320,256]{2,1,0:T(8,128)(2,1)S(1)}, bf16[1,320,256]{2,1,0:T(8,128)(2,1)S(1)}, u32[]{:S(2)}, u32[]{:S(2)}) %collective-permute-start.30) | collective-permute-done | bytes 163872 | tf_op jit(solution)/shard_map/ppermute | solution.py:363
  28.5 1.4 collective-permute-done.29
  30.3 1.7 collective-permute-start.35
  32.0 1.5 collective-permute-start.31
  33.5 3.4 %collective-permute-done.36.rest_2_ = bf16[1,320,256]{2,1,0:T(8,128)(2,1)S(1)} collective-permute-done((bf16[1,320,256]{2,1,0:T(8,128)(2,1)S(1)}, bf16[1,320,256]{2,1,0:T(8,128)(2,1)S(1)}, u32[]{:S(2)}, u32[]{:S(2)}) %collective-permute-start.36) | collective-permute-done | bytes 163872 | tf_op jit(solution)/shard_map/ppermute | solution.py:363
  37.0 0.5 collective-permute-start.38
  37.4 1.2 collective-permute-done.31._.rest_3_
  38.7 0.6 copy-done.12
  39.8 2.7 %share.1 = (f32[2,320,256]{2,1,0:T(8,128)}, bf16[2,320,256]{2,1,0:T(8,128)(2,1)}, bf16[2,320,256]{2,1,0:T(8,128)(2,1)}, bf16[2,320,256]{2,1,0:T(8,128)(2,1)}) custom-call(bf16[2,1280,256]{2,1,0:T(8,128)(2,1)} %get-tuple-element.465.keep, bf16[2,1280,256]{2,1,0:T(8,128)(2,1)} %copy-done, bf16[1,320,256]{2,1,0:T(8,128)(2,1)} %copy-done.12), custom_call_target="tpu_custom_call" | custom-call | tf_op jit(solution)/shard_map/share/pallas_call | solution.py:404
  42.5 1.5 collective-permute-start.32
  44.0 0.5 collective-permute-start.33
  44.5 1.5 collective-permute-start.34
  46.1 0.6 copy-done.23
  46.7 0.7 copy-done.24
  47.3 8.6 %update.1 = (bf16[3,1024,896]{2,1,0:T(8,128)(2,1)}, bf16[512,896]{1,0:T(8,128)(2,1)}, bf16[512,896]{1,0:T(8,128)(2,1)}) custom-call(s32[11]{0:T(128)S(1)} %get-tuple-element.663.meta, bf16[3,1024,896]{2,1,0:T(8,128)(2,1)} %x_ref.5, bf16[1,320,256]{2,1,0:T(8,128)(2,1)} %copy-done.11, bf16[1,320,256]{2,1,0:T(8,128)(2,1)} %copy-done.20, ...), custom_call_target="tpu_custom_call" | custom-call | flops 3758096384 | bytes 1 | tf_op jit(solution)/shard_map/update/pallas_call | solution.py:501
  56.0 5.1 %collective-permute-done.33.rest_1_ = bf16[2,320,256]{2,1,0:T(8,128)(2,1)S(1)} collective-permute-done((bf16[2,320,256]{2,1,0:T(8,128)(2,1)}, bf16[2,320,256]{2,1,0:T(8,128)(2,1)S(1)}, u32[]{:S(2)}, u32[]{:S(2)}) %collective-permute-start.33) | collective-permute-done | bytes 327712 | tf_op jit(solution)/shard_map/ppermute | solution.py:363
  61.1 0.7 copy-done.2
  61.9 2.2 %total.1.rest_0_ = bf16[2,320,256]{2,1,0:T(8,128)(2,1)} custom-call(f32[2,320,256]{2,1,0:T(8,128)} %get-tuple-element.469.mine, bf16[2,320,256]{2,1,0:T(8,128)(2,1)} %copy-done.1, bf16[2,320,256]{2,1,0:T(8,128)(2,1)} %copy-done.2, bf16[2,320,256]{2,1,0:T(8,128)(2,1)} %copy-done.3, bf16[512,896]{1,0:T(8,128)(2,1)} %get-tuple-element.473.rest_3_), custom_call_target="tpu_custom_call" | custom-call | bytes 1 | tf_op jit(solution)/shard_map/total/pallas_call | solution.py:414
  64.1 1.4 collective-permute-start.43
  65.4 0.6 collective-permute-start.42
  66.0 1.3 collective-permute-start.49
  67.3 4.6 %collective-permute-start.48 = (bf16[512,896]{1,0:T(8,128)(2,1)}, bf16[512,896]{1,0:T(8,128)(2,1)S(1)}, u32[]{:S(2)}, u32[]{:S(2)}) collective-permute-start(bf16[512,896]{1,0:T(8,128)(2,1)} %get-tuple-element.473.rest_3_), channel_id=1, source_target_pairs={{0,8},{8,16},{16,24},{1,9},{9,17},{17,25},{2,10},{10,18},{18,26},{... | collective-permute-start | bytes 2752520 | tf_op jit(solution)/shard_map/ppermute | solution.py:211
  72.0 1.6 collective-permute-start.41
  73.5 2.0 collective-permute-done.43.rest_3_
  75.5 6.8 %collective-permute-done.42.rest_2_ = bf16[2,320,256]{2,1,0:T(8,128)(2,1)S(1)} collective-permute-done((bf16[2,320,256]{2,1,0:T(8,128)(2,1)}, bf16[2,320,256]{2,1,0:T(8,128)(2,1)S(1)}, u32[]{:S(2)}, u32[]{:S(2)}) %collective-permute-start.42) | collective-permute-done | bytes 327712 | tf_op jit(solution)/shard_map/ppermute | solution.py:363
  82.4 1.3 collective-permute-start.51
  83.7 5.5 %collective-permute-start.50 = (bf16[512,896]{1,0:T(8,128)(2,1)}, bf16[512,896]{1,0:T(8,128)(2,1)}, u32[]{:S(2)}, u32[]{:S(2)}) collective-permute-start(bf16[512,896]{1,0:T(8,128)(2,1)} %get-tuple-element.475), channel_id=1, source_target_pairs={{0,8},{8,16},{16,24},{1,9},{9,17},{17,25},{2,10},{10,18},{18,26},{... | collective-permute-start | bytes 2752520 | tf_op jit(solution)/shard_map/ppermute | solution.py:211
  89.2 1.6 collective-permute-done.45.rest_5_
  90.8 0.7 copy-done.10
  91.5 4.8 %others.1.update_ref = bf16[3,1024,896]{2,1,0:T(8,128)(2,1)} custom-call(s32[11]{0:T(128)S(1)} %get-tuple-element.663.meta, bf16[3,1024,896]{2,1,0:T(8,128)(2,1)} %x_ref.5, bf16[2,320,256]{2,1,0:T(8,128)(2,1)} %total.1.rest_0_, bf16[2,320,256]{2,1,0:T(8,128)(2,1)} %copy-done.7, bf16[2,320,256]{2,1,0:T(8,128)(2,1)} %copy-done.6, ...), custom_call_target="tpu_custom_call", output_to_operand_aliasing={{}: (10, {})} | custom-call | bytes 1 | tf_op jit(solution)/shard_map/others/pallas_call | solution.py:555
  96.4 3.3 %pick.21 = (bf16[512,896]{1,0:T(8,128)(2,1)}, bf16[512,896]{1,0:T(8,128)(2,1)}) custom-call(s32[2,20]{1,0:T(2,128)S(1)} %get-tuple-element.665.snd, bf16[6,512,896]{2,1,0:T(8,128)(2,1)} %bitcast.19.own, bf16[512,896]{1,0:T(8,128)(2,1)S(1)} %collective-permute-done.48.rest_0_, bf16[512,896]{1,0:T(8,128)(2,1)S(1)} %collective-permute-done.49.rest_1_), custom_call_target="tpu_custom_call" | custom-call | bytes 1 | tf_op jit(solution)/shard_map/pick/pallas_call | solution.py:196
  99.7 3.6 %collective-permute-start.52 = (bf16[512,896]{1,0:T(8,128)(2,1)}, bf16[512,896]{1,0:T(8,128)(2,1)}, u32[]{:S(2)}, u32[]{:S(2)}) collective-permute-start(bf16[512,896]{1,0:T(8,128)(2,1)} %get-tuple-element.477), channel_id=1, source_target_pairs={{0,8},{8,16},{16,24},{1,9},{9,17},{17,25},{2,10},{10,18},{18,26},{... | collective-permute-start | bytes 2752520 | tf_op jit(solution)/shard_map/ppermute | solution.py:211
  103.2 1.3 collective-permute-start.53
  104.5 6.5 %collective-permute-done.51.rest_3_ = bf16[512,896]{1,0:T(8,128)(2,1)S(1)} collective-permute-done((bf16[512,896]{1,0:T(8,128)(2,1)}, bf16[512,896]{1,0:T(8,128)(2,1)S(1)}, u32[]{:S(2)}, u32[]{:S(2)}) %collective-permute-start.51) | collective-permute-done | bytes 917536 | tf_op jit(solution)/shard_map/ppermute | solution.py:212
  111.0 1.6 collective-permute-done.50.rest_2_
  112.6 3.3 %pick.23 = (bf16[512,896]{1,0:T(8,128)(2,1)}, bf16[512,896]{1,0:T(8,128)(2,1)}) custom-call(s32[2,20]{1,0:T(2,128)S(1)} %get-tuple-element.665.snd, bf16[6,512,896]{2,1,0:T(8,128)(2,1)} %bitcast.19.own, bf16[512,896]{1,0:T(8,128)(2,1)S(1)} %collective-permute-done.48.rest_0_, bf16[512,896]{1,0:T(8,128)(2,1)S(1)} %collective-permute-done.49.rest_1_, ...), custom_call_target="tpu_custom_call" | custom-call | bytes 1 | tf_op jit(solution)/shard_map/pick/pallas_call | solution.py:196
  115.9 5.3 %collective-permute-start.54 = (bf16[512,896]{1,0:T(8,128)(2,1)}, bf16[512,896]{1,0:T(8,128)(2,1)}, u32[]{:S(2)}, u32[]{:S(2)}) collective-permute-start(bf16[512,896]{1,0:T(8,128)(2,1)} %get-tuple-element.480), channel_id=1, source_target_pairs={{0,8},{8,16},{16,24},{1,9},{9,17},{17,25},{2,10},{10,18},{18,26},{... | collective-permute-start | bytes 2752520 | tf_op jit(solution)/shard_map/ppermute | solution.py:211
  121.3 1.3 collective-permute-start.55
  122.6 9.7 %collective-permute-done.52.rest_4_ = bf16[512,896]{1,0:T(8,128)(2,1)} collective-permute-done((bf16[512,896]{1,0:T(8,128)(2,1)}, bf16[512,896]{1,0:T(8,128)(2,1)}, u32[]{:S(2)}, u32[]{:S(2)}) %collective-permute-start.52) | collective-permute-done | bytes 917536 | tf_op jit(solution)/shard_map/ppermute | solution.py:211
  132.3 3.3 %pick.22 = (bf16[512,896]{1,0:T(8,128)(2,1)}, bf16[512,896]{1,0:T(8,128)(2,1)}) custom-call(s32[2,20]{1,0:T(2,128)S(1)} %get-tuple-element.665.snd, bf16[6,512,896]{2,1,0:T(8,128)(2,1)} %bitcast.19.own, bf16[512,896]{1,0:T(8,128)(2,1)S(1)} %collective-permute-done.48.rest_0_, bf16[512,896]{1,0:T(8,128)(2,1)S(1)} %collective-permute-done.49.rest_1_, ...), custom_call_target="tpu_custom_call" | custom-call | bytes 1 | tf_op jit(solution)/shard_map/pick/pallas_call | solution.py:196
  135.6 3.1 %place.1._ = bf16[2,1024,896]{2,1,0:T(8,128)(2,1)} custom-call(s32[11]{0:T(128)S(1)} %get-tuple-element.663.meta, bf16[3,1024,896]{2,1,0:T(8,128)(2,1)} %others.1.update_ref, bf16[512,896]{1,0:T(8,128)(2,1)S(1)} %collective-permute-done.48.rest_0_, bf16[512,896]{1,0:T(8,128)(2,1)S(1)} %collective-permute-done.49.rest_1_, ...), custom_call_target="tpu_custom_call" | custom-call | flops 5000000000 | bytes 1 | tf_op jit(solution)/shard_map/place/pallas_call | solution.py:275
  138.7 12.0 %collective-permute-done.54.rest_0_ = bf16[512,896]{1,0:T(8,128)(2,1)} collective-permute-done((bf16[512,896]{1,0:T(8,128)(2,1)}, bf16[512,896]{1,0:T(8,128)(2,1)}, u32[]{:S(2)}, u32[]{:S(2)}) %collective-permute-start.54) | collective-permute-done | bytes 917536 | tf_op jit(solution)/shard_map/ppermute | solution.py:211
  150.6 1.5 last.25
  152.2 53.1 %conditional.1 = (bf16[1,2,1024,896]{3,2,1,0:T(8,128)(2,1)}) conditional(s32[]{:T(128)} %bitcast.18, bf16[2,1024,896]{2,1,0:T(8,128)(2,1)} %last.25, (bf16[512,896]{1,0:T(8,128)(2,1)}, bf16[512,896]{1,0:T(8,128)(2,1)}, s32[11]{0:T(128)S(1)}, bf16[2,1024,896]{2,1,0:T(8,128)(2,1)}, bf16[3,1024,896]{2,1,0:T(8,128)(2,1)}, ...), branch_computations={%region_0.0_spmd, %region_1.0_spmd, %region_2.0_spmd, %region_3.0_... | conditional | flops 29999998976 | bytes 51380772 | solution.py:680
  152.2 7.5 %collective-permute-start = (bf16[512,896]{1,0:T(8,128)(2,1)}, bf16[512,896]{1,0:T(8,128)(2,1)}, u32[]{:S(2)}, u32[]{:S(2)}) collective-permute-start(bf16[512,896]{1,0:T(8,128)(2,1)} %get-tuple-element.355), channel_id=1, source_target_pairs={{0,8},{8,16},{16,24},{1,9},{9,17},{17,25},{2,10},{10,18},{18,26},{... | collective-permute-start | bytes 2752520 | tf_op jit(solution)/shard_map/cond/branch_1_fun/ppermute | solution.py:211
  159.6 1.3 collective-permute-start.1
  160.9 3.3 %pick.12 = (bf16[512,896]{1,0:T(8,128)(2,1)}, bf16[512,896]{1,0:T(8,128)(2,1)}) custom-call(s32[2,20]{1,0:T(2,128)S(1)} %get-tuple-element.357.snd, bf16[6,512,896]{2,1,0:T(8,128)(2,1)} %bitcast.1.own, bf16[512,896]{1,0:T(8,128)(2,1)S(1)} %get-tuple-element.359.rest_0_, bf16[512,896]{1,0:T(8,128)(2,1)S(1)} %get-tuple-element.360.rest_1_, ...), custom_call_target="tpu_custom_call" | custom-call | bytes 1 | tf_op jit(solution)/shard_map/cond/branch_1_fun/pick/pallas_call | solution.py:196
  164.2 4.6 %collective-permute-start.2 = (bf16[512,896]{1,0:T(8,128)(2,1)}, bf16[512,896]{1,0:T(8,128)(2,1)S(1)}, u32[]{:S(2)}, u32[]{:S(2)}) collective-permute-start(bf16[512,896]{1,0:T(8,128)(2,1)} %get-tuple-element.367), channel_id=1, source_target_pairs={{0,8},{8,16},{16,24},{1,9},{9,17},{17,25},{2,10},{10,18},{18,26},{... | collective-permute-start | bytes 2752520 | tf_op jit(solution)/shard_map/cond/branch_1_fun/ppermute | solution.py:211
  168.8 1.3 collective-permute-start.3
  170.1 9.7 %collective-permute-done.rest_0_ = bf16[512,896]{1,0:T(8,128)(2,1)} collective-permute-done((bf16[512,896]{1,0:T(8,128)(2,1)}, bf16[512,896]{1,0:T(8,128)(2,1)}, u32[]{:S(2)}, u32[]{:S(2)}) %collective-permute-start) | collective-permute-done | bytes 917536 | tf_op jit(solution)/shard_map/cond/branch_1_fun/ppermute | solution.py:211
  179.8 5.3 %collective-permute-done.1.rest_1_ = bf16[512,896]{1,0:T(8,128)(2,1)} collective-permute-done((bf16[512,896]{1,0:T(8,128)(2,1)}, bf16[512,896]{1,0:T(8,128)(2,1)}, u32[]{:S(2)}, u32[]{:S(2)}) %collective-permute-start.1) | collective-permute-done | bytes 917536 | tf_op jit(solution)/shard_map/cond/branch_1_fun/ppermute | solution.py:212
  185.1 1.5 last.13._
  186.7 11.2 %collective-permute-done.2.rest_0_ = bf16[512,896]{1,0:T(8,128)(2,1)S(1)} collective-permute-done((bf16[512,896]{1,0:T(8,128)(2,1)}, bf16[512,896]{1,0:T(8,128)(2,1)S(1)}, u32[]{:S(2)}, u32[]{:S(2)}) %collective-permute-start.2) | collective-permute-done | bytes 917536 | tf_op jit(solution)/shard_map/cond/branch_1_fun/ppermute | solution.py:211
  197.8 4.9 %collective-permute-done.3.rest_1_ = bf16[512,896]{1,0:T(8,128)(2,1)S(1)} collective-permute-done((bf16[512,896]{1,0:T(8,128)(2,1)}, bf16[512,896]{1,0:T(8,128)(2,1)S(1)}, u32[]{:S(2)}, u32[]{:S(2)}) %collective-permute-start.3) | collective-permute-done | bytes 917536 | tf_op jit(solution)/shard_map/cond/branch_1_fun/ppermute | solution.py:212
  202.8 0.9 copy-done.18
  203.7 1.5 last.14
  (65 shorter events, 1.8 us)
Async XLA Ops:
  12.5 2.4 %collective-permute-start.27 = (bf16[1,1280,256]{2,1,0:T(8,128)(2,1)}, bf16[1,1280,256]{2,1,0:T(8,128)(2,1)S(1)}, u32[]{:S(2)}, u32[]{:S(2)}) collective-permute-start(bf16[1,1280,256]{2,1,0:T(8,128)(2,1)} %get-tuple-element.468), channel_id=1, source_target_pairs={{0,1},{1,0},{2,3},{3,2},{4,5},{5,4},{6,7},{7,6},{8,9},{9,8},{10,11... | collective-permute-start | bytes 1966088 | tf_op jit(solution)/shard_map/ppermute | solution.py:363
  13.0 25.7 %collective-permute-start.26 = (bf16[2,1280,256]{2,1,0:T(8,128)(2,1)}, bf16[2,1280,256]{2,1,0:T(8,128)(2,1)S(1)}, u32[]{:S(2)}, u32[]{:S(2)}) collective-permute-start(bf16[2,1280,256]{2,1,0:T(8,128)(2,1)} %get-tuple-element.466), channel_id=1, source_target_pairs={{0,1},{1,0},{2,3},{3,2},{4,5},{5,4},{6,7},{7,6},{8,9},{9,8},{10,11... | collective-permute-start | bytes 3932168 | tf_op jit(solution)/shard_map/ppermute | solution.py:363
  16.2 7.9 %collective-permute-start.28 = (bf16[1,320,256]{2,1,0:T(8,128)(2,1)S(1)}, bf16[1,320,256]{2,1,0:T(8,128)(2,1)S(1)}, u32[]{:S(2)}, u32[]{:S(2)}) collective-permute-start(bf16[1,320,256]{2,1,0:T(8,128)(2,1)S(1)} %get-tuple-element.511), channel_id=1, source_target_pairs={{0,2},{1,3},{2,0},{3,1},{4,6},{5,7},{6,4},{7,5},{8,10},{9,11},{10,... | collective-permute-start | bytes 491528 | tf_op jit(solution)/shard_map/ppermute | solution.py:363
  19.1 9.3 %collective-permute-start.30 = (bf16[1,320,256]{2,1,0:T(8,128)(2,1)S(1)}, bf16[1,320,256]{2,1,0:T(8,128)(2,1)S(1)}, u32[]{:S(2)}, u32[]{:S(2)}) collective-permute-start(bf16[1,320,256]{2,1,0:T(8,128)(2,1)S(1)} %get-tuple-element.512), channel_id=1, source_target_pairs={{0,6},{1,7},{2,4},{3,5},{4,2},{5,3},{6,0},{7,1},{8,14},{9,15},{10,... | collective-permute-start | bytes 491528 | tf_op jit(solution)/shard_map/ppermute | solution.py:363
  20.6 9.2 %collective-permute-start.29 = (bf16[1,320,256]{2,1,0:T(8,128)(2,1)S(1)}, bf16[1,320,256]{2,1,0:T(8,128)(2,1)S(1)}, u32[]{:S(2)}, u32[]{:S(2)}) collective-permute-start(bf16[1,320,256]{2,1,0:T(8,128)(2,1)S(1)} %get-tuple-element.513), channel_id=1, source_target_pairs={{0,4},{1,5},{2,6},{3,7},{4,0},{5,1},{6,2},{7,3},{8,12},{9,13},{10,... | collective-permute-start | bytes 491528 | tf_op jit(solution)/shard_map/ppermute | solution.py:363
  29.9 16.1 %copy-start.11 = (bf16[1,320,256]{2,1,0:T(8,128)(2,1)}, bf16[1,320,256]{2,1,0:T(8,128)(2,1)S(1)}, u32[]{:S(2)}) copy-start(bf16[1,320,256]{2,1,0:T(8,128)(2,1)S(1)} %fusion.3.rest_0_) | copy-start | bytes 491524
  29.9 7.0 %collective-permute-start.36 = (bf16[1,320,256]{2,1,0:T(8,128)(2,1)S(1)}, bf16[1,320,256]{2,1,0:T(8,128)(2,1)S(1)}, u32[]{:S(2)}, u32[]{:S(2)}) collective-permute-start(bf16[1,320,256]{2,1,0:T(8,128)(2,1)S(1)} %fusion.3.rest_0_), channel_id=1, source_target_pairs={{0,4},{1,5},{2,6},{3,7},{4,0},{5,1},{6,2},{7,3},{8,12},{9,13},{10,... | collective-permute-start | bytes 491528 | tf_op jit(solution)/shard_map/ppermute | solution.py:363
  30.3 6.6 %collective-permute-start.35 = (bf16[1,320,256]{2,1,0:T(8,128)(2,1)S(1)}, bf16[1,320,256]{2,1,0:T(8,128)(2,1)S(1)}, u32[]{:S(2)}, u32[]{:S(2)}) collective-permute-start(bf16[1,320,256]{2,1,0:T(8,128)(2,1)S(1)} %fusion.3.rest_0_), channel_id=1, source_target_pairs={{0,2},{1,3},{2,0},{3,1},{4,6},{5,7},{6,4},{7,5},{8,10},{9,11},{10,... | collective-permute-start | bytes 491528 | tf_op jit(solution)/shard_map/ppermute | solution.py:363
  32.0 6.7 %collective-permute-start.31 = (bf16[1,320,256]{2,1,0:T(8,128)(2,1)S(1)}, bf16[1,320,256]{2,1,0:T(8,128)(2,1)S(1)}, u32[]{:S(2)}, u32[]{:S(2)}) collective-permute-start(bf16[1,320,256]{2,1,0:T(8,128)(2,1)S(1)} %fusion.3.rest_0_), channel_id=1, source_target_pairs={{0,6},{1,7},{2,4},{3,5},{4,2},{5,3},{6,0},{7,1},{8,14},{9,15},{10,... | collective-permute-start | bytes 491528 | tf_op jit(solution)/shard_map/ppermute | solution.py:363
  33.5 10.5 %collective-permute-start.37 = (bf16[1,320,256]{2,1,0:T(8,128)(2,1)S(1)}, bf16[1,320,256]{2,1,0:T(8,128)(2,1)S(1)}, u32[]{:S(2)}, u32[]{:S(2)}) collective-permute-start(bf16[1,320,256]{2,1,0:T(8,128)(2,1)S(1)} %fusion.3.rest_0_), channel_id=1, source_target_pairs={{0,1},{1,0},{2,3},{3,2},{4,5},{5,4},{6,7},{7,6},{8,9},{9,8},{10,11... | collective-permute-start | bytes 491528 | tf_op jit(solution)/shard_map/ppermute | solution.py:363
  36.9 9.1 %copy-start.19 = (bf16[1,320,256]{2,1,0:T(8,128)(2,1)}, bf16[1,320,256]{2,1,0:T(8,128)(2,1)S(1)}, u32[]{:S(2)}) copy-start(bf16[1,320,256]{2,1,0:T(8,128)(2,1)S(1)} %collective-permute-done.36.rest_2_) | copy-start | bytes 491524
  36.9 7.6 %collective-permute-start.39 = (bf16[1,320,256]{2,1,0:T(8,128)(2,1)S(1)}, bf16[1,320,256]{2,1,0:T(8,128)(2,1)S(1)}, u32[]{:S(2)}, u32[]{:S(2)}) collective-permute-start(bf16[1,320,256]{2,1,0:T(8,128)(2,1)S(1)} %collective-permute-done.36.rest_2_), channel_id=1, source_target_pairs={{0,1},{1,0},{2,3},{3,2},{4,5},{5,4},{6,7},{7,6},{8,9},{9,8},{10,11... | collective-permute-start | bytes 491528 | tf_op jit(solution)/shard_map/ppermute | solution.py:363
  36.9 9.1 %copy-start.20 = (bf16[1,320,256]{2,1,0:T(8,128)(2,1)}, bf16[1,320,256]{2,1,0:T(8,128)(2,1)S(1)}, u32[]{:S(2)}) copy-start(bf16[1,320,256]{2,1,0:T(8,128)(2,1)S(1)} %collective-permute-done.35.rest_1_) | copy-start | bytes 491524
  37.0 9.1 %collective-permute-start.38 = (bf16[1,320,256]{2,1,0:T(8,128)(2,1)S(1)}, bf16[1,320,256]{2,1,0:T(8,128)(2,1)S(1)}, u32[]{:S(2)}, u32[]{:S(2)}) collective-permute-start(bf16[1,320,256]{2,1,0:T(8,128)(2,1)S(1)} %collective-permute-done.35.rest_1_), channel_id=1, source_target_pairs={{0,1},{1,0},{2,3},{3,2},{4,5},{5,4},{6,7},{7,6},{8,9},{9,8},{10,11... | collective-permute-start | bytes 491528 | tf_op jit(solution)/shard_map/ppermute | solution.py:363
  38.7 0.6 copy-start.12
  38.7 7.3 %collective-permute-start.40 = (bf16[1,320,256]{2,1,0:T(8,128)(2,1)S(1)}, bf16[1,320,256]{2,1,0:T(8,128)(2,1)S(1)}, u32[]{:S(2)}, u32[]{:S(2)}) collective-permute-start(bf16[1,320,256]{2,1,0:T(8,128)(2,1)S(1)} %collective-permute-done.31._.rest_3_), channel_id=1, source_target_pairs={{0,1},{1,0},{2,3},{3,2},{4,5},{5,4},{6,7},{7,6},{8,9},{9,8},{10,11... | collective-permute-start | bytes 491528 | tf_op jit(solution)/shard_map/ppermute | solution.py:363
  38.7 1.1 copy-start
  42.5 13.4 %collective-permute-start.32 = (bf16[2,320,256]{2,1,0:T(8,128)(2,1)}, bf16[2,320,256]{2,1,0:T(8,128)(2,1)S(1)}, u32[]{:S(2)}, u32[]{:S(2)}) collective-permute-start(bf16[2,320,256]{2,1,0:T(8,128)(2,1)} %get-tuple-element.470), channel_id=1, source_target_pairs={{0,2},{1,3},{2,0},{3,1},{4,6},{5,7},{6,4},{7,5},{8,10},{9,11},{10,... | collective-permute-start | bytes 983048 | tf_op jit(solution)/shard_map/ppermute | solution.py:363
  44.0 2.0 copy-start.21
  44.0 17.0 %collective-permute-start.33 = (bf16[2,320,256]{2,1,0:T(8,128)(2,1)}, bf16[2,320,256]{2,1,0:T(8,128)(2,1)S(1)}, u32[]{:S(2)}, u32[]{:S(2)}) collective-permute-start(bf16[2,320,256]{2,1,0:T(8,128)(2,1)} %get-tuple-element.471), channel_id=1, source_target_pairs={{0,4},{1,5},{2,6},{3,7},{4,0},{5,1},{6,2},{7,3},{8,12},{9,13},{10,... | collective-permute-start | bytes 983048 | tf_op jit(solution)/shard_map/ppermute | solution.py:363
  44.5 1.5 copy-start.22
  44.5 16.5 %collective-permute-start.34 = (bf16[2,320,256]{2,1,0:T(8,128)(2,1)}, bf16[2,320,256]{2,1,0:T(8,128)(2,1)S(1)}, u32[]{:S(2)}, u32[]{:S(2)}) collective-permute-start(bf16[2,320,256]{2,1,0:T(8,128)(2,1)} %get-tuple-element.472), channel_id=1, source_target_pairs={{0,6},{1,7},{2,4},{3,5},{4,2},{5,3},{6,0},{7,1},{8,14},{9,15},{10,... | collective-permute-start | bytes 983048 | tf_op jit(solution)/shard_map/ppermute | solution.py:363
  46.0 0.7 copy-start.23
  46.7 0.7 copy-start.24
  55.9 5.1 %copy-start.1 = (bf16[2,320,256]{2,1,0:T(8,128)(2,1)}, bf16[2,320,256]{2,1,0:T(8,128)(2,1)S(1)}, u32[]{:S(2)}) copy-start(bf16[2,320,256]{2,1,0:T(8,128)(2,1)S(1)} %collective-permute-done.32.rest_0_) | copy-start | bytes 983044
  61.0 0.7 copy-start.2
  61.0 0.8 copy-start.3
  64.0 7.9 %collective-permute-start.44 = (bf16[2,320,256]{2,1,0:T(8,128)(2,1)}, bf16[2,320,256]{2,1,0:T(8,128)(2,1)S(1)}, u32[]{:S(2)}, u32[]{:S(2)}) collective-permute-start(bf16[2,320,256]{2,1,0:T(8,128)(2,1)} %total.1.rest_0_), channel_id=1, source_target_pairs={{0,1},{1,0},{2,3},{3,2},{4,5},{5,4},{6,7},{7,6},{8,9},{9,8},{10,11... | collective-permute-start | bytes 983048 | tf_op jit(solution)/shard_map/ppermute | solution.py:363
  64.1 11.5 %collective-permute-start.43 = (bf16[2,320,256]{2,1,0:T(8,128)(2,1)}, bf16[2,320,256]{2,1,0:T(8,128)(2,1)S(1)}, u32[]{:S(2)}, u32[]{:S(2)}) collective-permute-start(bf16[2,320,256]{2,1,0:T(8,128)(2,1)} %total.1.rest_0_), channel_id=1, source_target_pairs={{0,6},{1,7},{2,4},{3,5},{4,2},{5,3},{6,0},{7,1},{8,14},{9,15},{10,... | collective-permute-start | bytes 983048 | tf_op jit(solution)/shard_map/ppermute | solution.py:363
  65.4 16.9 %collective-permute-start.42 = (bf16[2,320,256]{2,1,0:T(8,128)(2,1)}, bf16[2,320,256]{2,1,0:T(8,128)(2,1)S(1)}, u32[]{:S(2)}, u32[]{:S(2)}) collective-permute-start(bf16[2,320,256]{2,1,0:T(8,128)(2,1)} %total.1.rest_0_), channel_id=1, source_target_pairs={{0,4},{1,5},{2,6},{3,7},{4,0},{5,1},{6,2},{7,3},{8,12},{9,13},{10,... | collective-permute-start | bytes 983048 | tf_op jit(solution)/shard_map/ppermute | solution.py:363
  66.0 30.3 %collective-permute-start.49 = (bf16[512,896]{1,0:T(8,128)(2,1)}, bf16[512,896]{1,0:T(8,128)(2,1)S(1)}, u32[]{:S(2)}, u32[]{:S(2)}) collective-permute-start(bf16[512,896]{1,0:T(8,128)(2,1)} %get-tuple-element.473.rest_3_), channel_id=1, source_target_pairs={{8,0},{16,8},{24,16},{9,1},{17,9},{25,17},{10,2},{18,10},{26,18},{... | collective-permute-start | bytes 2752520 | tf_op jit(solution)/shard_map/ppermute | solution.py:212
  67.3 29.0 %collective-permute-start.48 = (bf16[512,896]{1,0:T(8,128)(2,1)}, bf16[512,896]{1,0:T(8,128)(2,1)S(1)}, u32[]{:S(2)}, u32[]{:S(2)}) collective-permute-start(bf16[512,896]{1,0:T(8,128)(2,1)} %get-tuple-element.473.rest_3_), channel_id=1, source_target_pairs={{0,8},{8,16},{16,24},{1,9},{9,17},{17,25},{2,10},{10,18},{18,26},{... | collective-permute-start | bytes 2752520 | tf_op jit(solution)/shard_map/ppermute | solution.py:211
  72.0 18.8 %copy-start.4 = (bf16[2,320,256]{2,1,0:T(8,128)(2,1)}, bf16[2,320,256]{2,1,0:T(8,128)(2,1)S(1)}, u32[]{:S(2)}) copy-start(bf16[2,320,256]{2,1,0:T(8,128)(2,1)S(1)} %collective-permute-done.44.rest_4_) | copy-start | bytes 983044
  72.0 10.4 %collective-permute-start.41 = (bf16[2,320,256]{2,1,0:T(8,128)(2,1)}, bf16[2,320,256]{2,1,0:T(8,128)(2,1)S(1)}, u32[]{:S(2)}, u32[]{:S(2)}) collective-permute-start(bf16[2,320,256]{2,1,0:T(8,128)(2,1)} %total.1.rest_0_), channel_id=1, source_target_pairs={{0,2},{1,3},{2,0},{3,1},{4,6},{5,7},{6,4},{7,5},{8,10},{9,11},{10,... | collective-permute-start | bytes 983048 | tf_op jit(solution)/shard_map/ppermute | solution.py:363
  75.5 15.3 %copy-start.5 = (bf16[2,320,256]{2,1,0:T(8,128)(2,1)}, bf16[2,320,256]{2,1,0:T(8,128)(2,1)S(1)}, u32[]{:S(2)}) copy-start(bf16[2,320,256]{2,1,0:T(8,128)(2,1)S(1)} %collective-permute-done.43.rest_3_) | copy-start | bytes 983044
  75.5 8.1 %collective-permute-start.47 = (bf16[2,320,256]{2,1,0:T(8,128)(2,1)S(1)}, bf16[2,320,256]{2,1,0:T(8,128)(2,1)S(1)}, u32[]{:S(2)}, u32[]{:S(2)}) collective-permute-start(bf16[2,320,256]{2,1,0:T(8,128)(2,1)S(1)} %collective-permute-done.43.rest_3_), channel_id=1, source_target_pairs={{0,1},{1,0},{2,3},{3,2},{4,5},{5,4},{6,7},{7,6},{8,9},{9,8},{10,11... | collective-permute-start | bytes 983048 | tf_op jit(solution)/shard_map/ppermute | solution.py:363
  82.3 8.5 %copy-start.6 = (bf16[2,320,256]{2,1,0:T(8,128)(2,1)}, bf16[2,320,256]{2,1,0:T(8,128)(2,1)S(1)}, u32[]{:S(2)}) copy-start(bf16[2,320,256]{2,1,0:T(8,128)(2,1)S(1)} %collective-permute-done.42.rest_2_) | copy-start | bytes 983044
  82.3 6.9 %collective-permute-start.46 = (bf16[2,320,256]{2,1,0:T(8,128)(2,1)S(1)}, bf16[2,320,256]{2,1,0:T(8,128)(2,1)S(1)}, u32[]{:S(2)}, u32[]{:S(2)}) collective-permute-start(bf16[2,320,256]{2,1,0:T(8,128)(2,1)S(1)} %collective-permute-done.42.rest_2_), channel_id=1, source_target_pairs={{0,1},{1,0},{2,3},{3,2},{4,5},{5,4},{6,7},{7,6},{8,9},{9,8},{10,11... | collective-permute-start | bytes 983048 | tf_op jit(solution)/shard_map/ppermute | solution.py:363
  82.4 8.5 %copy-start.7 = (bf16[2,320,256]{2,1,0:T(8,128)(2,1)}, bf16[2,320,256]{2,1,0:T(8,128)(2,1)S(1)}, u32[]{:S(2)}) copy-start(bf16[2,320,256]{2,1,0:T(8,128)(2,1)S(1)} %collective-permute-done.41.rest_1_) | copy-start | bytes 983044
  82.4 28.7 %collective-permute-start.51 = (bf16[512,896]{1,0:T(8,128)(2,1)}, bf16[512,896]{1,0:T(8,128)(2,1)S(1)}, u32[]{:S(2)}, u32[]{:S(2)}) collective-permute-start(bf16[512,896]{1,0:T(8,128)(2,1)} %get-tuple-element.475), channel_id=1, source_target_pairs={{8,0},{16,8},{24,16},{9,1},{17,9},{25,17},{10,2},{18,10},{26,18},{... | collective-permute-start | bytes 2752520 | tf_op jit(solution)/shard_map/ppermute | solution.py:212
  83.7 7.2 %copy-start.8 = (bf16[2,320,256]{2,1,0:T(8,128)(2,1)}, bf16[2,320,256]{2,1,0:T(8,128)(2,1)S(1)}, u32[]{:S(2)}) copy-start(bf16[2,320,256]{2,1,0:T(8,128)(2,1)S(1)} %collective-permute-done.47.rest_7_) | copy-start | bytes 983044
  83.7 29.0 %collective-permute-start.50 = (bf16[512,896]{1,0:T(8,128)(2,1)}, bf16[512,896]{1,0:T(8,128)(2,1)}, u32[]{:S(2)}, u32[]{:S(2)}) collective-permute-start(bf16[512,896]{1,0:T(8,128)(2,1)} %get-tuple-element.475), channel_id=1, source_target_pairs={{0,8},{8,16},{16,24},{1,9},{9,17},{17,25},{2,10},{10,18},{18,26},{... | collective-permute-start | bytes 2752520 | tf_op jit(solution)/shard_map/ppermute | solution.py:211
  89.2 1.7 copy-start.9
  89.2 1.6 collective-permute-start.45
  90.8 0.7 copy-start.10
  99.7 32.6 %collective-permute-start.52 = (bf16[512,896]{1,0:T(8,128)(2,1)}, bf16[512,896]{1,0:T(8,128)(2,1)}, u32[]{:S(2)}, u32[]{:S(2)}) collective-permute-start(bf16[512,896]{1,0:T(8,128)(2,1)} %get-tuple-element.477), channel_id=1, source_target_pairs={{0,8},{8,16},{16,24},{1,9},{9,17},{17,25},{2,10},{10,18},{18,26},{... | collective-permute-start | bytes 2752520 | tf_op jit(solution)/shard_map/ppermute | solution.py:211
  103.2 29.0 %collective-permute-start.53 = (bf16[512,896]{1,0:T(8,128)(2,1)}, bf16[512,896]{1,0:T(8,128)(2,1)}, u32[]{:S(2)}, u32[]{:S(2)}) collective-permute-start(bf16[512,896]{1,0:T(8,128)(2,1)} %get-tuple-element.478), channel_id=1, source_target_pairs={{8,0},{16,8},{24,16},{9,1},{17,9},{25,17},{10,2},{18,10},{26,18},{... | collective-permute-start | bytes 2752520 | tf_op jit(solution)/shard_map/ppermute | solution.py:212
  115.9 34.7 %collective-permute-start.54 = (bf16[512,896]{1,0:T(8,128)(2,1)}, bf16[512,896]{1,0:T(8,128)(2,1)}, u32[]{:S(2)}, u32[]{:S(2)}) collective-permute-start(bf16[512,896]{1,0:T(8,128)(2,1)} %get-tuple-element.480), channel_id=1, source_target_pairs={{0,8},{8,16},{16,24},{1,9},{9,17},{17,25},{2,10},{10,18},{18,26},{... | collective-permute-start | bytes 2752520 | tf_op jit(solution)/shard_map/ppermute | solution.py:211
  121.3 29.4 %collective-permute-start.55 = (bf16[512,896]{1,0:T(8,128)(2,1)}, bf16[512,896]{1,0:T(8,128)(2,1)}, u32[]{:S(2)}, u32[]{:S(2)}) collective-permute-start(bf16[512,896]{1,0:T(8,128)(2,1)} %get-tuple-element.481), channel_id=1, source_target_pairs={{8,0},{16,8},{24,16},{9,1},{17,9},{25,17},{10,2},{18,10},{26,18},{... | collective-permute-start | bytes 2752520 | tf_op jit(solution)/shard_map/ppermute | solution.py:212
  152.2 27.6 %collective-permute-start = (bf16[512,896]{1,0:T(8,128)(2,1)}, bf16[512,896]{1,0:T(8,128)(2,1)}, u32[]{:S(2)}, u32[]{:S(2)}) collective-permute-start(bf16[512,896]{1,0:T(8,128)(2,1)} %get-tuple-element.355), channel_id=1, source_target_pairs={{0,8},{8,16},{16,24},{1,9},{9,17},{17,25},{2,10},{10,18},{18,26},{... | collective-permute-start | bytes 2752520 | tf_op jit(solution)/shard_map/cond/branch_1_fun/ppermute | solution.py:211
  159.6 25.5 %collective-permute-start.1 = (bf16[512,896]{1,0:T(8,128)(2,1)}, bf16[512,896]{1,0:T(8,128)(2,1)}, u32[]{:S(2)}, u32[]{:S(2)}) collective-permute-start(bf16[512,896]{1,0:T(8,128)(2,1)} %get-tuple-element.356), channel_id=1, source_target_pairs={{8,0},{16,8},{24,16},{9,1},{17,9},{25,17},{10,2},{18,10},{26,18},{... | collective-permute-start | bytes 2752520 | tf_op jit(solution)/shard_map/cond/branch_1_fun/ppermute | solution.py:212
  164.2 33.6 %collective-permute-start.2 = (bf16[512,896]{1,0:T(8,128)(2,1)}, bf16[512,896]{1,0:T(8,128)(2,1)S(1)}, u32[]{:S(2)}, u32[]{:S(2)}) collective-permute-start(bf16[512,896]{1,0:T(8,128)(2,1)} %get-tuple-element.367), channel_id=1, source_target_pairs={{0,8},{8,16},{16,24},{1,9},{9,17},{17,25},{2,10},{10,18},{18,26},{... | collective-permute-start | bytes 2752520 | tf_op jit(solution)/shard_map/cond/branch_1_fun/ppermute | solution.py:211
  168.8 33.9 %collective-permute-start.3 = (bf16[512,896]{1,0:T(8,128)(2,1)}, bf16[512,896]{1,0:T(8,128)(2,1)S(1)}, u32[]{:S(2)}, u32[]{:S(2)}) collective-permute-start(bf16[512,896]{1,0:T(8,128)(2,1)} %get-tuple-element.368), channel_id=1, source_target_pairs={{8,0},{16,8},{24,16},{9,1},{17,9},{25,17},{10,2},{18,10},{26,18},{... | collective-permute-start | bytes 2752520 | tf_op jit(solution)/shard_map/cond/branch_1_fun/ppermute | solution.py:212
  197.8 4.9 %copy-start.17 = (bf16[512,896]{1,0:T(8,128)(2,1)}, bf16[512,896]{1,0:T(8,128)(2,1)S(1)}, u32[]{:S(2)}) copy-start(bf16[512,896]{1,0:T(8,128)(2,1)S(1)} %collective-permute-done.2.rest_0_) | copy-start | bytes 2752516 | tf_op jit(solution)/shard_map/cond
  202.8 0.9 copy-start.18

commit v4 on v3

--- a/solution.py
+++ b/solution.py
@@ -453,12 +453,14 @@
     rows = x_ref.shape[1]
     chunk = rows // CHUNKS
 
-    def copies(j):
-        span = pl.ds(j * chunk, chunk)
+    def copies(at):
+        span = pl.ds(at, BLOCK)
         targets = [outs[0].at[chosen, span]]
         if place == 0:
-            targets.append(outs[1 + j])
-        return [pltpu.make_async_copy(second_ref.at[span], to, sems.at[j, i]) for i, to in enumerate(targets)]
+            targets.append(outs[1 + at // chunk].at[pl.ds(at % chunk, BLOCK)])
+        return [
+            pltpu.make_async_copy(second_ref.at[span], to, sems.at[at // BLOCK, i]) for i, to in enumerate(targets)
+        ]
 
     @pl.when(live == 1)
     def _():
@@ -468,25 +470,24 @@
             first_ref[span, :] = jnp.dot(
                 gram_ref[span, :], x_ref[0], preferred_element_type=jnp.float32
             ).astype(jnp.bfloat16)
-        for j in range(CHUNKS):
-            for at in range(j * chunk, (j + 1) * chunk, BLOCK):
-                span = pl.ds(at, BLOCK)
-                second = jnp.dot(gram_ref[span, :], first_ref[...], preferred_element_type=jnp.float32)
-                x, first = x_ref[0, span, :].astype(jnp.float32), first_ref[span, :].astype(jnp.float32)
-                mixed = 3.4445 * x - 4.775 * first + 2.0315 * second
-                second_ref[span, :] = (SCALE * mixed).astype(jnp.bfloat16)
-            for copy in copies(j):
+        for at in range(0, rows, BLOCK):
+            span = pl.ds(at, BLOCK)
+            second = jnp.dot(gram_ref[span, :], first_ref[...], preferred_element_type=jnp.float32)
+            x, first = x_ref[0, span, :].astype(jnp.float32), first_ref[span, :].astype(jnp.float32)
+            mixed = 3.4445 * x - 4.775 * first + 2.0315 * second
+            second_ref[span, :] = (SCALE * mixed).astype(jnp.bfloat16)
+            for copy in copies(at):
                 copy.start()
 
     @pl.when(live == 0)
     def _():
         second_ref[...] = jnp.zeros_like(second_ref)
-        for j in range(CHUNKS):
-            for copy in copies(j):
+        for at in range(0, rows, BLOCK):
+            for copy in copies(at):
                 copy.start()
 
-    for j in range(CHUNKS):
-        for copy in copies(j):
+    for at in range(0, rows, BLOCK):
+        for copy in copies(at):
             copy.wait()
 
 
@@ -511,7 +512,7 @@
                 pltpu.VMEM((rows, rows), jnp.bfloat16),
                 pltpu.VMEM((rows, cols), jnp.bfloat16),
                 pltpu.VMEM((rows, cols), jnp.bfloat16),
-                pltpu.SemaphoreType.DMA((CHUNKS, 2)),
+                pltpu.SemaphoreType.DMA((rows // BLOCK, 2)),
             ],
         ),
         out_shape=out_shape,

time: 206 us -> 156 us (0.76)
  waiting for transfers between devices: 92.1 us -> 56.8 us
  starting transfers between devices: 54.9 us -> 38.9 us
  Pallas kernels: 50.3 us -> 53.8 us
    ppermute x6 -> x4, waiting for transfers between devices: 44.1 us -> 16.8 us  [hop(): lax.ppermute(right, 'group', [(i, i + 1) for i in range(n - 1)])]
    ppermute x6 -> x4, starting transfers between devices: 31.1 us -> 17.7 us  [hop(): lax.ppermute(right, 'group', [(i, i + 1) for i in range(n - 1)])]
    pallas_call x1, Pallas kernels: 4.83 us -> 13.5 us  [other_updates(): pl.pallas_call(functools.partial(rest_kernel, rows // BLOCK, width, hold)...]
    ppermute x6 -> x4, waiting for transfers between devices: 16.8 us -> 8.46 us  [hop(): lax.ppermute(left, 'group', [(i + 1, i) for i in range(n - 1)])]
    pallas_call x4 -> x3, Pallas kernels: 13.1 us -> 9.84 us  [pick(): pl.pallas_call(functools.partial(pick_kernel, step, count), out_shape=[ch...]
    pallas_call x3 -> x1, Pallas kernels: 4.59 us -> 1.53 us  [place_last(): pl.pallas_call(functools.partial(last_kernel, hold, step), out_shape=jax....]
    ppermute x6 -> x4, starting transfers between devices: 7.69 us -> 5.12 us  [hop(): lax.ppermute(left, 'group', [(i + 1, i) for i in range(n - 1)])]
  transfers between devices with their start and end apart: 34 -> 30, of which waited for: 18 -> 15; matrix products, arithmetic and copies ran while one was open for 1% -> 1% of each run, Pallas kernels for 16% -> 25%
where the time goes in v4:
time: 156 us; the launch traced here: 157 us
  waiting for transfers between devices  56.8 us (36%)
  Pallas kernels  53.8 us (34%)
  starting transfers between devices  38.9 us (25%)
  local copies, waits for them, and re-layouts  3.94 us (3%)
  other arithmetic  1.99 us (1%)
    ppermute x22, waiting for transfers between devices, exchange(): return lax.ppermute(x, 'width', [(i, i ^ other) for i in range(width)])  31.5 us
    ppermute x4, starting transfers between devices, hop(): lax.ppermute(right, 'group', [(i, i + 1) for i in range(n - 1)])  17.7 us
    ppermute x4, waiting for transfers between devices, hop(): lax.ppermute(right, 'group', [(i, i + 1) for i in range(n - 1)])  16.8 us
    ppermute x22, starting transfers between devices, exchange(): return lax.ppermute(x, 'width', [(i, i ^ other) for i in range(width)])  16.1 us
    pallas_call x1, Pallas kernels, other_updates(): pl.pallas_call(functools.partial(rest_kernel, rows // BLOCK, width, hold)...  13.5 us
    pallas_call x3, Pallas kernels, pick(): pl.pallas_call(functools.partial(pick_kernel, step, count), out_shape=[ch...  9.84 us
    pallas_call x1, Pallas kernels, partial_gram(): pl.pallas_call(functools.partial(gram_kernel, blocks, width), grid_spec=p...  8.55 us
    ppermute x4, waiting for transfers between devices, hop(): lax.ppermute(left, 'group', [(i + 1, i) for i in range(n - 1)])  8.46 us
  transfers between devices with their start and end apart: 30, of which 15 were waited for; matrix products, arithmetic and copies ran while one was open for 1% of the time, Pallas kernels for 25%

profile of v4, /device:TPU:0, one launch (start us, length us, event | category | flops | bytes accessed | tf_op | source)
XLA Modules:
  0.0 156.5 jit_solution(4196576925785620691)
XLA Ops:
  0.6 0.6 pad_add_fusion.where
  1.2 2.7 %plan.1 = (s32[2,20]{1,0:T(2,128)S(1)}, s32[11]{0:T(128)S(1)}) custom-call(s32[12]{0:T(128)} %assign.1, s32[2]{0:T(128)} %pad_add_fusion.where), custom_call_target="tpu_custom_call" | custom-call | tf_op jit(solution)/shard_map/plan/pallas_call | solution.py:160
  3.9 8.5 %gram.1 = (bf16[1,1280,256]{2,1,0:T(8,128)(2,1)}, bf16[1,1280,256]{2,1,0:T(8,128)(2,1)}, bf16[2,1280,256]{2,1,0:T(8,128)(2,1)}, bf16[2,1280,256]{2,1,0:T(8,128)(2,1)}) custom-call(s32[11]{0:T(128)S(1)} %get-tuple-element.663.meta, bf16[3,1024,896]{2,1,0:T(8,128)(2,1)} %x_ref.5), custom_call_target="tpu_custom_call" | custom-call | flops 3523215360 | bytes 9437184 | tf_op jit(solution)/shard_map/gram/pallas_call | solution.py:342
  12.5 0.5 collective-permute-start.27
  13.0 0.1 collective-permute-start.26
  13.0 1.9 %collective-permute-done.27 = bf16[1,1280,256]{2,1,0:T(8,128)(2,1)S(1)} collective-permute-done((bf16[1,1280,256]{2,1,0:T(8,128)(2,1)}, bf16[1,1280,256]{2,1,0:T(8,128)(2,1)S(1)}, u32[]{:S(2)}, u32[]{:S(2)}) %collective-permute-start.27) | collective-permute-done | bytes 655392 | tf_op jit(solution)/shard_map/ppermute | solution.py:363
  14.9 1.3 fusion.4
  16.2 2.9 %collective-permute-start.28 = (bf16[1,320,256]{2,1,0:T(8,128)(2,1)S(1)}, bf16[1,320,256]{2,1,0:T(8,128)(2,1)S(1)}, u32[]{:S(2)}, u32[]{:S(2)}) collective-permute-start(bf16[1,320,256]{2,1,0:T(8,128)(2,1)S(1)} %get-tuple-element.511), channel_id=1, source_target_pairs={{0,2},{1,3},{2,0},{3,1},{4,6},{5,7},{6,4},{7,5},{8,10},{9,11},{10,... | collective-permute-start | bytes 491528 | tf_op jit(solution)/shard_map/ppermute | solution.py:363
  19.1 1.5 collective-permute-start.30
  20.6 0.1 collective-permute-start.29
  20.7 3.4 %collective-permute-done.28 = bf16[1,320,256]{2,1,0:T(8,128)(2,1)S(1)} collective-permute-done((bf16[1,320,256]{2,1,0:T(8,128)(2,1)S(1)}, bf16[1,320,256]{2,1,0:T(8,128)(2,1)S(1)}, u32[]{:S(2)}, u32[]{:S(2)}) %collective-permute-start.28) | collective-permute-done | bytes 163872 | tf_op jit(solution)/shard_map/ppermute | solution.py:363
  24.1 4.3 %collective-permute-done.30 = bf16[1,320,256]{2,1,0:T(8,128)(2,1)S(1)} collective-permute-done((bf16[1,320,256]{2,1,0:T(8,128)(2,1)S(1)}, bf16[1,320,256]{2,1,0:T(8,128)(2,1)S(1)}, u32[]{:S(2)}, u32[]{:S(2)}) %collective-permute-start.30) | collective-permute-done | bytes 163872 | tf_op jit(solution)/shard_map/ppermute | solution.py:363
  28.5 1.4 collective-permute-done.29
  29.8 0.1 fusion.3.rest_0_
  29.9 0.4 collective-permute-start.36
  30.3 1.7 %collective-permute-start.35 = (bf16[1,320,256]{2,1,0:T(8,128)(2,1)S(1)}, bf16[1,320,256]{2,1,0:T(8,128)(2,1)S(1)}, u32[]{:S(2)}, u32[]{:S(2)}) collective-permute-start(bf16[1,320,256]{2,1,0:T(8,128)(2,1)S(1)} %fusion.3.rest_0_), channel_id=1, source_target_pairs={{0,2},{1,3},{2,0},{3,1},{4,6},{5,7},{6,4},{7,5},{8,10},{9,11},{10,... | collective-permute-start | bytes 491528 | tf_op jit(solution)/shard_map/ppermute | solution.py:363
  32.0 1.5 collective-permute-start.31
  33.5 3.4 %collective-permute-done.36.rest_2_ = bf16[1,320,256]{2,1,0:T(8,128)(2,1)S(1)} collective-permute-done((bf16[1,320,256]{2,1,0:T(8,128)(2,1)S(1)}, bf16[1,320,256]{2,1,0:T(8,128)(2,1)S(1)}, u32[]{:S(2)}, u32[]{:S(2)}) %collective-permute-start.36) | collective-permute-done | bytes 163872 | tf_op jit(solution)/shard_map/ppermute | solution.py:363
  37.0 0.5 collective-permute-start.38
  37.4 1.2 collective-permute-done.31._.rest_3_
  38.7 0.0 copy-start
  38.7 0.6 copy-done.12
  39.3 0.5 copy-done
  39.8 2.7 %share.1 = (f32[2,320,256]{2,1,0:T(8,128)}, bf16[2,320,256]{2,1,0:T(8,128)(2,1)}, bf16[2,320,256]{2,1,0:T(8,128)(2,1)}, bf16[2,320,256]{2,1,0:T(8,128)(2,1)}) custom-call(bf16[2,1280,256]{2,1,0:T(8,128)(2,1)} %get-tuple-element.465.keep, bf16[2,1280,256]{2,1,0:T(8,128)(2,1)} %copy-done, bf16[1,320,256]{2,1,0:T(8,128)(2,1)} %copy-done.12), custom_call_target="tpu_custom_call" | custom-call | tf_op jit(solution)/shard_map/share/pallas_call | solution.py:404
  42.5 1.5 collective-permute-start.32
  44.0 0.0 collective-permute-done.37.rest_4_
  44.0 0.5 collective-permute-start.33
  44.5 1.5 collective-permute-start.34
  46.0 0.0 collective-permute-done.38.rest_5_
  46.0 0.0 collective-permute-done.40.rest_7_
  46.1 0.6 copy-done.23
  46.7 0.7 copy-done.24
  47.3 8.3 %update.1 = (bf16[3,1024,896]{2,1,0:T(8,128)(2,1)}, bf16[512,896]{1,0:T(8,128)(2,1)}, bf16[512,896]{1,0:T(8,128)(2,1)}) custom-call(s32[11]{0:T(128)S(1)} %get-tuple-element.663.meta, bf16[3,1024,896]{2,1,0:T(8,128)(2,1)} %x_ref.5, bf16[1,320,256]{2,1,0:T(8,128)(2,1)} %copy-done.11, bf16[1,320,256]{2,1,0:T(8,128)(2,1)} %copy-done.20, ...), custom_call_target="tpu_custom_call" | custom-call | flops 3758096384 | bytes 1 | tf_op jit(solution)/shard_map/update/pallas_call | solution.py:502
  55.7 5.4 %collective-permute-done.33.rest_1_ = bf16[2,320,256]{2,1,0:T(8,128)(2,1)S(1)} collective-permute-done((bf16[2,320,256]{2,1,0:T(8,128)(2,1)}, bf16[2,320,256]{2,1,0:T(8,128)(2,1)S(1)}, u32[]{:S(2)}, u32[]{:S(2)}) %collective-permute-start.33) | collective-permute-done | bytes 327712 | tf_op jit(solution)/shard_map/ppermute | solution.py:363
  61.1 0.7 copy-done.2
  61.8 0.1 copy-done.3
  61.9 2.2 %total.1.rest_0_ = bf16[2,320,256]{2,1,0:T(8,128)(2,1)} custom-call(f32[2,320,256]{2,1,0:T(8,128)} %get-tuple-element.469.mine, bf16[2,320,256]{2,1,0:T(8,128)(2,1)} %copy-done.1, bf16[2,320,256]{2,1,0:T(8,128)(2,1)} %copy-done.2, bf16[2,320,256]{2,1,0:T(8,128)(2,1)} %copy-done.3, bf16[512,896]{1,0:T(8,128)(2,1)} %get-tuple-element.473.rest_3_), custom_call_target="tpu_custom_call" | custom-call | bytes 1 | tf_op jit(solution)/shard_map/total/pallas_call | solution.py:414
  64.1 1.4 collective-permute-start.43
  65.4 0.6 collective-permute-start.42
  66.0 1.3 collective-permute-start.49
  67.3 4.6 %collective-permute-start.48 = (bf16[512,896]{1,0:T(8,128)(2,1)}, bf16[512,896]{1,0:T(8,128)(2,1)S(1)}, u32[]{:S(2)}, u32[]{:S(2)}) collective-permute-start(bf16[512,896]{1,0:T(8,128)(2,1)} %get-tuple-element.473.rest_3_), channel_id=1, source_target_pairs={{0,8},{8,16},{16,24},{1,9},{9,17},{17,25},{2,10},{10,18},{18,26},{... | collective-permute-start | bytes 2752520 | tf_op jit(solution)/shard_map/ppermute | solution.py:211
  72.0 1.6 collective-permute-start.41
  73.5 2.0 %collective-permute-done.43.rest_3_ = bf16[2,320,256]{2,1,0:T(8,128)(2,1)S(1)} collective-permute-done((bf16[2,320,256]{2,1,0:T(8,128)(2,1)}, bf16[2,320,256]{2,1,0:T(8,128)(2,1)S(1)}, u32[]{:S(2)}, u32[]{:S(2)}) %collective-permute-start.43) | collective-permute-done | bytes 327712 | tf_op jit(solution)/shard_map/ppermute | solution.py:363
  75.5 6.8 %collective-permute-done.42.rest_2_ = bf16[2,320,256]{2,1,0:T(8,128)(2,1)S(1)} collective-permute-done((bf16[2,320,256]{2,1,0:T(8,128)(2,1)}, bf16[2,320,256]{2,1,0:T(8,128)(2,1)S(1)}, u32[]{:S(2)}, u32[]{:S(2)}) %collective-permute-start.42) | collective-permute-done | bytes 327712 | tf_op jit(solution)/shard_map/ppermute | solution.py:363
  82.3 0.0 collective-permute-start.46
  82.4 1.3 collective-permute-start.51
  83.7 5.5 %collective-permute-start.50 = (bf16[512,896]{1,0:T(8,128)(2,1)}, bf16[512,896]{1,0:T(8,128)(2,1)}, u32[]{:S(2)}, u32[]{:S(2)}) collective-permute-start(bf16[512,896]{1,0:T(8,128)(2,1)} %get-tuple-element.475), channel_id=1, source_target_pairs={{0,8},{8,16},{16,24},{1,9},{9,17},{17,25},{2,10},{10,18},{18,26},{... | collective-permute-start | bytes 2752520 | tf_op jit(solution)/shard_map/ppermute | solution.py:211
  89.2 1.6 %collective-permute-done.45.rest_5_ = bf16[2,320,256]{2,1,0:T(8,128)(2,1)S(1)} collective-permute-done((bf16[2,320,256]{2,1,0:T(8,128)(2,1)S(1)}, bf16[2,320,256]{2,1,0:T(8,128)(2,1)S(1)}, u32[]{:S(2)}, u32[]{:S(2)}) %collective-permute-start.45) | collective-permute-done | bytes 327712 | tf_op jit(solution)/shard_map/ppermute | solution.py:363
  90.8 0.7 copy-done.10
  91.5 13.5 %others.1.update_ref = bf16[3,1024,896]{2,1,0:T(8,128)(2,1)} custom-call(s32[11]{0:T(128)S(1)} %get-tuple-element.663.meta, bf16[3,1024,896]{2,1,0:T(8,128)(2,1)} %x_ref.5, bf16[2,320,256]{2,1,0:T(8,128)(2,1)} %total.1.rest_0_, bf16[2,320,256]{2,1,0:T(8,128)(2,1)} %copy-done.7, bf16[2,320,256]{2,1,0:T(8,128)(2,1)} %copy-done.6, ...), custom_call_target="tpu_custom_call", output_to_operand_aliasing={{}: (10, {})} | custom-call | bytes 1 | tf_op jit(solution)/shard_map/others/pallas_call | solution.py:556
  105.0 3.3 %pick.21 = (bf16[512,896]{1,0:T(8,128)(2,1)}, bf16[512,896]{1,0:T(8,128)(2,1)}) custom-call(s32[2,20]{1,0:T(2,128)S(1)} %get-tuple-element.665.snd, bf16[6,512,896]{2,1,0:T(8,128)(2,1)} %bitcast.19.own, bf16[512,896]{1,0:T(8,128)(2,1)S(1)} %collective-permute-done.48.rest_0_, bf16[512,896]{1,0:T(8,128)(2,1)S(1)} %collective-permute-done.49.rest_1_), custom_call_target="tpu_custom_call" | custom-call | bytes 1 | tf_op jit(solution)/shard_map/pick/pallas_call | solution.py:196
  108.3 2.3 %collective-permute-start.52 = (bf16[512,896]{1,0:T(8,128)(2,1)}, bf16[512,896]{1,0:T(8,128)(2,1)}, u32[]{:S(2)}, u32[]{:S(2)}) collective-permute-start(bf16[512,896]{1,0:T(8,128)(2,1)} %get-tuple-element.477), channel_id=1, source_target_pairs={{0,8},{8,16},{16,24},{1,9},{9,17},{17,25},{2,10},{10,18},{18,26},{... | collective-permute-start | bytes 2752520 | tf_op jit(solution)/shard_map/ppermute | solution.py:211
  110.6 1.3 collective-permute-start.53
  111.9 0.2 collective-permute-done.50.rest_2_
  112.1 3.3 %pick.23 = (bf16[512,896]{1,0:T(8,128)(2,1)}, bf16[512,896]{1,0:T(8,128)(2,1)}) custom-call(s32[2,20]{1,0:T(2,128)S(1)} %get-tuple-element.665.snd, bf16[6,512,896]{2,1,0:T(8,128)(2,1)} %bitcast.19.own, bf16[512,896]{1,0:T(8,128)(2,1)S(1)} %collective-permute-done.48.rest_0_, bf16[512,896]{1,0:T(8,128)(2,1)S(1)} %collective-permute-done.49.rest_1_, ...), custom_call_target="tpu_custom_call" | custom-call | bytes 1 | tf_op jit(solution)/shard_map/pick/pallas_call | solution.py:196
  115.4 5.3 %collective-permute-start.54 = (bf16[512,896]{1,0:T(8,128)(2,1)}, bf16[512,896]{1,0:T(8,128)(2,1)}, u32[]{:S(2)}, u32[]{:S(2)}) collective-permute-start(bf16[512,896]{1,0:T(8,128)(2,1)} %get-tuple-element.480), channel_id=1, source_target_pairs={{0,8},{8,16},{16,24},{1,9},{9,17},{17,25},{2,10},{10,18},{18,26},{... | collective-permute-start | bytes 2752520 | tf_op jit(solution)/shard_map/ppermute | solution.py:211
  120.7 1.3 collective-permute-start.55
  122.0 9.7 %collective-permute-done.52.rest_4_ = bf16[512,896]{1,0:T(8,128)(2,1)} collective-permute-done((bf16[512,896]{1,0:T(8,128)(2,1)}, bf16[512,896]{1,0:T(8,128)(2,1)}, u32[]{:S(2)}, u32[]{:S(2)}) %collective-permute-start.52) | collective-permute-done | bytes 917536 | tf_op jit(solution)/shard_map/ppermute | solution.py:211
  131.7 4.2 %collective-permute-done.53.rest_5_ = bf16[512,896]{1,0:T(8,128)(2,1)} collective-permute-done((bf16[512,896]{1,0:T(8,128)(2,1)}, bf16[512,896]{1,0:T(8,128)(2,1)}, u32[]{:S(2)}, u32[]{:S(2)}) %collective-permute-start.53) | collective-permute-done | bytes 917536 | tf_op jit(solution)/shard_map/ppermute | solution.py:212
  136.0 3.3 %pick.22 = (bf16[512,896]{1,0:T(8,128)(2,1)}, bf16[512,896]{1,0:T(8,128)(2,1)}) custom-call(s32[2,20]{1,0:T(2,128)S(1)} %get-tuple-element.665.snd, bf16[6,512,896]{2,1,0:T(8,128)(2,1)} %bitcast.19.own, bf16[512,896]{1,0:T(8,128)(2,1)S(1)} %collective-permute-done.48.rest_0_, bf16[512,896]{1,0:T(8,128)(2,1)S(1)} %collective-permute-done.49.rest_1_, ...), custom_call_target="tpu_custom_call" | custom-call | bytes 1 | tf_op jit(solution)/shard_map/pick/pallas_call | solution.py:196
  139.3 4.4 %place.1._ = bf16[2,1024,896]{2,1,0:T(8,128)(2,1)} custom-call(s32[11]{0:T(128)S(1)} %get-tuple-element.663.meta, bf16[3,1024,896]{2,1,0:T(8,128)(2,1)} %others.1.update_ref, bf16[512,896]{1,0:T(8,128)(2,1)S(1)} %collective-permute-done.48.rest_0_, bf16[512,896]{1,0:T(8,128)(2,1)S(1)} %collective-permute-done.49.rest_1_, ...), custom_call_target="tpu_custom_call" | custom-call | flops 5000000000 | bytes 1 | tf_op jit(solution)/shard_map/place/pallas_call | solution.py:275
  143.7 6.9 %collective-permute-done.54.rest_0_ = bf16[512,896]{1,0:T(8,128)(2,1)} collective-permute-done((bf16[512,896]{1,0:T(8,128)(2,1)}, bf16[512,896]{1,0:T(8,128)(2,1)}, u32[]{:S(2)}, u32[]{:S(2)}) %collective-permute-start.54) | collective-permute-done | bytes 917536 | tf_op jit(solution)/shard_map/ppermute | solution.py:211
  150.6 4.2 %collective-permute-done.55.rest_1_ = bf16[512,896]{1,0:T(8,128)(2,1)} collective-permute-done((bf16[512,896]{1,0:T(8,128)(2,1)}, bf16[512,896]{1,0:T(8,128)(2,1)}, u32[]{:S(2)}, u32[]{:S(2)}) %collective-permute-start.55) | collective-permute-done | bytes 917536 | tf_op jit(solution)/shard_map/ppermute | solution.py:212
  154.8 1.5 last.25
  (50 shorter events, 0.2 us)
Async XLA Ops:
  12.5 2.4 %collective-permute-start.27 = (bf16[1,1280,256]{2,1,0:T(8,128)(2,1)}, bf16[1,1280,256]{2,1,0:T(8,128)(2,1)S(1)}, u32[]{:S(2)}, u32[]{:S(2)}) collective-permute-start(bf16[1,1280,256]{2,1,0:T(8,128)(2,1)} %get-tuple-element.468), channel_id=1, source_target_pairs={{0,1},{1,0},{2,3},{3,2},{4,5},{5,4},{6,7},{7,6},{8,9},{9,8},{10,11... | collective-permute-start | bytes 1966088 | tf_op jit(solution)/shard_map/ppermute | solution.py:363
  13.0 25.7 %collective-permute-start.26 = (bf16[2,1280,256]{2,1,0:T(8,128)(2,1)}, bf16[2,1280,256]{2,1,0:T(8,128)(2,1)S(1)}, u32[]{:S(2)}, u32[]{:S(2)}) collective-permute-start(bf16[2,1280,256]{2,1,0:T(8,128)(2,1)} %get-tuple-element.466), channel_id=1, source_target_pairs={{0,1},{1,0},{2,3},{3,2},{4,5},{5,4},{6,7},{7,6},{8,9},{9,8},{10,11... | collective-permute-start | bytes 3932168 | tf_op jit(solution)/shard_map/ppermute | solution.py:363
  16.2 7.9 %collective-permute-start.28 = (bf16[1,320,256]{2,1,0:T(8,128)(2,1)S(1)}, bf16[1,320,256]{2,1,0:T(8,128)(2,1)S(1)}, u32[]{:S(2)}, u32[]{:S(2)}) collective-permute-start(bf16[1,320,256]{2,1,0:T(8,128)(2,1)S(1)} %get-tuple-element.511), channel_id=1, source_target_pairs={{0,2},{1,3},{2,0},{3,1},{4,6},{5,7},{6,4},{7,5},{8,10},{9,11},{10,... | collective-permute-start | bytes 491528 | tf_op jit(solution)/shard_map/ppermute | solution.py:363
  19.1 9.3 %collective-permute-start.30 = (bf16[1,320,256]{2,1,0:T(8,128)(2,1)S(1)}, bf16[1,320,256]{2,1,0:T(8,128)(2,1)S(1)}, u32[]{:S(2)}, u32[]{:S(2)}) collective-permute-start(bf16[1,320,256]{2,1,0:T(8,128)(2,1)S(1)} %get-tuple-element.512), channel_id=1, source_target_pairs={{0,6},{1,7},{2,4},{3,5},{4,2},{5,3},{6,0},{7,1},{8,14},{9,15},{10,... | collective-permute-start | bytes 491528 | tf_op jit(solution)/shard_map/ppermute | solution.py:363
  20.6 9.2 %collective-permute-start.29 = (bf16[1,320,256]{2,1,0:T(8,128)(2,1)S(1)}, bf16[1,320,256]{2,1,0:T(8,128)(2,1)S(1)}, u32[]{:S(2)}, u32[]{:S(2)}) collective-permute-start(bf16[1,320,256]{2,1,0:T(8,128)(2,1)S(1)} %get-tuple-element.513), channel_id=1, source_target_pairs={{0,4},{1,5},{2,6},{3,7},{4,0},{5,1},{6,2},{7,3},{8,12},{9,13},{10,... | collective-permute-start | bytes 491528 | tf_op jit(solution)/shard_map/ppermute | solution.py:363
  29.9 16.1 %copy-start.11 = (bf16[1,320,256]{2,1,0:T(8,128)(2,1)}, bf16[1,320,256]{2,1,0:T(8,128)(2,1)S(1)}, u32[]{:S(2)}) copy-start(bf16[1,320,256]{2,1,0:T(8,128)(2,1)S(1)} %fusion.3.rest_0_) | copy-start | bytes 491524
  29.9 7.0 %collective-permute-start.36 = (bf16[1,320,256]{2,1,0:T(8,128)(2,1)S(1)}, bf16[1,320,256]{2,1,0:T(8,128)(2,1)S(1)}, u32[]{:S(2)}, u32[]{:S(2)}) collective-permute-start(bf16[1,320,256]{2,1,0:T(8,128)(2,1)S(1)} %fusion.3.rest_0_), channel_id=1, source_target_pairs={{0,4},{1,5},{2,6},{3,7},{4,0},{5,1},{6,2},{7,3},{8,12},{9,13},{10,... | collective-permute-start | bytes 491528 | tf_op jit(solution)/shard_map/ppermute | solution.py:363
  30.3 6.6 %collective-permute-start.35 = (bf16[1,320,256]{2,1,0:T(8,128)(2,1)S(1)}, bf16[1,320,256]{2,1,0:T(8,128)(2,1)S(1)}, u32[]{:S(2)}, u32[]{:S(2)}) collective-permute-start(bf16[1,320,256]{2,1,0:T(8,128)(2,1)S(1)} %fusion.3.rest_0_), channel_id=1, source_target_pairs={{0,2},{1,3},{2,0},{3,1},{4,6},{5,7},{6,4},{7,5},{8,10},{9,11},{10,... | collective-permute-start | bytes 491528 | tf_op jit(solution)/shard_map/ppermute | solution.py:363
  32.0 6.7 %collective-permute-start.31 = (bf16[1,320,256]{2,1,0:T(8,128)(2,1)S(1)}, bf16[1,320,256]{2,1,0:T(8,128)(2,1)S(1)}, u32[]{:S(2)}, u32[]{:S(2)}) collective-permute-start(bf16[1,320,256]{2,1,0:T(8,128)(2,1)S(1)} %fusion.3.rest_0_), channel_id=1, source_target_pairs={{0,6},{1,7},{2,4},{3,5},{4,2},{5,3},{6,0},{7,1},{8,14},{9,15},{10,... | collective-permute-start | bytes 491528 | tf_op jit(solution)/shard_map/ppermute | solution.py:363
  33.5 10.5 %collective-permute-start.37 = (bf16[1,320,256]{2,1,0:T(8,128)(2,1)S(1)}, bf16[1,320,256]{2,1,0:T(8,128)(2,1)S(1)}, u32[]{:S(2)}, u32[]{:S(2)}) collective-permute-start(bf16[1,320,256]{2,1,0:T(8,128)(2,1)S(1)} %fusion.3.rest_0_), channel_id=1, source_target_pairs={{0,1},{1,0},{2,3},{3,2},{4,5},{5,4},{6,7},{7,6},{8,9},{9,8},{10,11... | collective-permute-start | bytes 491528 | tf_op jit(solution)/shard_map/ppermute | solution.py:363
  36.9 9.1 %copy-start.19 = (bf16[1,320,256]{2,1,0:T(8,128)(2,1)}, bf16[1,320,256]{2,1,0:T(8,128)(2,1)S(1)}, u32[]{:S(2)}) copy-start(bf16[1,320,256]{2,1,0:T(8,128)(2,1)S(1)} %collective-permute-done.36.rest_2_) | copy-start | bytes 491524
  36.9 7.6 %collective-permute-start.39 = (bf16[1,320,256]{2,1,0:T(8,128)(2,1)S(1)}, bf16[1,320,256]{2,1,0:T(8,128)(2,1)S(1)}, u32[]{:S(2)}, u32[]{:S(2)}) collective-permute-start(bf16[1,320,256]{2,1,0:T(8,128)(2,1)S(1)} %collective-permute-done.36.rest_2_), channel_id=1, source_target_pairs={{0,1},{1,0},{2,3},{3,2},{4,5},{5,4},{6,7},{7,6},{8,9},{9,8},{10,11... | collective-permute-start | bytes 491528 | tf_op jit(solution)/shard_map/ppermute | solution.py:363
  36.9 9.1 %copy-start.20 = (bf16[1,320,256]{2,1,0:T(8,128)(2,1)}, bf16[1,320,256]{2,1,0:T(8,128)(2,1)S(1)}, u32[]{:S(2)}) copy-start(bf16[1,320,256]{2,1,0:T(8,128)(2,1)S(1)} %collective-permute-done.35.rest_1_) | copy-start | bytes 491524
  37.0 9.1 %collective-permute-start.38 = (bf16[1,320,256]{2,1,0:T(8,128)(2,1)S(1)}, bf16[1,320,256]{2,1,0:T(8,128)(2,1)S(1)}, u32[]{:S(2)}, u32[]{:S(2)}) collective-permute-start(bf16[1,320,256]{2,1,0:T(8,128)(2,1)S(1)} %collective-permute-done.35.rest_1_), channel_id=1, source_target_pairs={{0,1},{1,0},{2,3},{3,2},{4,5},{5,4},{6,7},{7,6},{8,9},{9,8},{10,11... | collective-permute-start | bytes 491528 | tf_op jit(solution)/shard_map/ppermute | solution.py:363
  38.7 0.6 copy-start.12
  38.7 7.3 %collective-permute-start.40 = (bf16[1,320,256]{2,1,0:T(8,128)(2,1)S(1)}, bf16[1,320,256]{2,1,0:T(8,128)(2,1)S(1)}, u32[]{:S(2)}, u32[]{:S(2)}) collective-permute-start(bf16[1,320,256]{2,1,0:T(8,128)(2,1)S(1)} %collective-permute-done.31._.rest_3_), channel_id=1, source_target_pairs={{0,1},{1,0},{2,3},{3,2},{4,5},{5,4},{6,7},{7,6},{8,9},{9,8},{10,11... | collective-permute-start | bytes 491528 | tf_op jit(solution)/shard_map/ppermute | solution.py:363
  38.7 1.1 copy-start
  42.5 13.2 %collective-permute-start.32 = (bf16[2,320,256]{2,1,0:T(8,128)(2,1)}, bf16[2,320,256]{2,1,0:T(8,128)(2,1)S(1)}, u32[]{:S(2)}, u32[]{:S(2)}) collective-permute-start(bf16[2,320,256]{2,1,0:T(8,128)(2,1)} %get-tuple-element.470), channel_id=1, source_target_pairs={{0,2},{1,3},{2,0},{3,1},{4,6},{5,7},{6,4},{7,5},{8,10},{9,11},{10,... | collective-permute-start | bytes 983048 | tf_op jit(solution)/shard_map/ppermute | solution.py:363
  44.0 2.0 %copy-start.21 = (bf16[1,320,256]{2,1,0:T(8,128)(2,1)}, bf16[1,320,256]{2,1,0:T(8,128)(2,1)S(1)}, u32[]{:S(2)}) copy-start(bf16[1,320,256]{2,1,0:T(8,128)(2,1)S(1)} %collective-permute-done.37.rest_4_) | copy-start | bytes 491524
  44.0 17.0 %collective-permute-start.33 = (bf16[2,320,256]{2,1,0:T(8,128)(2,1)}, bf16[2,320,256]{2,1,0:T(8,128)(2,1)S(1)}, u32[]{:S(2)}, u32[]{:S(2)}) collective-permute-start(bf16[2,320,256]{2,1,0:T(8,128)(2,1)} %get-tuple-element.471), channel_id=1, source_target_pairs={{0,4},{1,5},{2,6},{3,7},{4,0},{5,1},{6,2},{7,3},{8,12},{9,13},{10,... | collective-permute-start | bytes 983048 | tf_op jit(solution)/shard_map/ppermute | solution.py:363
  44.5 1.5 copy-start.22
  44.5 16.5 %collective-permute-start.34 = (bf16[2,320,256]{2,1,0:T(8,128)(2,1)}, bf16[2,320,256]{2,1,0:T(8,128)(2,1)S(1)}, u32[]{:S(2)}, u32[]{:S(2)}) collective-permute-start(bf16[2,320,256]{2,1,0:T(8,128)(2,1)} %get-tuple-element.472), channel_id=1, source_target_pairs={{0,6},{1,7},{2,4},{3,5},{4,2},{5,3},{6,0},{7,1},{8,14},{9,15},{10,... | collective-permute-start | bytes 983048 | tf_op jit(solution)/shard_map/ppermute | solution.py:363
  46.0 0.7 copy-start.23
  46.7 0.7 copy-start.24
  55.7 5.4 %copy-start.1 = (bf16[2,320,256]{2,1,0:T(8,128)(2,1)}, bf16[2,320,256]{2,1,0:T(8,128)(2,1)S(1)}, u32[]{:S(2)}) copy-start(bf16[2,320,256]{2,1,0:T(8,128)(2,1)S(1)} %collective-permute-done.32.rest_0_) | copy-start | bytes 983044
  61.0 0.7 copy-start.2
  61.0 0.8 copy-start.3
  64.0 7.9 %collective-permute-start.44 = (bf16[2,320,256]{2,1,0:T(8,128)(2,1)}, bf16[2,320,256]{2,1,0:T(8,128)(2,1)S(1)}, u32[]{:S(2)}, u32[]{:S(2)}) collective-permute-start(bf16[2,320,256]{2,1,0:T(8,128)(2,1)} %total.1.rest_0_), channel_id=1, source_target_pairs={{0,1},{1,0},{2,3},{3,2},{4,5},{5,4},{6,7},{7,6},{8,9},{9,8},{10,11... | collective-permute-start | bytes 983048 | tf_op jit(solution)/shard_map/ppermute | solution.py:363
  64.1 11.5 %collective-permute-start.43 = (bf16[2,320,256]{2,1,0:T(8,128)(2,1)}, bf16[2,320,256]{2,1,0:T(8,128)(2,1)S(1)}, u32[]{:S(2)}, u32[]{:S(2)}) collective-permute-start(bf16[2,320,256]{2,1,0:T(8,128)(2,1)} %total.1.rest_0_), channel_id=1, source_target_pairs={{0,6},{1,7},{2,4},{3,5},{4,2},{5,3},{6,0},{7,1},{8,14},{9,15},{10,... | collective-permute-start | bytes 983048 | tf_op jit(solution)/shard_map/ppermute | solution.py:363
  65.4 16.9 %collective-permute-start.42 = (bf16[2,320,256]{2,1,0:T(8,128)(2,1)}, bf16[2,320,256]{2,1,0:T(8,128)(2,1)S(1)}, u32[]{:S(2)}, u32[]{:S(2)}) collective-permute-start(bf16[2,320,256]{2,1,0:T(8,128)(2,1)} %total.1.rest_0_), channel_id=1, source_target_pairs={{0,4},{1,5},{2,6},{3,7},{4,0},{5,1},{6,2},{7,3},{8,12},{9,13},{10,... | collective-permute-start | bytes 983048 | tf_op jit(solution)/shard_map/ppermute | solution.py:363
  66.0 39.0 %collective-permute-start.49 = (bf16[512,896]{1,0:T(8,128)(2,1)}, bf16[512,896]{1,0:T(8,128)(2,1)S(1)}, u32[]{:S(2)}, u32[]{:S(2)}) collective-permute-start(bf16[512,896]{1,0:T(8,128)(2,1)} %get-tuple-element.473.rest_3_), channel_id=1, source_target_pairs={{8,0},{16,8},{24,16},{9,1},{17,9},{25,17},{10,2},{18,10},{26,18},{... | collective-permute-start | bytes 2752520 | tf_op jit(solution)/shard_map/ppermute | solution.py:212
  67.3 37.7 %collective-permute-start.48 = (bf16[512,896]{1,0:T(8,128)(2,1)}, bf16[512,896]{1,0:T(8,128)(2,1)S(1)}, u32[]{:S(2)}, u32[]{:S(2)}) collective-permute-start(bf16[512,896]{1,0:T(8,128)(2,1)} %get-tuple-element.473.rest_3_), channel_id=1, source_target_pairs={{0,8},{8,16},{16,24},{1,9},{9,17},{17,25},{2,10},{10,18},{18,26},{... | collective-permute-start | bytes 2752520 | tf_op jit(solution)/shard_map/ppermute | solution.py:211
  72.0 18.8 %copy-start.4 = (bf16[2,320,256]{2,1,0:T(8,128)(2,1)}, bf16[2,320,256]{2,1,0:T(8,128)(2,1)S(1)}, u32[]{:S(2)}) copy-start(bf16[2,320,256]{2,1,0:T(8,128)(2,1)S(1)} %collective-permute-done.44.rest_4_) | copy-start | bytes 983044
  72.0 10.4 %collective-permute-start.41 = (bf16[2,320,256]{2,1,0:T(8,128)(2,1)}, bf16[2,320,256]{2,1,0:T(8,128)(2,1)S(1)}, u32[]{:S(2)}, u32[]{:S(2)}) collective-permute-start(bf16[2,320,256]{2,1,0:T(8,128)(2,1)} %total.1.rest_0_), channel_id=1, source_target_pairs={{0,2},{1,3},{2,0},{3,1},{4,6},{5,7},{6,4},{7,5},{8,10},{9,11},{10,... | collective-permute-start | bytes 983048 | tf_op jit(solution)/shard_map/ppermute | solution.py:363
  75.5 15.3 %copy-start.5 = (bf16[2,320,256]{2,1,0:T(8,128)(2,1)}, bf16[2,320,256]{2,1,0:T(8,128)(2,1)S(1)}, u32[]{:S(2)}) copy-start(bf16[2,320,256]{2,1,0:T(8,128)(2,1)S(1)} %collective-permute-done.43.rest_3_) | copy-start | bytes 983044
  75.5 8.1 %collective-permute-start.47 = (bf16[2,320,256]{2,1,0:T(8,128)(2,1)S(1)}, bf16[2,320,256]{2,1,0:T(8,128)(2,1)S(1)}, u32[]{:S(2)}, u32[]{:S(2)}) collective-permute-start(bf16[2,320,256]{2,1,0:T(8,128)(2,1)S(1)} %collective-permute-done.43.rest_3_), channel_id=1, source_target_pairs={{0,1},{1,0},{2,3},{3,2},{4,5},{5,4},{6,7},{7,6},{8,9},{9,8},{10,11... | collective-permute-start | bytes 983048 | tf_op jit(solution)/shard_map/ppermute | solution.py:363
  82.3 8.5 %copy-start.6 = (bf16[2,320,256]{2,1,0:T(8,128)(2,1)}, bf16[2,320,256]{2,1,0:T(8,128)(2,1)S(1)}, u32[]{:S(2)}) copy-start(bf16[2,320,256]{2,1,0:T(8,128)(2,1)S(1)} %collective-permute-done.42.rest_2_) | copy-start | bytes 983044
  82.3 6.9 %collective-permute-start.46 = (bf16[2,320,256]{2,1,0:T(8,128)(2,1)S(1)}, bf16[2,320,256]{2,1,0:T(8,128)(2,1)S(1)}, u32[]{:S(2)}, u32[]{:S(2)}) collective-permute-start(bf16[2,320,256]{2,1,0:T(8,128)(2,1)S(1)} %collective-permute-done.42.rest_2_), channel_id=1, source_target_pairs={{0,1},{1,0},{2,3},{3,2},{4,5},{5,4},{6,7},{7,6},{8,9},{9,8},{10,11... | collective-permute-start | bytes 983048 | tf_op jit(solution)/shard_map/ppermute | solution.py:363
  82.4 8.5 %copy-start.7 = (bf16[2,320,256]{2,1,0:T(8,128)(2,1)}, bf16[2,320,256]{2,1,0:T(8,128)(2,1)S(1)}, u32[]{:S(2)}) copy-start(bf16[2,320,256]{2,1,0:T(8,128)(2,1)S(1)} %collective-permute-done.41.rest_1_) | copy-start | bytes 983044
  82.4 29.5 %collective-permute-start.51 = (bf16[512,896]{1,0:T(8,128)(2,1)}, bf16[512,896]{1,0:T(8,128)(2,1)S(1)}, u32[]{:S(2)}, u32[]{:S(2)}) collective-permute-start(bf16[512,896]{1,0:T(8,128)(2,1)} %get-tuple-element.475), channel_id=1, source_target_pairs={{8,0},{16,8},{24,16},{9,1},{17,9},{25,17},{10,2},{18,10},{26,18},{... | collective-permute-start | bytes 2752520 | tf_op jit(solution)/shard_map/ppermute | solution.py:212
  83.7 7.2 %copy-start.8 = (bf16[2,320,256]{2,1,0:T(8,128)(2,1)}, bf16[2,320,256]{2,1,0:T(8,128)(2,1)S(1)}, u32[]{:S(2)}) copy-start(bf16[2,320,256]{2,1,0:T(8,128)(2,1)S(1)} %collective-permute-done.47.rest_7_) | copy-start | bytes 983044
  83.7 28.4 %collective-permute-start.50 = (bf16[512,896]{1,0:T(8,128)(2,1)}, bf16[512,896]{1,0:T(8,128)(2,1)}, u32[]{:S(2)}, u32[]{:S(2)}) collective-permute-start(bf16[512,896]{1,0:T(8,128)(2,1)} %get-tuple-element.475), channel_id=1, source_target_pairs={{0,8},{8,16},{16,24},{1,9},{9,17},{17,25},{2,10},{10,18},{18,26},{... | collective-permute-start | bytes 2752520 | tf_op jit(solution)/shard_map/ppermute | solution.py:211
  89.2 1.7 %copy-start.9 = (bf16[2,320,256]{2,1,0:T(8,128)(2,1)}, bf16[2,320,256]{2,1,0:T(8,128)(2,1)S(1)}, u32[]{:S(2)}) copy-start(bf16[2,320,256]{2,1,0:T(8,128)(2,1)S(1)} %collective-permute-done.46.rest_6_) | copy-start | bytes 983044
  89.2 1.6 %collective-permute-start.45 = (bf16[2,320,256]{2,1,0:T(8,128)(2,1)S(1)}, bf16[2,320,256]{2,1,0:T(8,128)(2,1)S(1)}, u32[]{:S(2)}, u32[]{:S(2)}) collective-permute-start(bf16[2,320,256]{2,1,0:T(8,128)(2,1)S(1)} %collective-permute-done.41.rest_1_), channel_id=1, source_target_pairs={{0,1},{1,0},{2,3},{3,2},{4,5},{5,4},{6,7},{7,6},{8,9},{9,8},{10,11... | collective-permute-start | bytes 983048 | tf_op jit(solution)/shard_map/ppermute | solution.py:363
  90.8 0.7 copy-start.10
  108.3 23.4 %collective-permute-start.52 = (bf16[512,896]{1,0:T(8,128)(2,1)}, bf16[512,896]{1,0:T(8,128)(2,1)}, u32[]{:S(2)}, u32[]{:S(2)}) collective-permute-start(bf16[512,896]{1,0:T(8,128)(2,1)} %get-tuple-element.477), channel_id=1, source_target_pairs={{0,8},{8,16},{16,24},{1,9},{9,17},{17,25},{2,10},{10,18},{18,26},{... | collective-permute-start | bytes 2752520 | tf_op jit(solution)/shard_map/ppermute | solution.py:211
  110.6 25.4 %collective-permute-start.53 = (bf16[512,896]{1,0:T(8,128)(2,1)}, bf16[512,896]{1,0:T(8,128)(2,1)}, u32[]{:S(2)}, u32[]{:S(2)}) collective-permute-start(bf16[512,896]{1,0:T(8,128)(2,1)} %get-tuple-element.478), channel_id=1, source_target_pairs={{8,0},{16,8},{24,16},{9,1},{17,9},{25,17},{10,2},{18,10},{26,18},{... | collective-permute-start | bytes 2752520 | tf_op jit(solution)/shard_map/ppermute | solution.py:212
  115.4 35.2 %collective-permute-start.54 = (bf16[512,896]{1,0:T(8,128)(2,1)}, bf16[512,896]{1,0:T(8,128)(2,1)}, u32[]{:S(2)}, u32[]{:S(2)}) collective-permute-start(bf16[512,896]{1,0:T(8,128)(2,1)} %get-tuple-element.480), channel_id=1, source_target_pairs={{0,8},{8,16},{16,24},{1,9},{9,17},{17,25},{2,10},{10,18},{18,26},{... | collective-permute-start | bytes 2752520 | tf_op jit(solution)/shard_map/ppermute | solution.py:211
  120.7 34.1 %collective-permute-start.55 = (bf16[512,896]{1,0:T(8,128)(2,1)}, bf16[512,896]{1,0:T(8,128)(2,1)}, u32[]{:S(2)}, u32[]{:S(2)}) collective-permute-start(bf16[512,896]{1,0:T(8,128)(2,1)} %get-tuple-element.481), channel_id=1, source_target_pairs={{8,0},{16,8},{24,16},{9,1},{17,9},{25,17},{10,2},{18,10},{26,18},{... | collective-permute-start | bytes 2752520 | tf_op jit(solution)/shard_map/ppermute | solution.py:212
